TPU v7x, 32 devices: a whole 2x2x4 slice. The times are simulated.
32 devices in a mesh: ens: 4 (over z), dom: 8 (over y, x, core).
Axes of the slice: x: 2, y: 2, z: 4, core: 2. Of those that a mesh axis runs over, the one named last changes fastest.
Arguments:
- state: float32 [128, 256, 128], P('ens', 'dom'), may hold values from -6 to 6
- row_courant: float32 [256, 128], P('dom'), may hold values from 0.3 to 0.6
- col_courant: float32 [256, 128], P('dom'), may hold values from 0.05 to 0.2
- diffusion: float32 [256, 128], P('dom'), may hold values from 0.01 to 0.05
- obs_values: float32 [4, 256], replicated, may hold values from -8 to 8
- obs_variance: float32 [4, 256], replicated, may hold values from 0.25 to 4
- obs_offsets: int32 [4, 256], replicated, may hold values from 0 to 4095
- owners: int32 [4], replicated, may hold values from 0 to 7, as said below
Outputs:
- analysis: float32 [128, 256, 128], P('ens', 'dom')
Inputs may be any that keep to these rules, and one draw needn't show every extreme that they name: `owners`: distinct domain blocks, one for each batch.
All inputs are finite; a program needn't handle non-finite values.
Results may differ from a plain program's by a relative error of at most 0.0002.
Values sent between devices are 32-bit elements; how exact they have to be, the bound alone decides.
No kernel may reach another device: no remote copies, remote signals or barrier semaphores. Data moves between devices by JAX's collectives and lax.ppermute only.
A program may use at most 64 MiB of HBM per device.

v0:
```python
import jax
import jax.numpy as jnp
from jax import lax
from jax.sharding import PartitionSpec as P

FSTEPS = 4


def with_halo(x, sides, width):
    for axis, dim in sides:
        devices, length = (lax.axis_size(axis), x.shape[dim])
        up = [(i, (i + 1) % devices) for i in range(devices)]
        down = [(j, i) for i, j in up]
        last = lax.slice_in_dim(x, length - width, length, axis=dim)
        leading = lax.slice_in_dim(x, 0, width, axis=dim)
        before = lax.ppermute(last, axis, up)
        after = lax.ppermute(leading, axis, down)
        x = jnp.concatenate([before, x, after], axis=dim)
    return x


def advance_rows(padded, coef):
    center = padded[:, 1:-1]
    upper = padded[:, :-2]
    lower = padded[:, 2:]
    left = jnp.roll(center, 1, axis=2)
    right = jnp.roll(center, -1, axis=2)
    inner = coef[:, 1:-1]
    row_c = inner[0][None]
    col_c = inner[1][None]
    diff_c = inner[2][None]
    fresh = (
        center
        - row_c * (center - upper)
        - col_c * (center - left)
        + diff_c * (upper + lower + left + right - 4.0 * center)
    )
    return (fresh, inner)


def contract_members(left_side, right_side):
    return lax.dot_general(
        left_side,
        right_side,
        (((0,), (0,)), ((), ())),
        precision=lax.Precision.HIGHEST,
        preferred_element_type=jnp.float32,
    )


def on_device(
    state, row_courant, col_courant, diffusion, obs_values, obs_variance, obs_offsets, owners
):
    mem_count, rows_dev, cols = state.shape
    coefs = jnp.stack([row_courant, col_courant, diffusion])
    field = state
    for step in range(FSTEPS):
        padded = with_halo(jnp.concatenate([field, coefs], axis=0), (("dom", 1),), 1)
        field, unused = advance_rows(padded[:mem_count], padded[mem_count:])
    regrouped = lax.all_to_all(field, "ens", split_axis=1, concat_axis=0, tiled=True)
    members, sub_rows, unused_cols = regrouped.shape
    local_cells = sub_rows * cols
    matrix = regrouped.reshape(members, local_cells)
    base = (lax.axis_index("dom") * rows_dev + lax.axis_index("ens") * sub_rows) * cols
    scale = 1.0 / (members - 1.0)

    def fetch(matrix, batch):
        cells = owners[batch] * (rows_dev * cols) + obs_offsets[batch]
        local = cells - base
        inside = (local >= 0) & (local < local_cells)
        picked = jnp.take(matrix, jnp.clip(local, 0, local_cells - 1), axis=1)
        values = jnp.where(inside[None, :], picked, 0.0)
        return lax.psum(values, ("ens", "dom"))

    batches = obs_values.shape[0]
    priors = [fetch(matrix, batch) for batch in range(batches)]
    for batch in range(batches):
        observed = priors[batch]
        ybar = jnp.mean(observed, axis=0)
        anom_obs = observed - ybar
        system = contract_members(anom_obs, anom_obs) * scale + jnp.diag(obs_variance[batch])
        factor = jnp.linalg.cholesky(system)
        target = (obs_values[batch] - ybar)[None, :] - 0.5 * anom_obs
        weights = jax.scipy.linalg.cho_solve((factor, True), target.T).T
        anomaly = matrix - jnp.mean(matrix, axis=0)
        spread = contract_members(anom_obs, anomaly) * scale
        updated = matrix + jnp.dot(weights, spread, precision=lax.Precision.HIGHEST)
        matrix, weights, anom_obs = (updated, weights, anom_obs)
        for later in range(batch + 1, batches):
            column = priors[later]
            centered = column - jnp.mean(column, axis=0)
            shift_obs = contract_members(anom_obs, centered) * scale
            priors[later] = column + jnp.dot(weights, shift_obs, precision=lax.Precision.HIGHEST)
    back = matrix.reshape(members, sub_rows, cols)
    return lax.all_to_all(back, "ens", split_axis=0, concat_axis=1, tiled=True)


def solution(mesh):
    return jax.shard_map(
        on_device,
        mesh=mesh,
        in_specs=(
            P("ens", "dom", None),
            P("dom", None),
            P("dom", None),
            P("dom", None),
            P(),
            P(),
            P(),
            P(),
        ),
        out_specs=P("ens", "dom", None),
        check_vma=False,
    )
```

profile of v0, /device:TPU:0, one launch (start us, length us, event | category | flops | bytes accessed | tf_op | source)
XLA Modules:
  0.0 476.5 jit_solution(18178906944772717136)
XLA Ops:
  33.2 5.6 %all-to-all-start = ((f32[32,32,128]{2,0,1:T(8,128)}), f32[32,32,128]{2,0,1:T(8,128)S(1)}, u32[]{:S(2)}, u32[]{:S(2)}) async-start(f32[32,32,128]{2,0,1:T(8,128)} %fusion.36), calls=%async_computation | async-start | bytes 1048576 | tf_op jit(solution)/shard_map/all_to_all | solution.py:60
  39.7 14.3 %all-to-all-done = f32[32,32,128]{2,0,1:T(8,128)S(1)} async-done(((f32[32,32,128]{2,0,1:T(8,128)}), f32[32,32,128]{2,0,1:T(8,128)S(1)}, u32[]{:S(2)}, u32[]{:S(2)}) %all-to-all-start) | async-done | bytes 524320 | tf_op jit(solution)/shard_map/all_to_all | solution.py:60
  60.9 126.0 %all-reduce.4.cloned.1.call-done = (f32[128,256]{1,0:T(8,128)}, f32[128,256]{1,0:T(8,128)}, f32[128,256]{1,0:T(8,128)}, f32[128,256]{1,0:T(8,128)}) async-done(((f32[128,256]{1,0:T(8,128)}, f32[128,256]{1,0:T(8,128)}, f32[128,256]{1,0:T(8,128)}, f32[128,256]{1,0:T(8,128)}), (f32[128,256]{1,0:T(8,128)}, f32[128,256]{1,0:T(8,128)}, f32[128,256]{1,0:T(8,128)}, ...) | async-done | bytes 524304 | tf_op jit(solution)/shard_map/psum | solution.py:73
  189.0 11.7 %cholesky.214 = f32[128,128]{1,0:T(8,128)S(1)} custom-call(f32[128,128]{1,0:T(8,128)S(1)} %cholesky.346), custom_call_target="Cholesky" | custom-call | tf_op jit(solution)/shard_map/jit(cholesky)/cholesky | solution.py:82
  200.8 9.8 %custom-call.19 = f32[1,128,128]{1,2,0:T(8,128)S(1)} custom-call(f32[1,128,128]{2,1,0:T(8,128)S(1)} %get-tuple-element.129), custom_call_target="InvertDiagBlocksLowerTriangular" | custom-call | tf_op jit(solution)/shard_map/jit(cholesky)/cholesky | solution.py:82
  211.1 12.1 %cholesky.231 = f32[128,128]{1,0:T(8,128)S(1)} custom-call(f32[128,128]{1,0:T(8,128)S(1)} %convolution_subtract_fusion.11), custom_call_target="Cholesky" | custom-call | tf_op jit(solution)/shard_map/jit(cholesky)/cholesky | solution.py:82
  226.0 4.0 while.8
  229.9 19.7 %custom-call.20 = f32[2,128,128]{1,2,0:T(8,128)S(1)} custom-call(f32[2,128,128]{2,1,0:T(8,128)S(1)} %get-tuple-element.34), custom_call_target="InvertDiagBlocksLowerTriangular" | custom-call | tf_op jit(solution)/shard_map/jit(_cho_solve)/triangular_solve | solution.py:84
  253.7 11.7 %cholesky.248 = f32[128,128]{1,0:T(8,128)S(1)} custom-call(f32[128,128]{1,0:T(8,128)S(1)} %cholesky.349), custom_call_target="Cholesky" | custom-call | tf_op jit(solution)/shard_map/jit(cholesky)/cholesky | solution.py:82
  265.5 9.8 %custom-call.21 = f32[1,128,128]{1,2,0:T(8,128)S(1)} custom-call(f32[1,128,128]{2,1,0:T(8,128)S(1)} %get-tuple-element.125), custom_call_target="InvertDiagBlocksLowerTriangular" | custom-call | tf_op jit(solution)/shard_map/jit(cholesky)/cholesky | solution.py:82
  275.8 11.9 %cholesky.265 = f32[128,128]{1,0:T(8,128)S(1)} custom-call(f32[128,128]{1,0:T(8,128)S(1)} %convolution_subtract_fusion.8), custom_call_target="Cholesky" | custom-call | tf_op jit(solution)/shard_map/jit(cholesky)/cholesky | solution.py:82
  290.2 3.8 while.9
  294.0 19.7 %custom-call.22 = f32[2,128,128]{1,2,0:T(8,128)S(1)} custom-call(f32[2,128,128]{2,1,0:T(8,128)S(1)} %get-tuple-element.35), custom_call_target="InvertDiagBlocksLowerTriangular" | custom-call | tf_op jit(solution)/shard_map/jit(_cho_solve)/triangular_solve | solution.py:84
  319.0 11.7 %cholesky.282 = f32[128,128]{1,0:T(8,128)S(1)} custom-call(f32[128,128]{1,0:T(8,128)S(1)} %cholesky.352), custom_call_target="Cholesky" | custom-call | tf_op jit(solution)/shard_map/jit(cholesky)/cholesky | solution.py:82
  330.8 9.8 %custom-call.23 = f32[1,128,128]{1,2,0:T(8,128)S(1)} custom-call(f32[1,128,128]{2,1,0:T(8,128)S(1)} %get-tuple-element.121), custom_call_target="InvertDiagBlocksLowerTriangular" | custom-call | tf_op jit(solution)/shard_map/jit(cholesky)/cholesky | solution.py:82
  341.1 12.1 %cholesky.299 = f32[128,128]{1,0:T(8,128)S(1)} custom-call(f32[128,128]{1,0:T(8,128)S(1)} %convolution_subtract_fusion.5), custom_call_target="Cholesky" | custom-call | tf_op jit(solution)/shard_map/jit(cholesky)/cholesky | solution.py:82
  356.0 4.1 while.10
  360.1 19.7 %custom-call.24 = f32[2,128,128]{1,2,0:T(8,128)S(1)} custom-call(f32[2,128,128]{2,1,0:T(8,128)S(1)} %get-tuple-element.36), custom_call_target="InvertDiagBlocksLowerTriangular" | custom-call | tf_op jit(solution)/shard_map/jit(_cho_solve)/triangular_solve | solution.py:84
  382.9 11.7 %cholesky.316 = f32[128,128]{1,0:T(8,128)S(1)} custom-call(f32[128,128]{1,0:T(8,128)S(1)} %cholesky.355), custom_call_target="Cholesky" | custom-call | tf_op jit(solution)/shard_map/jit(cholesky)/cholesky | solution.py:82
  394.7 9.8 %custom-call.25 = f32[1,128,128]{1,2,0:T(8,128)S(1)} custom-call(f32[1,128,128]{2,1,0:T(8,128)S(1)} %get-tuple-element.117), custom_call_target="InvertDiagBlocksLowerTriangular" | custom-call | tf_op jit(solution)/shard_map/jit(cholesky)/cholesky | solution.py:82
  404.9 11.9 %cholesky.333 = f32[128,128]{1,0:T(8,128)S(1)} custom-call(f32[128,128]{1,0:T(8,128)S(1)} %convolution_subtract_fusion.2), custom_call_target="Cholesky" | custom-call | tf_op jit(solution)/shard_map/jit(cholesky)/cholesky | solution.py:82
  419.6 4.1 while.11
  423.7 19.7 %custom-call.26 = f32[2,128,128]{1,2,0:T(8,128)S(1)} custom-call(f32[2,128,128]{2,1,0:T(8,128)S(1)} %get-tuple-element.37), custom_call_target="InvertDiagBlocksLowerTriangular" | custom-call | tf_op jit(solution)/shard_map/jit(_cho_solve)/triangular_solve | solution.py:84
  452.3 16.3 %all_to_all.33 = f32[128,8,128]{2,1,0:T(8,128)S(1)} all-to-all(f32[128,8,128]{2,1,0:T(8,128)S(1)} %bitcast.246), channel_id=1, replica_groups=mesh['ens'=4,'dom'=8] {'ens'}, dimensions={0} | all-to-all | bytes 1048576 | tf_op jit(solution)/shard_map/all_to_all | solution.py:95
  (242 shorter events, 78.9 us)
Async XLA Ops:
  6.5 1.4 copy-start.1
  6.5 1.4 copy-start.2
  6.5 1.4 copy-start.3
  8.0 8.7 %collective-permute-start = (f32[35,1,128]{2,0,1:T(8,128)S(1)}, f32[35,1,128]{2,0,1:T(8,128)S(1)}, u32[]{:S(2)}, u32[]{:S(2)}) collective-permute-start(f32[35,1,128]{2,0,1:T(8,128)S(1)} %get-tuple-element.96), channel_id=1, source_target_pairs={{0,1},{1,2},{2,3},{3,4},{4,5},{5,6},{6,7},{7,0},{8,9},{9,10},{10,1... | collective-permute-start | bytes 53768 | tf_op jit(solution)/shard_map/ppermute | solution.py:16
  8.5 8.2 %collective-permute-start.1 = (f32[35,1,128]{2,0,1:T(8,128)S(1)}, f32[35,1,128]{2,0,1:T(8,128)S(1)}, u32[]{:S(2)}, u32[]{:S(2)}) collective-permute-start(f32[35,1,128]{2,0,1:T(8,128)S(1)} %get-tuple-element.97), channel_id=1, source_target_pairs={{1,0},{2,1},{3,2},{4,3},{5,4},{6,5},{7,6},{0,7},{9,8},{10,9},{11,1... | collective-permute-start | bytes 53768 | tf_op jit(solution)/shard_map/ppermute | solution.py:17
  11.9 0.7 copy-start.7
  15.9 0.7 copy-start.8
  17.5 4.2 collective-permute-start.2
  17.6 4.1 collective-permute-start.3
  22.6 4.2 collective-permute-start.4
  23.3 3.5 collective-permute-start.5
  27.7 4.2 collective-permute-start.6
  28.9 3.0 collective-permute-start.7
  33.2 20.8 %all-to-all-start = ((f32[32,32,128]{2,0,1:T(8,128)}), f32[32,32,128]{2,0,1:T(8,128)S(1)}, u32[]{:S(2)}, u32[]{:S(2)}) async-start(f32[32,32,128]{2,0,1:T(8,128)} %fusion.36), calls=%async_computation | async-start | bytes 1048576 | tf_op jit(solution)/shard_map/all_to_all | solution.py:60
  38.8 148.1 %all-reduce.4.cloned.1.call-start = ((), (), s32[]{:S(2)}) async-start(), calls=%async_computation.2 | async-start | bytes 1048576 | tf_op jit(solution)/shard_map/psum | solution.py:73
  39.0 0.7 copy-start.10
  186.9 1.0 copy-start.6
  186.9 1.1 copy-start
  229.9 19.7 %copy-start.9 = (f32[4,256]{1,0:T(4,128)S(1)}, f32[4,256]{1,0:T(4,128)}, u32[]{:S(2)}) copy-start(f32[4,256]{1,0:T(4,128)} %param.17) | copy-start | bytes 12292
  251.3 0.9 copy-start.5
  315.8 0.9 copy-start.4
Sparse Core Ops, SparseCore 0:
  60.8 126.1 all-reduce.3
where the time goes:
time: 481 us; the launch traced here: 477 us
  other arithmetic  226 us (47%)
  waiting for transfers between devices  144 us (30%)
  local copies, waits for them, and re-layouts  28.1 us (6%)
  between operations  22.5 us (5%)
  matrix products  21.8 us (5%)
  starting transfers between devices  17.4 us (4%)
  blocking collectives  16.3 us (3%)
    another operation x28, other arithmetic, on_device(): factor = jnp.linalg.cholesky(system)  140 us
    psum x1, waiting for transfers between devices, fetch(): return lax.psum(values, ('ens', 'dom'))  126 us
    another operation x9, other arithmetic, on_device(): weights = jax.scipy.linalg.cho_solve((factor, True), target.T).T  78.8 us
    all_to_all x1, blocking collectives, on_device(): return lax.all_to_all(back, 'ens', split_axis=0, concat_axis=1, tiled=True)  16.3 us
    another operation x29, local copies, waits for them, and re-layouts, on_device(): weights = jax.scipy.linalg.cho_solve((factor, True), target.T).T  15.9 us
    all_to_all x1, waiting for transfers between devices, on_device(): lax.all_to_all(field, 'ens', split_axis=1, concat_axis=0, tiled=True)  14.3 us
  transfers between devices with their start and end apart: 10, of which 7 were waited for; matrix products, arithmetic and copies ran while one was open for 0% of the time, Pallas kernels for 0%

commit v1 on v0

v1 whole, which is shorter than its diff:
```python
import functools

import jax
import jax.numpy as jnp
from jax import lax
from jax.experimental import pallas as pl
from jax.experimental.pallas import tpu as pltpu
from jax.sharding import PartitionSpec as P

FSTEPS = 4
TOLERANCE = 1e-6
WIDE_BOUND = 16.0
HIGHEST = lax.Precision.HIGHEST
NN = (((1,), (0,)), ((), ()))
NT = (((1,), (1,)), ((), ()))

VMEM = pl.BlockSpec(memory_space=pltpu.VMEM)
SMEM = pl.BlockSpec(memory_space=pltpu.SMEM)
PARAMS = pltpu.CompilerParams(vmem_limit_bytes=40 * 1024 * 1024)


def own_batch(place_ref, owners_ref):
    batch = jnp.int32(0)
    for i in range(owners_ref.shape[0]):
        batch = jnp.where(owners_ref[i] == place_ref[0], i, batch)
    return batch


def forecast_kernel(
    place_ref, owners_ref, offsets_ref, state_ref, row_ref, col_ref, diff_ref, up_ref, down_ref,
    field_ref, seen_ref, a_ref, b_ref, coef_ref,
):
    rows, mem, cols = field_ref.shape
    width = FSTEPS
    span = rows + 2 * width
    for r in range(width):
        a_ref[r] = up_ref[r, :mem, :]
        a_ref[width + rows + r] = down_ref[r, :mem, :]

    @pl.loop(0, rows, unroll=4)
    def _(r):
        a_ref[width + r] = state_ref[pl.ds(r, mem, stride=rows), :]

    def put_coefs(r, row_c, col_c, diff_c):
        shape = (8, cols)
        coef_ref[0, r] = jnp.broadcast_to(1.0 - row_c - col_c - 4.0 * diff_c, shape)
        coef_ref[1, r] = jnp.broadcast_to(row_c + diff_c, shape)
        coef_ref[2, r] = jnp.broadcast_to(col_c + diff_c, shape)
        coef_ref[3, r] = jnp.broadcast_to(diff_c, shape)

    for r in range(width):
        for base, ref in ((r, up_ref), (width + rows + r, down_ref)):
            put_coefs(base, *[ref[r, mem + i:mem + i + 1, :] for i in range(3)])
    for r in range(rows):
        put_coefs(width + r, row_ref[r:r + 1, :], col_ref[r:r + 1, :], diff_ref[r:r + 1, :])

    source, target = a_ref, b_ref
    for step in range(1, FSTEPS + 1):
        last = step == FSTEPS

        def one_row(r, source=source, target=target, last=last):
            x = source[r]
            left = pltpu.roll(x, 1, 1)
            right = pltpu.roll(x, cols - 1, 1)
            fold = lambda v: v.reshape(mem // 8, 8, cols)
            fresh = (
                coef_ref[0, r][None] * fold(x)
                + coef_ref[1, r][None] * fold(source[r - 1])
                + coef_ref[2, r][None] * fold(left)
                + coef_ref[3, r][None] * (fold(source[r + 1]) + fold(right))
            ).reshape(mem, cols)
            if last:
                field_ref[r - width] = fresh
            else:
                target[r] = fresh

        pl.loop(step, span - step, unroll=2)(one_row)
        source, target = target, source

    batch = own_batch(place_ref, owners_ref)
    lanes = lax.broadcasted_iota(jnp.int32, (mem, cols), 1)
    for part in range(seen_ref.shape[1] // cols):

        def pick(k, total, part=part):
            cell = offsets_ref[batch, part * cols + k]
            row = cell // cols
            lane = cell - row * cols
            moved = pltpu.roll(field_ref[row], lax.rem(k - lane + cols, cols), 1)
            return jnp.where(lanes == k, moved, total)

        total = lax.fori_loop(0, cols, pick, jnp.zeros((mem, cols), jnp.float32), unroll=8)
        seen_ref[:, part * cols:(part + 1) * cols] = total


def gram_kernel(place_ref, owners_ref, obs_ref, var_ref, *refs):
    seen_refs, out_ref = refs[:-1], refs[-1]
    batch = own_batch(place_ref, owners_ref)
    seen = jnp.concatenate([ref[...] for ref in seen_refs], axis=0)
    members, count = seen.shape
    ybar = jnp.mean(seen, axis=0, keepdims=True)
    anom = seen - ybar
    weight = 1.0 / (var_ref[pl.ds(batch, 1), :] * (members - 1.0))
    gap = obs_ref[pl.ds(batch, 1), :] - ybar
    left = jnp.concatenate([anom * weight, jnp.broadcast_to(gap * weight, (8, count))], axis=0)
    out_ref[...] = lax.dot_general(
        left, anom, NT, precision=HIGHEST, preferred_element_type=jnp.float32
    )


def split(x):
    high = x.astype(jnp.bfloat16)
    return high, (x - high.astype(jnp.float32)).astype(jnp.bfloat16)


def product(wide, a, b, dims=NN):
    dot = functools.partial(
        lax.dot_general, dimension_numbers=dims, preferred_element_type=jnp.float32
    )
    if wide:
        return dot(a, b, precision=HIGHEST)
    a_high, a_low = split(a)
    b_high, b_low = split(b)
    return dot(a_high, b_high) + (dot(a_high, b_low) + dot(a_low, b_high))


def chain_kernel(owners_ref, gram_ref, out_ref):
    mem, members = out_ref.shape
    batches = owners_ref.shape[0]
    eye = (
        lax.broadcasted_iota(jnp.int32, (members, members), 0)
        == lax.broadcasted_iota(jnp.int32, (members, members), 1)
    ).astype(jnp.float32)

    def chain(wide):
        mul = functools.partial(product, wide)
        trans = mean_row = forward = None
        for b in range(batches):
            gram = gram_ref[owners_ref[b], :members, :]
            lead = gram_ref[owners_ref[b], members:members + 8, :]
            if b == 0:
                excess, vec = gram, lead
                trans, mean_row = eye, jnp.zeros_like(lead)
            else:
                first = mul(jnp.concatenate([gram, lead], axis=0), trans)
                second = mul(jnp.concatenate([forward, mean_row], axis=0), first[:members])
                excess = second[:members]
                vec = first[members:] - second[members:]
            bound = 1.0 + jnp.max(jnp.sum(jnp.abs(excess), axis=0, keepdims=True))
            scale = 2.0 / (1.0 + bound)
            off = (bound - 1.0) / (bound + 1.0)
            rest = (1.0 - scale) * eye - scale * excess
            power = scale * jnp.concatenate([trans, vec], axis=0)

            def unfinished(carry):
                off = carry[0]
                return off * off / (2.0 - off * off) > TOLERANCE

            def refine(carry):
                off, rest, power = carry
                factor = 2.0 / (2.0 - off * off)
                both = mul(jnp.concatenate([rest, power], axis=0), rest)
                rest = factor * both[:members] + (1.0 - factor) * eye
                power = factor * (power + both[members:])
                return off * off / (2.0 - off * off), rest, power

            off, rest, power = lax.while_loop(unfinished, refine, (off, rest, power))
            power = 2.0 / (2.0 - off * off) * (power + mul(power, rest))
            move = power[members:]
            mean_row = mean_row + (move if b == 0 else mul(move, forward))
            trans = 0.5 * (trans + power[:members])
            forward = trans.T
        out_ref[...] = forward[:mem] + mean_row[:1]

    worst = jnp.float32(0.0)
    for b in range(batches):
        gram = gram_ref[owners_ref[b], :members, :]
        worst = jnp.maximum(worst, jnp.max(jnp.sum(jnp.abs(gram), axis=0, keepdims=True)))
    pl.when(worst > WIDE_BOUND)(lambda: chain(True))
    pl.when(jnp.logical_not(worst > WIDE_BOUND))(lambda: chain(False))


def apply_kernel(mix_ref, *refs):
    field_refs, out_ref = refs[:-1], refs[-1]
    rows, mem, cols = field_refs[0].shape
    mix_high, mix_low = split(mix_ref[...])
    dot = functools.partial(jnp.dot, preferred_element_type=jnp.float32)

    @pl.loop(0, rows // 2, unroll=2)
    def _(pair):
        r = 2 * pair
        x = jnp.concatenate(
            [jnp.concatenate([ref[r + i] for ref in field_refs], axis=0) for i in range(2)], axis=1
        )
        high, low = split(x)
        fresh = dot(mix_high, high) + (dot(mix_high, low) + dot(mix_low, high))
        for i in range(2):
            out_ref[pl.ds(r + i, mem, stride=rows), :] = fresh[:, i * cols:(i + 1) * cols]


def shift(x, axis, step):
    count = lax.axis_size(axis)
    return lax.ppermute(x, axis, [(i, (i + step) % count) for i in range(count)])


def on_device(
    state, row_courant, col_courant, diffusion, obs_values, obs_variance, obs_offsets, owners
):
    mem, rows, cols = state.shape
    ens = lax.axis_size("ens")
    members = mem * ens
    observed = obs_values.shape[1]
    f32 = functools.partial(jax.ShapeDtypeStruct, dtype=jnp.float32)
    place = lax.axis_index("dom").astype(jnp.int32).reshape(1)

    def edge(part):
        coefs = jnp.stack([row_courant[part], col_courant[part], diffusion[part]], axis=1)
        return jnp.concatenate([state[:, part].transpose(1, 0, 2), coefs], axis=1)

    up = shift(edge(slice(rows - FSTEPS, rows)), "dom", 1)
    down = shift(edge(slice(0, FSTEPS)), "dom", -1)
    span = rows + 2 * FSTEPS
    field, seen = pl.pallas_call(
        forecast_kernel,
        out_shape=(f32((rows, mem, cols)), f32((mem, observed))),
        in_specs=[SMEM] * 3 + [VMEM] * 6,
        out_specs=(VMEM, VMEM),
        scratch_shapes=[
            pltpu.VMEM((span, mem, cols), jnp.float32),
            pltpu.VMEM((span, mem, cols), jnp.float32),
            pltpu.VMEM((4, span, 8, cols), jnp.float32),
        ],
        compiler_params=PARAMS,
        name="forecast",
    )(place, owners, obs_offsets, state.reshape(mem * rows, cols), row_courant, col_courant,
      diffusion, up, down)

    seens = [seen] + [shift(seen, "ens", k) for k in range(1, ens)]
    gram = pl.pallas_call(
        gram_kernel,
        out_shape=f32((members + 8, members)),
        in_specs=[SMEM] * 2 + [VMEM] * (2 + ens),
        out_specs=VMEM,
        compiler_params=PARAMS,
        name="gram",
    )(place, owners, obs_values, obs_variance, *seens)
    grams = lax.all_gather(gram, "dom")

    fields = [field]
    for _ in range(1, ens):
        fields.append(shift(fields[-1], "ens", 1))

    mix = pl.pallas_call(
        chain_kernel,
        out_shape=f32((mem, members)),
        in_specs=[SMEM, VMEM],
        out_specs=VMEM,
        compiler_params=PARAMS,
        cost_estimate=pl.CostEstimate(
            flops=2 * 4 * 20 * members**3, bytes_accessed=grams.size * 4, transcendentals=0
        ),
        name="chain",
    )(owners, grams)
    out = pl.pallas_call(
        apply_kernel,
        out_shape=f32((mem * rows, cols)),
        in_specs=[VMEM] * (1 + ens),
        out_specs=VMEM,
        compiler_params=PARAMS,
        name="apply",
    )(mix, *fields)
    return out.reshape(mem, rows, cols)


def solution(mesh):
    return jax.shard_map(
        on_device,
        mesh=mesh,
        in_specs=(
            P("ens", "dom", None),
            P("dom", None),
            P("dom", None),
            P("dom", None),
            P(),
            P(),
            P(),
            P(),
        ),
        out_specs=P("ens", "dom", None),
        check_vma=False,
    )
```

time: 481 us -> 92.5 us (0.19)
  other arithmetic: 226 us -> 0.03 us
  waiting for transfers between devices: 144 us -> 45.2 us
  local copies, waits for them, and re-layouts: 28.1 us -> 3.83 us
  Pallas kernels: 0 us -> 23.1 us
  between operations: 22.5 us -> 0.09 us
  matrix products: 21.8 us -> 0 us
  starting transfers between devices: 17.4 us -> 10.2 us
  blocking collectives: 16.3 us -> 9.87 us
    another operation x37 -> x0, other arithmetic: 218 us -> none  [the longest x28 140 us: on_device(): factor = jnp.linalg.cholesky(system)]
    psum x1 -> x0, waiting for transfers between devices: 126 us -> none  [fetch(): return lax.psum(values, ('ens', 'dom'))]
    ppermute x8, waiting for transfers between devices: 3.83 us -> 45.2 us  [shift(): lax.ppermute(x, axis, [(i, (i + step) % count) for i in range(count)])]
    pallas_call x0 -> x4, Pallas kernels: none -> 23.1 us  [the longest x1 11.8 us: on_device(): pl.pallas_call(forecast_kernel, out_shape=(f32((rows, mem, cols)), f32((m...]
    all_to_all x1 -> x0, blocking collectives: 16.3 us -> none  [on_device(): return lax.all_to_all(back, 'ens', split_axis=0, concat_axis=1, tiled=True)]
    another operation x37 -> x0, local copies, waits for them, and re-layouts: 16 us -> none  [the longest x29 15.9 us: on_device(): weights = jax.scipy.linalg.cho_solve((factor, True), target.T).T]
    all_to_all x1 -> x0, waiting for transfers between devices: 14.3 us -> none  [on_device(): lax.all_to_all(field, 'ens', split_axis=1, concat_axis=0, tiled=True)]
    dot_general x24 -> x0, matrix products: 13.7 us -> none  [the longest x14 8.31 us: contract_members(): lax.dot_general(left_side, right_side, (((0,), (0,)), ((), ())), precisio...]
  transfers between devices with their start and end apart: 10 -> 8, of which waited for: 7 -> 7; matrix products, arithmetic and copies ran while one was open for 0% -> 0% of each run, Pallas kernels for 0% -> 9%
where the time goes in v1:
time: 92.5 us; the launch traced here: 92.3 us
  waiting for transfers between devices  45.2 us (49%)
  Pallas kernels  23.1 us (25%)
  starting transfers between devices  10.2 us (11%)
  blocking collectives  9.87 us (11%)
  local copies, waits for them, and re-layouts  3.83 us (4%)
    ppermute x8, waiting for transfers between devices, shift(): lax.ppermute(x, axis, [(i, (i + step) % count) for i in range(count)])  45.2 us
    pallas_call x1, Pallas kernels, on_device(): pl.pallas_call(forecast_kernel, out_shape=(f32((rows, mem, cols)), f32((m...  11.8 us
    ppermute x8, starting transfers between devices, shift(): lax.ppermute(x, axis, [(i, (i + step) % count) for i in range(count)])  10.2 us
    all_gather x1, blocking collectives, on_device(): grams = lax.all_gather(gram, 'dom')  9.87 us
    pallas_call x1, Pallas kernels, on_device(): pl.pallas_call(chain_kernel, out_shape=f32((mem, members)), in_specs=[SME...  7.86 us
    pallas_call x1, Pallas kernels, on_device(): pl.pallas_call(apply_kernel, out_shape=f32((mem * rows, cols)), in_specs=...  2.6 us
  transfers between devices with their start and end apart: 8, of which 7 were waited for; matrix products, arithmetic and copies ran while one was open for 0% of the time, Pallas kernels for 9%

profile of v1, /device:TPU:0, one launch (start us, length us, event | category | flops | bytes accessed | tf_op | source)
XLA Modules:
  0.0 92.3 jit_solution(11448919949583957127)
XLA Ops:
  0.0 0.8 fusion.1
  0.8 0.7 fusion.2
  1.5 0.7 fusion.3
  2.2 1.0 %fusion = (f32[32,4,128]{2,1,0:T(4,128)S(1)}, f32[32,4,128]{2,1,0:T(4,128)S(1)}) fusion(f32[32,32,128]{2,1,0:T(8,128)} %param.8), kind=kLoop, calls=%fused_computation.4 | loop fusion | bytes 262144 | tf_op jit(solution)/shard_map/slice | solution.py:217
  3.2 0.5 collective-permute-start
  3.7 0.0 copy-start.3
  3.8 3.0 %collective-permute-start.1 = (f32[4,35,128]{2,1,0:T(8,128)S(1)}, f32[4,35,128]{2,1,0:T(8,128)S(1)}, u32[]{:S(2)}, u32[]{:S(2)}) collective-permute-start(f32[4,35,128]{2,1,0:T(8,128)S(1)} %pad_maximum_fusion.1), channel_id=1, source_target_pairs={{0,7},{1,0},{2,1},{3,2},{4,3},{5,4},{6,5},{7,6},{8,15},{9,8},{10,9... | collective-permute-start | bytes 215048 | tf_op jit(solution)/shard_map/ppermute | solution.py:202
  6.7 2.0 %collective-permute-done.up_ref = f32[4,35,128]{2,1,0:T(8,128)S(1)} collective-permute-done((f32[4,35,128]{2,1,0:T(8,128)S(1)}, f32[4,35,128]{2,1,0:T(8,128)S(1)}, u32[]{:S(2)}, u32[]{:S(2)}) %collective-permute-start) | collective-permute-done | bytes 71712 | tf_op jit(solution)/shard_map/ppermute | solution.py:202
  8.7 0.1 collective-permute-done.1.down_ref
  8.8 0.6 copy-done.7
  9.5 11.8 %forecast.1 = (f32[32,32,128]{2,1,0:T(8,128)S(1)}, f32[32,256]{1,0:T(8,128)S(1)}) custom-call(s32[1]{0:T(128)} %bitcast.place_ref, s32[4]{0:T(128)S(1)} %copy-done.7, s32[4,256]{1,0:T(4,128)S(1)} %copy-done.4, f32[1024,128]{1,0:T(8,128)S(1)} %bitcast.16, f32[32,128]{1,0:T(8,128)S(1)} %copy-done.1, f32[32,128]{1,0:T(8,128)S(1)} %copy-done.2, ...), custom_call_target="tpu_custom_call" | custom-call | tf_op jit(solution)/shard_map/forecast/pallas_call | solution.py:222
  21.2 2.3 %collective-permute-start.5 = (f32[32,32,128]{2,1,0:T(8,128)S(1)}, f32[32,32,128]{2,1,0:T(8,128)S(1)}, u32[]{:S(2)}, u32[]{:S(2)}) collective-permute-start(f32[32,32,128]{2,1,0:T(8,128)S(1)} %get-tuple-element.8.refs_0_), channel_id=1, source_target_pairs={{0,8},{8,16},{16,24},{24,0},{1,9},{9,17},{17,25},{25,1},{2,10},{10... | collective-permute-start | bytes 1572872 | tf_op jit(solution)/shard_map/ppermute | solution.py:202
  23.5 14.7 %collective-permute-done.5.refs_1_ = f32[32,32,128]{2,1,0:T(8,128)S(1)} collective-permute-done((f32[32,32,128]{2,1,0:T(8,128)S(1)}, f32[32,32,128]{2,1,0:T(8,128)S(1)}, u32[]{:S(2)}, u32[]{:S(2)}) %collective-permute-start.5) | collective-permute-done | bytes 524320 | tf_op jit(solution)/shard_map/ppermute | solution.py:202
  38.3 15.7 %collective-permute-done.6.refs_2_ = f32[32,32,128]{2,1,0:T(8,128)S(1)} collective-permute-done((f32[32,32,128]{2,1,0:T(8,128)S(1)}, f32[32,32,128]{2,1,0:T(8,128)S(1)}, u32[]{:S(2)}, u32[]{:S(2)}) %collective-permute-start.6) | collective-permute-done | bytes 524320 | tf_op jit(solution)/shard_map/ppermute | solution.py:202
  54.0 3.8 %collective-permute-start.4 = (f32[32,256]{1,0:T(8,128)S(1)}, f32[32,256]{1,0:T(8,128)S(1)}, u32[]{:S(2)}, u32[]{:S(2)}) collective-permute-start(f32[32,256]{1,0:T(8,128)S(1)} %get-tuple-element.7.refs_0_), channel_id=1, source_target_pairs={{0,24},{8,0},{16,8},{24,16},{1,25},{9,1},{17,9},{25,17},{2,26},{10... | collective-permute-start | bytes 98312 | tf_op jit(solution)/shard_map/ppermute | solution.py:202
  57.8 0.6 collective-permute-start.2
  58.4 9.9 %collective-permute-done.4.refs_3_ = f32[32,256]{1,0:T(8,128)S(1)} collective-permute-done((f32[32,256]{1,0:T(8,128)S(1)}, f32[32,256]{1,0:T(8,128)S(1)}, u32[]{:S(2)}, u32[]{:S(2)}) %collective-permute-start.4) | collective-permute-done | bytes 32800 | tf_op jit(solution)/shard_map/ppermute | solution.py:202
  68.3 2.0 %collective-permute-done.3.refs_2_ = f32[32,256]{1,0:T(8,128)S(1)} collective-permute-done((f32[32,256]{1,0:T(8,128)S(1)}, f32[32,256]{1,0:T(8,128)S(1)}, u32[]{:S(2)}, u32[]{:S(2)}) %collective-permute-start.3) | collective-permute-done | bytes 32800 | tf_op jit(solution)/shard_map/ppermute | solution.py:202
  70.4 0.7 collective-permute-done.2.refs_1_
  71.1 0.8 gram.1
  72.0 9.9 %all-gather = f32[1088,128]{1,0:T(8,128)S(1)} all-gather(f32[136,128]{1,0:T(8,128)S(1)} %gram.1), channel_id=2, replica_groups=mesh['ens'=4,'dom'=8] {'dom'}, dimensions={0}, use_global_device_ids=true | all-gather | bytes 626688 | tf_op jit(solution)/shard_map/all_gather | solution.py:246
  81.8 7.9 %chain.1.mix_ref = f32[32,128]{1,0:T(8,128)S(1)} custom-call(s32[4]{0:T(128)S(1)} %copy-done.7, f32[8,136,128]{2,1,0:T(8,128)S(1)} %bitcast.17), custom_call_target="tpu_custom_call" | custom-call | flops 335544320 | bytes 557056 | tf_op jit(solution)/shard_map/chain/pallas_call | solution.py:252
  89.7 0.0 collective-permute-done.7.refs_3_
  89.7 2.6 %apply.1 = f32[1024,128]{1,0:T(8,128)} custom-call(f32[32,128]{1,0:T(8,128)S(1)} %chain.1.mix_ref, f32[32,32,128]{2,1,0:T(8,128)S(1)} %get-tuple-element.8.refs_0_, f32[32,32,128]{2,1,0:T(8,128)S(1)} %collective-permute-done.5.refs_1_, f32[32,32,128]{2,1,0:T(8,128)S(1)} %collective-permute-done.6.refs_2_, f32[32,32,128]{2,1,0:T(8,128)S(1)} %collective-permute-done.7.refs_3_), custom_call_target="tpu_custom_call" | custom-call | tf_op jit(solution)/shard_map/apply/pallas_call | solution.py:263
  (21 shorter events, 0.1 us)
Async XLA Ops:
  0.0 8.8 %copy-start = (f32[32,32,128]{2,1,0:T(8,128)S(1)}, f32[32,32,128]{2,1,0:T(8,128)}, u32[]{:S(2)}) copy-start(f32[32,32,128]{2,1,0:T(8,128)} %param.8) | copy-start | bytes 1572868
  3.2 5.5 %collective-permute-start = (f32[4,35,128]{2,1,0:T(8,128)S(1)}, f32[4,35,128]{2,1,0:T(8,128)S(1)}, u32[]{:S(2)}, u32[]{:S(2)}) collective-permute-start(f32[4,35,128]{2,1,0:T(8,128)S(1)} %pad_maximum_fusion), channel_id=1, source_target_pairs={{0,1},{1,2},{2,3},{3,4},{4,5},{5,6},{6,7},{7,0},{8,9},{9,10},{10,1... | collective-permute-start | bytes 215048 | tf_op jit(solution)/shard_map/ppermute | solution.py:202
  3.7 5.1 %copy-start.1 = (f32[32,128]{1,0:T(8,128)S(1)}, f32[32,128]{1,0:T(8,128)}, u32[]{:S(2)}) copy-start(f32[32,128]{1,0:T(8,128)} %row_ref.1) | copy-start | bytes 49156
  3.7 5.1 %copy-start.2 = (f32[32,128]{1,0:T(8,128)S(1)}, f32[32,128]{1,0:T(8,128)}, u32[]{:S(2)}) copy-start(f32[32,128]{1,0:T(8,128)} %col_ref.1) | copy-start | bytes 49156
  3.7 5.1 %copy-start.3 = (f32[32,128]{1,0:T(8,128)S(1)}, f32[32,128]{1,0:T(8,128)}, u32[]{:S(2)}) copy-start(f32[32,128]{1,0:T(8,128)} %diff_ref.1) | copy-start | bytes 49156
  3.8 5.0 %collective-permute-start.1 = (f32[4,35,128]{2,1,0:T(8,128)S(1)}, f32[4,35,128]{2,1,0:T(8,128)S(1)}, u32[]{:S(2)}, u32[]{:S(2)}) collective-permute-start(f32[4,35,128]{2,1,0:T(8,128)S(1)} %pad_maximum_fusion.1), channel_id=1, source_target_pairs={{0,7},{1,0},{2,1},{3,2},{4,3},{5,4},{6,5},{7,6},{8,15},{9,8},{10,9... | collective-permute-start | bytes 215048 | tf_op jit(solution)/shard_map/ppermute | solution.py:202
  6.7 2.1 %copy-start.4 = (s32[4,256]{1,0:T(4,128)S(1)}, s32[4,256]{1,0:T(4,128)}, u32[]{:S(2)}) copy-start(s32[4,256]{1,0:T(4,128)} %offsets_ref.1) | copy-start | bytes 12292
  8.8 0.7 copy-start.7
  9.5 61.7 %copy-start.5 = (f32[4,256]{1,0:T(4,128)S(1)}, f32[4,256]{1,0:T(4,128)}, u32[]{:S(2)}) copy-start(f32[4,256]{1,0:T(4,128)} %obs_ref.1) | copy-start | bytes 12292
  9.5 61.7 %copy-start.6 = (f32[4,256]{1,0:T(4,128)S(1)}, f32[4,256]{1,0:T(4,128)}, u32[]{:S(2)}) copy-start(f32[4,256]{1,0:T(4,128)} %var_ref.1) | copy-start | bytes 12292
  21.2 17.0 %collective-permute-start.5 = (f32[32,32,128]{2,1,0:T(8,128)S(1)}, f32[32,32,128]{2,1,0:T(8,128)S(1)}, u32[]{:S(2)}, u32[]{:S(2)}) collective-permute-start(f32[32,32,128]{2,1,0:T(8,128)S(1)} %get-tuple-element.8.refs_0_), channel_id=1, source_target_pairs={{0,8},{8,16},{16,24},{24,0},{1,9},{9,17},{17,25},{25,1},{2,10},{10... | collective-permute-start | bytes 1572872 | tf_op jit(solution)/shard_map/ppermute | solution.py:202
  38.3 15.7 %collective-permute-start.6 = (f32[32,32,128]{2,1,0:T(8,128)S(1)}, f32[32,32,128]{2,1,0:T(8,128)S(1)}, u32[]{:S(2)}, u32[]{:S(2)}) collective-permute-start(f32[32,32,128]{2,1,0:T(8,128)S(1)} %collective-permute-done.5.refs_1_), channel_id=1, source_target_pairs={{0,8},{8,16},{16,24},{24,0},{1,9},{9,17},{17,25},{25,1},{2,10},{10... | collective-permute-start | bytes 1572872 | tf_op jit(solution)/shard_map/ppermute | solution.py:202
  54.0 35.7 %collective-permute-start.7 = (f32[32,32,128]{2,1,0:T(8,128)S(1)}, f32[32,32,128]{2,1,0:T(8,128)S(1)}, u32[]{:S(2)}, u32[]{:S(2)}) collective-permute-start(f32[32,32,128]{2,1,0:T(8,128)S(1)} %collective-permute-done.6.refs_2_), channel_id=1, source_target_pairs={{0,8},{8,16},{16,24},{24,0},{1,9},{9,17},{17,25},{25,1},{2,10},{10... | collective-permute-start | bytes 1572872 | tf_op jit(solution)/shard_map/ppermute | solution.py:202
  54.0 14.3 %collective-permute-start.4 = (f32[32,256]{1,0:T(8,128)S(1)}, f32[32,256]{1,0:T(8,128)S(1)}, u32[]{:S(2)}, u32[]{:S(2)}) collective-permute-start(f32[32,256]{1,0:T(8,128)S(1)} %get-tuple-element.7.refs_0_), channel_id=1, source_target_pairs={{0,24},{8,0},{16,8},{24,16},{1,25},{9,1},{17,9},{25,17},{2,26},{10... | collective-permute-start | bytes 98312 | tf_op jit(solution)/shard_map/ppermute | solution.py:202
  57.8 12.5 %collective-permute-start.3 = (f32[32,256]{1,0:T(8,128)S(1)}, f32[32,256]{1,0:T(8,128)S(1)}, u32[]{:S(2)}, u32[]{:S(2)}) collective-permute-start(f32[32,256]{1,0:T(8,128)S(1)} %get-tuple-element.7.refs_0_), channel_id=1, source_target_pairs={{0,16},{8,24},{16,0},{24,8},{1,17},{9,25},{17,1},{25,9},{2,18},{10... | collective-permute-start | bytes 98312 | tf_op jit(solution)/shard_map/ppermute | solution.py:202
  57.8 13.3 %collective-permute-start.2 = (f32[32,256]{1,0:T(8,128)S(1)}, f32[32,256]{1,0:T(8,128)S(1)}, u32[]{:S(2)}, u32[]{:S(2)}) collective-permute-start(f32[32,256]{1,0:T(8,128)S(1)} %get-tuple-element.7.refs_0_), channel_id=1, source_target_pairs={{0,8},{8,16},{16,24},{24,0},{1,9},{9,17},{17,25},{25,1},{2,10},{10... | collective-permute-start | bytes 98312 | tf_op jit(solution)/shard_map/ppermute | solution.py:202

commit v2 on v1

--- a/solution.py
+++ b/solution.py
@@ -26,56 +26,97 @@
     return batch
 
 
-def forecast_kernel(
+def estimate(micros):
+    return pl.CostEstimate(flops=int(1.15e9 * micros), bytes_accessed=0, transcendentals=0)
+
+
+def edge_kernel(state_ref, row_ref, col_ref, diff_ref, top_ref, bottom_ref):
+    width, _, cols = top_ref.shape
+    rows = row_ref.shape[0]
+    mem = state_ref.shape[0] // rows
+    for r in range(width):
+        for ref, row in ((top_ref, r), (bottom_ref, rows - width + r)):
+            ref[r, :mem, :] = state_ref[pl.ds(row, mem, stride=rows), :]
+            for i, coef in enumerate((row_ref, col_ref, diff_ref)):
+                ref[r, mem + i:mem + i + 1, :] = coef[row:row + 1, :]
+            ref[r, mem + 3:, :] = jnp.zeros((ref.shape[1] - mem - 3, cols), jnp.float32)
+
+
+def mixers(row_c, col_c, diff_c):
+    return 1.0 - row_c - col_c - 4.0 * diff_c, row_c + diff_c, col_c + diff_c, diff_c
+
+
+def advance(load, coef, store, count, scratches):
+    for step in range(1, FSTEPS + 1):
+        source = load if step == 1 else scratches[step % 2].__getitem__
+        for r in range(step, count - step):
+            x = source(r)
+            cols = x.shape[1]
+            here, upper, side, lower = coef(r)
+            fresh = (
+                here * x
+                + upper * source(r - 1)
+                + side * pltpu.roll(x, 1, 1)
+                + lower * (source(r + 1) + pltpu.roll(x, cols - 1, 1))
+            )
+            if step == FSTEPS:
+                store(r, fresh)
+            else:
+                scratches[(step + 1) % 2][r] = fresh
+
+
+def inner_kernel(state_ref, row_ref, col_ref, diff_ref, inner_ref, a_ref, b_ref):
+    rows = row_ref.shape[0]
+    mem = state_ref.shape[0] // rows
+
+    def load(r):
+        return state_ref[pl.ds(r, mem, stride=rows), :]
+
+    def coef(r):
+        return mixers(row_ref[r:r + 1, :], col_ref[r:r + 1, :], diff_ref[r:r + 1, :])
+
+    def store(r, value):
+        inner_ref[r - FSTEPS] = value
+
+    advance(load, coef, store, rows, (a_ref, b_ref))
+
+
+def outer_kernel(
     place_ref, owners_ref, offsets_ref, state_ref, row_ref, col_ref, diff_ref, up_ref, down_ref,
-    field_ref, seen_ref, a_ref, b_ref, coef_ref,
+    inner_ref, outer_ref, seen_ref, a_ref, b_ref, field_ref,
 ):
+    width = FSTEPS
     rows, mem, cols = field_ref.shape
-    width = FSTEPS
-    span = rows + 2 * width
-    for r in range(width):
-        a_ref[r] = up_ref[r, :mem, :]
-        a_ref[width + rows + r] = down_ref[r, :mem, :]
-
-    @pl.loop(0, rows, unroll=4)
-    def _(r):
-        a_ref[width + r] = state_ref[pl.ds(r, mem, stride=rows), :]
-
-    def put_coefs(r, row_c, col_c, diff_c):
-        shape = (8, cols)
-        coef_ref[0, r] = jnp.broadcast_to(1.0 - row_c - col_c - 4.0 * diff_c, shape)
-        coef_ref[1, r] = jnp.broadcast_to(row_c + diff_c, shape)
-        coef_ref[2, r] = jnp.broadcast_to(col_c + diff_c, shape)
-        coef_ref[3, r] = jnp.broadcast_to(diff_c, shape)
-
-    for r in range(width):
-        for base, ref in ((r, up_ref), (width + rows + r, down_ref)):
-            put_coefs(base, *[ref[r, mem + i:mem + i + 1, :] for i in range(3)])
-    for r in range(rows):
-        put_coefs(width + r, row_ref[r:r + 1, :], col_ref[r:r + 1, :], diff_ref[r:r + 1, :])
-
-    source, target = a_ref, b_ref
-    for step in range(1, FSTEPS + 1):
-        last = step == FSTEPS
-
-        def one_row(r, source=source, target=target, last=last):
-            x = source[r]
-            left = pltpu.roll(x, 1, 1)
-            right = pltpu.roll(x, cols - 1, 1)
-            fold = lambda v: v.reshape(mem // 8, 8, cols)
-            fresh = (
-                coef_ref[0, r][None] * fold(x)
-                + coef_ref[1, r][None] * fold(source[r - 1])
-                + coef_ref[2, r][None] * fold(left)
-                + coef_ref[3, r][None] * (fold(source[r + 1]) + fold(right))
-            ).reshape(mem, cols)
-            if last:
-                field_ref[r - width] = fresh
-            else:
-                target[r] = fresh
-
-        pl.loop(step, span - step, unroll=2)(one_row)
-        source, target = target, source
+
+    for side in range(2):
+        base = rows - 2 * width if side else -width
+
+        def place(r, side=side):
+            row = r + (rows - 2 * width if side else -width)
+            if row < 0:
+                return up_ref, row + width
+            if row >= rows:
+                return down_ref, row - rows
+            return None, row
+
+        def load(r, place=place):
+            ref, row = place(r)
+            return state_ref[pl.ds(row, mem, stride=rows), :] if ref is None else ref[row, :mem, :]
+
+        def coef(r, place=place):
+            ref, row = place(r)
+            if ref is None:
+                return mixers(*[c[row:row + 1, :] for c in (row_ref, col_ref, diff_ref)])
+            return mixers(*[ref[row, mem + i:mem + i + 1, :] for i in range(3)])
+
+        def store(r, value, side=side, base=base):
+            outer_ref[side * width + r - width] = value
+            field_ref[r + base] = value
+
+        advance(load, coef, store, 3 * width, (a_ref, b_ref))
+
+    for r in range(rows - 2 * width):
+        field_ref[width + r] = inner_ref[r]
 
     batch = own_batch(place_ref, owners_ref)
     lanes = lax.broadcasted_iota(jnp.int32, (mem, cols), 1)
@@ -88,7 +129,7 @@
             moved = pltpu.roll(field_ref[row], lax.rem(k - lane + cols, cols), 1)
             return jnp.where(lanes == k, moved, total)
 
-        total = lax.fori_loop(0, cols, pick, jnp.zeros((mem, cols), jnp.float32), unroll=8)
+        total = lax.fori_loop(0, cols, pick, jnp.zeros((mem, cols), jnp.float32), unroll=32)
         seen_ref[:, part * cols:(part + 1) * cols] = total
 
 
@@ -181,17 +222,20 @@
 
 def apply_kernel(mix_ref, *refs):
     field_refs, out_ref = refs[:-1], refs[-1]
-    rows, mem, cols = field_refs[0].shape
+    inner_refs, outer_refs = field_refs[::2], field_refs[1::2]
+    inner, mem, cols = inner_refs[0].shape
+    outer = outer_refs[0].shape[0]
+    rows, width = inner + outer, outer // 2
     mix_high, mix_low = split(mix_ref[...])
     dot = functools.partial(jnp.dot, preferred_element_type=jnp.float32)
 
-    @pl.loop(0, rows // 2, unroll=2)
-    def _(pair):
-        r = 2 * pair
-        x = jnp.concatenate(
-            [jnp.concatenate([ref[r + i] for ref in field_refs], axis=0) for i in range(2)], axis=1
-        )
-        high, low = split(x)
+    def part(r):
+        if width <= r < rows - width:
+            return jnp.concatenate([ref[r - width] for ref in inner_refs], axis=0)
+        return jnp.concatenate([ref[r if r < width else r - inner] for ref in outer_refs], axis=0)
+
+    for r in range(0, rows, 2):
+        high, low = split(jnp.concatenate([part(r), part(r + 1)], axis=1))
         fresh = dot(mix_high, high) + (dot(mix_high, low) + dot(mix_low, high))
         for i in range(2):
             out_ref[pl.ds(r + i, mem, stride=rows), :] = fresh[:, i * cols:(i + 1) * cols]
@@ -209,30 +253,44 @@
     ens = lax.axis_size("ens")
     members = mem * ens
     observed = obs_values.shape[1]
+    width = FSTEPS
     f32 = functools.partial(jax.ShapeDtypeStruct, dtype=jnp.float32)
+    scratch = functools.partial(pltpu.VMEM, dtype=jnp.float32)
     place = lax.axis_index("dom").astype(jnp.int32).reshape(1)
-
-    def edge(part):
-        coefs = jnp.stack([row_courant[part], col_courant[part], diffusion[part]], axis=1)
-        return jnp.concatenate([state[:, part].transpose(1, 0, 2), coefs], axis=1)
-
-    up = shift(edge(slice(rows - FSTEPS, rows)), "dom", 1)
-    down = shift(edge(slice(0, FSTEPS)), "dom", -1)
-    span = rows + 2 * FSTEPS
-    field, seen = pl.pallas_call(
-        forecast_kernel,
-        out_shape=(f32((rows, mem, cols)), f32((mem, observed))),
-        in_specs=[SMEM] * 3 + [VMEM] * 6,
+    state = state.reshape(mem * rows, cols)
+    coefs = (row_courant, col_courant, diffusion)
+
+    top, bottom = pl.pallas_call(
+        edge_kernel,
+        out_shape=(f32((width, mem + 8, cols)),) * 2,
+        in_specs=[VMEM] * 4,
         out_specs=(VMEM, VMEM),
-        scratch_shapes=[
-            pltpu.VMEM((span, mem, cols), jnp.float32),
-            pltpu.VMEM((span, mem, cols), jnp.float32),
-            pltpu.VMEM((4, span, 8, cols), jnp.float32),
-        ],
-        compiler_params=PARAMS,
-        name="forecast",
-    )(place, owners, obs_offsets, state.reshape(mem * rows, cols), row_courant, col_courant,
-      diffusion, up, down)
+        compiler_params=PARAMS,
+        cost_estimate=estimate(0.5),
+        name="edges",
+    )(state, *coefs)
+    up = shift(bottom, "dom", 1)
+    down = shift(top, "dom", -1)
+    inner = pl.pallas_call(
+        inner_kernel,
+        out_shape=f32((rows - 2 * width, mem, cols)),
+        in_specs=[VMEM] * 4,
+        out_specs=VMEM,
+        scratch_shapes=[scratch((rows, mem, cols))] * 2,
+        compiler_params=PARAMS,
+        cost_estimate=estimate(2),
+        name="inner",
+    )(state, *coefs)
+    outer, seen = pl.pallas_call(
+        outer_kernel,
+        out_shape=(f32((2 * width, mem, cols)), f32((mem, observed))),
+        in_specs=[SMEM] * 3 + [VMEM] * 7,
+        out_specs=(VMEM, VMEM),
+        scratch_shapes=[scratch((3 * width, mem, cols))] * 2 + [scratch((rows, mem, cols))],
+        compiler_params=PARAMS,
+        cost_estimate=estimate(3),
+        name="outer",
+    )(place, owners, obs_offsets, state, *coefs, up, down, inner)
 
     seens = [seen] + [shift(seen, "ens", k) for k in range(1, ens)]
     gram = pl.pallas_call(
@@ -241,13 +299,20 @@
         in_specs=[SMEM] * 2 + [VMEM] * (2 + ens),
         out_specs=VMEM,
         compiler_params=PARAMS,
+        cost_estimate=estimate(1),
         name="gram",
     )(place, owners, obs_values, obs_variance, *seens)
     grams = lax.all_gather(gram, "dom")
 
-    fields = [field]
-    for _ in range(1, ens):
-        fields.append(shift(fields[-1], "ens", 1))
+    def around(part):
+        slots = [part] * ens
+        for j in range(1, ens // 2 + 1):
+            slots[j] = shift(slots[j - 1], "ens", 1)
+        for j in range(1, (ens - 1) // 2 + 1):
+            slots[ens - j] = shift(slots[(ens - j + 1) % ens], "ens", -1)
+        return slots
+
+    fields = [x for pair in zip(around(inner), around(outer)) for x in pair]
 
     mix = pl.pallas_call(
         chain_kernel,
@@ -255,17 +320,16 @@
         in_specs=[SMEM, VMEM],
         out_specs=VMEM,
         compiler_params=PARAMS,
-        cost_estimate=pl.CostEstimate(
-            flops=2 * 4 * 20 * members**3, bytes_accessed=grams.size * 4, transcendentals=0
-        ),
+        cost_estimate=estimate(8),
         name="chain",
     )(owners, grams)
     out = pl.pallas_call(
         apply_kernel,
         out_shape=f32((mem * rows, cols)),
-        in_specs=[VMEM] * (1 + ens),
+        in_specs=[VMEM] * (1 + 2 * ens),
         out_specs=VMEM,
         compiler_params=PARAMS,
+        cost_estimate=estimate(2),
         name="apply",
     )(mix, *fields)
     return out.reshape(mem, rows, cols)

time: 92.5 us -> 60.9 us (0.66)
  waiting for transfers between devices: 45.2 us -> 9.12 us
  starting transfers between devices: 10.2 us -> 21.6 us
  Pallas kernels: 23.1 us -> 15.7 us
    ppermute x8 -> x11, waiting for transfers between devices: 45.2 us -> 9.12 us  [shift(): lax.ppermute(x, axis, [(i, (i + step) % count) for i in range(count)])]
    ppermute x8 -> x11, starting transfers between devices: 10.2 us -> 21.6 us  [shift(): lax.ppermute(x, axis, [(i, (i + step) % count) for i in range(count)])]
    pallas_call x1 -> x3, Pallas kernels: 11.8 us -> 5.74 us  [the longest x1 4.39 us: on_device(): pl.pallas_call(outer_kernel, out_shape=(f32((2 * width, mem, cols)), f32(...]
    slice x4 -> x0, local copies, waits for them, and re-layouts: 3.17 us -> none  [the longest x1 0.99 us: edge(): return jnp.concatenate([state[:, part].transpose(1, 0, 2), coefs], axis=1)]
    unnamed x18 -> x24, local copies, waits for them, and re-layouts: 0.66 us -> 3.83 us
    pallas_call x1, Pallas kernels: 2.6 us -> 1.53 us  [on_device(): pl.pallas_call(apply_kernel, out_shape=f32((mem * rows, cols)), in_specs=...]
  transfers between devices with their start and end apart: 8 -> 11, of which waited for: 7 -> 3; matrix products, arithmetic and copies ran while one was open for 0% -> 0% of each run, Pallas kernels for 9% -> 23%
where the time goes in v2:
time: 60.9 us; the launch traced here: 60.5 us
  starting transfers between devices  21.6 us (35%)
  Pallas kernels  15.7 us (26%)
  blocking collectives  10.2 us (17%)
  waiting for transfers between devices  9.12 us (15%)
  local copies, waits for them, and re-layouts  3.83 us (6%)
    ppermute x11, starting transfers between devices, shift(): lax.ppermute(x, axis, [(i, (i + step) % count) for i in range(count)])  21.6 us
    all_gather x1, blocking collectives, on_device(): grams = lax.all_gather(gram, 'dom')  10.2 us
    ppermute x11, waiting for transfers between devices, shift(): lax.ppermute(x, axis, [(i, (i + step) % count) for i in range(count)])  9.12 us
    pallas_call x1, Pallas kernels, on_device(): pl.pallas_call(chain_kernel, out_shape=f32((mem, members)), in_specs=[SME...  7.56 us
    pallas_call x1, Pallas kernels, on_device(): pl.pallas_call(outer_kernel, out_shape=(f32((2 * width, mem, cols)), f32(...  4.39 us
    unnamed x24, local copies, waits for them, and re-layouts  3.83 us
    pallas_call x1, Pallas kernels, on_device(): pl.pallas_call(apply_kernel, out_shape=f32((mem * rows, cols)), in_specs=...  1.53 us
    pallas_call x1, Pallas kernels, on_device(): pl.pallas_call(inner_kernel, out_shape=f32((rows - 2 * width, mem, cols))...  1.26 us
  transfers between devices with their start and end apart: 11, of which 3 were waited for; matrix products, arithmetic and copies ran while one was open for 0% of the time, Pallas kernels for 23%

profile of v2, /device:TPU:0, one launch (start us, length us, event | category | flops | bytes accessed | tf_op | source)
XLA Modules:
  0.0 60.5 jit_solution(11097785348032275114)
XLA Ops:
  0.0 1.0 %copy-done = f32[32,32,128]{2,1,0:T(8,128)S(1)} copy-done((f32[32,32,128]{2,1,0:T(8,128)S(1)}, f32[32,32,128]{2,1,0:T(8,128)}, u32[]{:S(2)}) %copy-start) | copy-done | bytes 524312
  1.0 0.7 %copy-done.2 = f32[32,128]{1,0:T(8,128)S(1)} copy-done((f32[32,128]{1,0:T(8,128)S(1)}, f32[32,128]{1,0:T(8,128)}, u32[]{:S(2)}) %copy-start.2) | copy-done | bytes 16408
  1.8 0.7 %copy-done.4 = f32[32,128]{1,0:T(8,128)S(1)} copy-done((f32[32,128]{1,0:T(8,128)S(1)}, f32[32,128]{1,0:T(8,128)}, u32[]{:S(2)}) %copy-start.4) | copy-done | bytes 16408
  2.5 0.7 %copy-done.6 = f32[32,128]{1,0:T(8,128)S(1)} copy-done((f32[32,128]{1,0:T(8,128)S(1)}, f32[32,128]{1,0:T(8,128)}, u32[]{:S(2)}) %copy-start.6) | copy-done | bytes 16408
  3.2 0.1 edges.1
  3.3 0.5 collective-permute-start
  3.8 3.0 %collective-permute-start.1 = (f32[4,40,128]{2,1,0:T(8,128)S(1)}, f32[4,40,128]{2,1,0:T(8,128)S(1)}, u32[]{:S(2)}, u32[]{:S(2)}) collective-permute-start(f32[4,40,128]{2,1,0:T(8,128)S(1)} %get-tuple-element.10), channel_id=1, source_target_pairs={{0,7},{1,0},{2,1},{3,2},{4,3},{5,4},{6,5},{7,6},{8,15},{9,8},{10,9... | collective-permute-start | bytes 245768 | tf_op jit(solution)/shard_map/ppermute | solution.py:246
  6.8 1.3 %inner.1.inner_ref.refs_0_ = f32[24,32,128]{2,1,0:T(8,128)S(1)} custom-call(f32[1024,128]{1,0:T(8,128)S(1)} %bitcast.6, f32[32,128]{1,0:T(8,128)S(1)} %copy-done.2, f32[32,128]{1,0:T(8,128)S(1)} %copy-done.4, f32[32,128]{1,0:T(8,128)S(1)} %copy-done.7), custom_call_target="tpu_custom_call" | custom-call | flops 2300000000 | tf_op jit(solution)/shard_map/inner/pallas_call | solution.py:274
  8.1 2.3 %collective-permute-start.5 = (f32[24,32,128]{2,1,0:T(8,128)S(1)}, f32[24,32,128]{2,1,0:T(8,128)S(1)}, u32[]{:S(2)}, u32[]{:S(2)}) collective-permute-start(f32[24,32,128]{2,1,0:T(8,128)S(1)} %inner.1.inner_ref.refs_0_), channel_id=1, source_target_pairs={{0,8},{8,16},{16,24},{24,0},{1,9},{9,17},{17,25},{25,1},{2,10},{10... | collective-permute-start | bytes 1179656 | tf_op jit(solution)/shard_map/ppermute | solution.py:246
  10.4 0.6 copy-done.11
  11.0 4.4 %outer.1 = (f32[8,32,128]{2,1,0:T(8,128)S(1)}, f32[32,256]{1,0:T(8,128)S(1)}) custom-call(s32[1]{0:T(128)} %bitcast.place_ref, s32[4]{0:T(128)S(1)} %copy-done.11, s32[4,256]{1,0:T(4,128)S(1)} %copy-done.8, f32[1024,128]{1,0:T(8,128)S(1)} %bitcast.7, f32[32,128]{1,0:T(8,128)S(1)} %copy-done.3, f32[32,128]{1,0:T(8,128)S(1)} %copy-done.5, ...), custom_call_target="tpu_custom_call" | custom-call | flops 3449999872 | tf_op jit(solution)/shard_map/outer/pallas_call | solution.py:284
  15.4 1.6 %collective-permute-start.2 = (f32[32,256]{1,0:T(8,128)S(1)}, f32[32,256]{1,0:T(8,128)S(1)}, u32[]{:S(2)}, u32[]{:S(2)}) collective-permute-start(f32[32,256]{1,0:T(8,128)S(1)} %get-tuple-element.11.refs_0_), channel_id=1, source_target_pairs={{0,8},{8,16},{16,24},{24,0},{1,9},{9,17},{17,25},{25,1},{2,10},{10... | collective-permute-start | bytes 98312 | tf_op jit(solution)/shard_map/ppermute | solution.py:246
  17.0 1.2 %collective-permute-start.3 = (f32[32,256]{1,0:T(8,128)S(1)}, f32[32,256]{1,0:T(8,128)S(1)}, u32[]{:S(2)}, u32[]{:S(2)}) collective-permute-start(f32[32,256]{1,0:T(8,128)S(1)} %get-tuple-element.11.refs_0_), channel_id=1, source_target_pairs={{0,16},{8,24},{16,0},{24,8},{1,17},{9,25},{17,1},{25,9},{2,18},{10... | collective-permute-start | bytes 98312 | tf_op jit(solution)/shard_map/ppermute | solution.py:246
  18.2 2.7 %collective-permute-start.4 = (f32[32,256]{1,0:T(8,128)S(1)}, f32[32,256]{1,0:T(8,128)S(1)}, u32[]{:S(2)}, u32[]{:S(2)}) collective-permute-start(f32[32,256]{1,0:T(8,128)S(1)} %get-tuple-element.11.refs_0_), channel_id=1, source_target_pairs={{0,24},{8,0},{16,8},{24,16},{1,25},{9,1},{17,9},{25,17},{2,26},{10... | collective-permute-start | bytes 98312 | tf_op jit(solution)/shard_map/ppermute | solution.py:246
  21.0 0.4 collective-permute-start.9
  21.4 0.7 %collective-permute-done.2.refs_1_ = f32[32,256]{1,0:T(8,128)S(1)} collective-permute-done((f32[32,256]{1,0:T(8,128)S(1)}, f32[32,256]{1,0:T(8,128)S(1)}, u32[]{:S(2)}, u32[]{:S(2)}) %collective-permute-start.2) | collective-permute-done | bytes 32800 | tf_op jit(solution)/shard_map/ppermute | solution.py:246
  22.1 0.8 %collective-permute-start.6 = (f32[8,32,128]{2,1,0:T(8,128)S(1)}, f32[8,32,128]{2,1,0:T(8,128)S(1)}, u32[]{:S(2)}, u32[]{:S(2)}) collective-permute-start(f32[8,32,128]{2,1,0:T(8,128)S(1)} %get-tuple-element.12.refs_1_), channel_id=1, source_target_pairs={{0,8},{8,16},{16,24},{24,0},{1,9},{9,17},{17,25},{25,1},{2,10},{10... | collective-permute-start | bytes 393224 | tf_op jit(solution)/shard_map/ppermute | solution.py:246
  23.0 8.9 %collective-permute-start.10 = (f32[8,32,128]{2,1,0:T(8,128)S(1)}, f32[8,32,128]{2,1,0:T(8,128)S(1)}, u32[]{:S(2)}, u32[]{:S(2)}) collective-permute-start(f32[8,32,128]{2,1,0:T(8,128)S(1)} %get-tuple-element.12.refs_1_), channel_id=1, source_target_pairs={{0,24},{8,0},{16,8},{24,16},{1,25},{9,1},{17,9},{25,17},{2,26},{10... | collective-permute-start | bytes 393224 | tf_op jit(solution)/shard_map/ppermute | solution.py:246
  31.9 0.9 %gram.1 = f32[136,128]{1,0:T(8,128)S(1)} custom-call(s32[1]{0:T(128)} %bitcast.place_ref, s32[4]{0:T(128)S(1)} %copy-done.11, f32[4,256]{1,0:T(4,128)S(1)} %copy-done.9, f32[4,256]{1,0:T(4,128)S(1)} %copy-done.10, f32[32,256]{1,0:T(8,128)S(1)} %get-tuple-element.11.refs_0_, f32[32,256]{1,0:T(8,128)S(1)} %collective-permute-done.2.refs_1_, ...), custom_call_target="tpu_custom_call" | custom-call | flops 1150000000 | tf_op jit(solution)/shard_map/gram/pallas_call | solution.py:296
  32.8 10.2 %all-gather = f32[1088,128]{1,0:T(8,128)S(1)} all-gather(f32[136,128]{1,0:T(8,128)S(1)} %gram.1), channel_id=2, replica_groups=mesh['ens'=4,'dom'=8] {'dom'}, dimensions={0}, use_global_device_ids=true | all-gather | bytes 626688 | tf_op jit(solution)/shard_map/all_gather | solution.py:305
  43.0 7.6 %chain.1.mix_ref = f32[32,128]{1,0:T(8,128)S(1)} custom-call(s32[4]{0:T(128)S(1)} %copy-done.11, f32[8,136,128]{2,1,0:T(8,128)S(1)} %bitcast.4), custom_call_target="tpu_custom_call" | custom-call | flops 9200000000 | tf_op jit(solution)/shard_map/chain/pallas_call | solution.py:317
  50.6 0.5 collective-permute-done.8.refs_5_
  51.1 7.9 %collective-permute-done.7.refs_4_ = f32[24,32,128]{2,1,0:T(8,128)S(1)} collective-permute-done((f32[24,32,128]{2,1,0:T(8,128)S(1)}, f32[24,32,128]{2,1,0:T(8,128)S(1)}, u32[]{:S(2)}, u32[]{:S(2)}) %collective-permute-start.7) | collective-permute-done | bytes 393248 | tf_op jit(solution)/shard_map/ppermute | solution.py:246
  59.0 1.5 %apply.1 = f32[1024,128]{1,0:T(8,128)} custom-call(f32[32,128]{1,0:T(8,128)S(1)} %chain.1.mix_ref, f32[24,32,128]{2,1,0:T(8,128)S(1)} %inner.1.inner_ref.refs_0_, f32[8,32,128]{2,1,0:T(8,128)S(1)} %get-tuple-element.12.refs_1_, f32[24,32,128]{2,1,0:T(8,128)S(1)} %collective-permute-done.5.refs_2_, f32[8,32,128]{2,1,0:T(8,128)S(1)} %collective-permute-done.6.refs_3_, ...), custom_call_target="tpu_custom_call" | custom-call | flops 2300000000 | tf_op jit(solution)/shard_map/apply/pallas_call | solution.py:326
  (29 shorter events, 0.1 us)
Async XLA Ops:
  0.0 1.0 %copy-start = (f32[32,32,128]{2,1,0:T(8,128)S(1)}, f32[32,32,128]{2,1,0:T(8,128)}, u32[]{:S(2)}) copy-start(f32[32,32,128]{2,1,0:T(8,128)} %param.8) | copy-start | bytes 1572868
  1.0 0.7 %copy-start.2 = (f32[32,128]{1,0:T(8,128)S(1)}, f32[32,128]{1,0:T(8,128)}, u32[]{:S(2)}) copy-start(f32[32,128]{1,0:T(8,128)} %row_ref.5) | copy-start | bytes 49156
  1.8 0.7 %copy-start.4 = (f32[32,128]{1,0:T(8,128)S(1)}, f32[32,128]{1,0:T(8,128)}, u32[]{:S(2)}) copy-start(f32[32,128]{1,0:T(8,128)} %col_ref.5) | copy-start | bytes 49156
  2.5 0.7 %copy-start.6 = (f32[32,128]{1,0:T(8,128)S(1)}, f32[32,128]{1,0:T(8,128)}, u32[]{:S(2)}) copy-start(f32[32,128]{1,0:T(8,128)} %diff_ref.5) | copy-start | bytes 49156
  3.2 3.6 %copy-start.7 = (f32[32,128]{1,0:T(8,128)S(1)}, f32[32,128]{1,0:T(8,128)}, u32[]{:S(2)}) copy-start(f32[32,128]{1,0:T(8,128)} %diff_ref.5) | copy-start | bytes 49156
  3.3 7.1 %collective-permute-start = (f32[4,40,128]{2,1,0:T(8,128)S(1)}, f32[4,40,128]{2,1,0:T(8,128)S(1)}, u32[]{:S(2)}, u32[]{:S(2)}) collective-permute-start(f32[4,40,128]{2,1,0:T(8,128)S(1)} %get-tuple-element.9), channel_id=1, source_target_pairs={{0,1},{1,2},{2,3},{3,4},{4,5},{5,6},{6,7},{7,0},{8,9},{9,10},{10,1... | collective-permute-start | bytes 245768 | tf_op jit(solution)/shard_map/ppermute | solution.py:246
  3.8 6.6 %copy-start.1 = (f32[32,32,128]{2,1,0:T(8,128)S(1)}, f32[32,32,128]{2,1,0:T(8,128)}, u32[]{:S(2)}) copy-start(f32[32,32,128]{2,1,0:T(8,128)} %param.8) | copy-start | bytes 1572868
  3.8 6.6 %copy-start.3 = (f32[32,128]{1,0:T(8,128)S(1)}, f32[32,128]{1,0:T(8,128)}, u32[]{:S(2)}) copy-start(f32[32,128]{1,0:T(8,128)} %row_ref.5) | copy-start | bytes 49156
  3.8 6.6 %copy-start.5 = (f32[32,128]{1,0:T(8,128)S(1)}, f32[32,128]{1,0:T(8,128)}, u32[]{:S(2)}) copy-start(f32[32,128]{1,0:T(8,128)} %col_ref.5) | copy-start | bytes 49156
  3.8 6.6 %collective-permute-start.1 = (f32[4,40,128]{2,1,0:T(8,128)S(1)}, f32[4,40,128]{2,1,0:T(8,128)S(1)}, u32[]{:S(2)}, u32[]{:S(2)}) collective-permute-start(f32[4,40,128]{2,1,0:T(8,128)S(1)} %get-tuple-element.10), channel_id=1, source_target_pairs={{0,7},{1,0},{2,1},{3,2},{4,3},{5,4},{6,5},{7,6},{8,15},{9,8},{10,9... | collective-permute-start | bytes 245768 | tf_op jit(solution)/shard_map/ppermute | solution.py:246
  8.0 2.3 %copy-start.8 = (s32[4,256]{1,0:T(4,128)S(1)}, s32[4,256]{1,0:T(4,128)}, u32[]{:S(2)}) copy-start(s32[4,256]{1,0:T(4,128)} %offsets_ref.1) | copy-start | bytes 12292
  8.1 34.9 %collective-permute-start.5 = (f32[24,32,128]{2,1,0:T(8,128)S(1)}, f32[24,32,128]{2,1,0:T(8,128)S(1)}, u32[]{:S(2)}, u32[]{:S(2)}) collective-permute-start(f32[24,32,128]{2,1,0:T(8,128)S(1)} %inner.1.inner_ref.refs_0_), channel_id=1, source_target_pairs={{0,8},{8,16},{16,24},{24,0},{1,9},{9,17},{17,25},{25,1},{2,10},{10... | collective-permute-start | bytes 1179656 | tf_op jit(solution)/shard_map/ppermute | solution.py:246
  10.4 0.7 %copy-start.11 = (s32[4]{0:T(128)S(1)}, s32[4]{0:T(128)}, u32[]{:S(2)}) copy-start(s32[4]{0:T(128)} %owners_ref.5) | copy-start | bytes 52
  11.0 20.9 %copy-start.9 = (f32[4,256]{1,0:T(4,128)S(1)}, f32[4,256]{1,0:T(4,128)}, u32[]{:S(2)}) copy-start(f32[4,256]{1,0:T(4,128)} %obs_ref.1) | copy-start | bytes 12292
  11.0 20.9 %copy-start.10 = (f32[4,256]{1,0:T(4,128)S(1)}, f32[4,256]{1,0:T(4,128)}, u32[]{:S(2)}) copy-start(f32[4,256]{1,0:T(4,128)} %var_ref.1) | copy-start | bytes 12292
  15.4 6.7 %collective-permute-start.2 = (f32[32,256]{1,0:T(8,128)S(1)}, f32[32,256]{1,0:T(8,128)S(1)}, u32[]{:S(2)}, u32[]{:S(2)}) collective-permute-start(f32[32,256]{1,0:T(8,128)S(1)} %get-tuple-element.11.refs_0_), channel_id=1, source_target_pairs={{0,8},{8,16},{16,24},{24,0},{1,9},{9,17},{17,25},{25,1},{2,10},{10... | collective-permute-start | bytes 98312 | tf_op jit(solution)/shard_map/ppermute | solution.py:246
  17.0 6.0 %collective-permute-start.3 = (f32[32,256]{1,0:T(8,128)S(1)}, f32[32,256]{1,0:T(8,128)S(1)}, u32[]{:S(2)}, u32[]{:S(2)}) collective-permute-start(f32[32,256]{1,0:T(8,128)S(1)} %get-tuple-element.11.refs_0_), channel_id=1, source_target_pairs={{0,16},{8,24},{16,0},{24,8},{1,17},{9,25},{17,1},{25,9},{2,18},{10... | collective-permute-start | bytes 98312 | tf_op jit(solution)/shard_map/ppermute | solution.py:246
  18.2 13.7 %collective-permute-start.4 = (f32[32,256]{1,0:T(8,128)S(1)}, f32[32,256]{1,0:T(8,128)S(1)}, u32[]{:S(2)}, u32[]{:S(2)}) collective-permute-start(f32[32,256]{1,0:T(8,128)S(1)} %get-tuple-element.11.refs_0_), channel_id=1, source_target_pairs={{0,24},{8,0},{16,8},{24,16},{1,25},{9,1},{17,9},{25,17},{2,26},{10... | collective-permute-start | bytes 98312 | tf_op jit(solution)/shard_map/ppermute | solution.py:246
  21.0 30.1 %collective-permute-start.9 = (f32[24,32,128]{2,1,0:T(8,128)S(1)}, f32[24,32,128]{2,1,0:T(8,128)S(1)}, u32[]{:S(2)}, u32[]{:S(2)}) collective-permute-start(f32[24,32,128]{2,1,0:T(8,128)S(1)} %inner.1.inner_ref.refs_0_), channel_id=1, source_target_pairs={{0,24},{8,0},{16,8},{24,16},{1,25},{9,1},{17,9},{25,17},{2,26},{10... | collective-permute-start | bytes 1179656 | tf_op jit(solution)/shard_map/ppermute | solution.py:246
  22.1 20.8 %collective-permute-start.6 = (f32[8,32,128]{2,1,0:T(8,128)S(1)}, f32[8,32,128]{2,1,0:T(8,128)S(1)}, u32[]{:S(2)}, u32[]{:S(2)}) collective-permute-start(f32[8,32,128]{2,1,0:T(8,128)S(1)} %get-tuple-element.12.refs_1_), channel_id=1, source_target_pairs={{0,8},{8,16},{16,24},{24,0},{1,9},{9,17},{17,25},{25,1},{2,10},{10... | collective-permute-start | bytes 393224 | tf_op jit(solution)/shard_map/ppermute | solution.py:246
  23.0 27.6 %collective-permute-start.10 = (f32[8,32,128]{2,1,0:T(8,128)S(1)}, f32[8,32,128]{2,1,0:T(8,128)S(1)}, u32[]{:S(2)}, u32[]{:S(2)}) collective-permute-start(f32[8,32,128]{2,1,0:T(8,128)S(1)} %get-tuple-element.12.refs_1_), channel_id=1, source_target_pairs={{0,24},{8,0},{16,8},{24,16},{1,25},{9,1},{17,9},{25,17},{2,26},{10... | collective-permute-start | bytes 393224 | tf_op jit(solution)/shard_map/ppermute | solution.py:246
  43.0 8.1 %collective-permute-start.8 = (f32[8,32,128]{2,1,0:T(8,128)S(1)}, f32[8,32,128]{2,1,0:T(8,128)S(1)}, u32[]{:S(2)}, u32[]{:S(2)}) collective-permute-start(f32[8,32,128]{2,1,0:T(8,128)S(1)} %collective-permute-done.6.refs_3_), channel_id=1, source_target_pairs={{0,8},{8,16},{16,24},{24,0},{1,9},{9,17},{17,25},{25,1},{2,10},{10... | collective-permute-start | bytes 393224 | tf_op jit(solution)/shard_map/ppermute | solution.py:246
  43.0 16.0 %collective-permute-start.7 = (f32[24,32,128]{2,1,0:T(8,128)S(1)}, f32[24,32,128]{2,1,0:T(8,128)S(1)}, u32[]{:S(2)}, u32[]{:S(2)}) collective-permute-start(f32[24,32,128]{2,1,0:T(8,128)S(1)} %collective-permute-done.5.refs_2_), channel_id=1, source_target_pairs={{0,8},{8,16},{16,24},{24,0},{1,9},{9,17},{17,25},{25,1},{2,10},{10... | collective-permute-start | bytes 1179656 | tf_op jit(solution)/shard_map/ppermute | solution.py:246

commit v3 on v2

--- a/solution.py
+++ b/solution.py
@@ -10,6 +10,7 @@
 FSTEPS = 4
 TOLERANCE = 1e-6
 WIDE_BOUND = 16.0
+CHAIN_US = 2
 HIGHEST = lax.Precision.HIGHEST
 NN = (((1,), (0,)), ((), ()))
 NT = (((1,), (1,)), ((), ()))
@@ -28,22 +29,6 @@
 
 def estimate(micros):
     return pl.CostEstimate(flops=int(1.15e9 * micros), bytes_accessed=0, transcendentals=0)
-
-
-def edge_kernel(state_ref, row_ref, col_ref, diff_ref, top_ref, bottom_ref):
-    width, _, cols = top_ref.shape
-    rows = row_ref.shape[0]
-    mem = state_ref.shape[0] // rows
-    for r in range(width):
-        for ref, row in ((top_ref, r), (bottom_ref, rows - width + r)):
-            ref[r, :mem, :] = state_ref[pl.ds(row, mem, stride=rows), :]
-            for i, coef in enumerate((row_ref, col_ref, diff_ref)):
-                ref[r, mem + i:mem + i + 1, :] = coef[row:row + 1, :]
-            ref[r, mem + 3:, :] = jnp.zeros((ref.shape[1] - mem - 3, cols), jnp.float32)
-
-
-def mixers(row_c, col_c, diff_c):
-    return 1.0 - row_c - col_c - 4.0 * diff_c, row_c + diff_c, col_c + diff_c, diff_c
 
 
 def advance(load, coef, store, count, scratches):
@@ -65,72 +50,75 @@
                 scratches[(step + 1) % 2][r] = fresh
 
 
-def inner_kernel(state_ref, row_ref, col_ref, diff_ref, inner_ref, a_ref, b_ref):
-    rows = row_ref.shape[0]
+def inner_kernel(
+    state_ref, coef_ref, top_ref, upper_ref, lower_ref, bottom_ref, inner_ref, a_ref, b_ref
+):
+    width = FSTEPS
+    count, rows, cols = coef_ref.shape
     mem = state_ref.shape[0] // rows
 
     def load(r):
         return state_ref[pl.ds(r, mem, stride=rows), :]
 
+    blocks = (top_ref, 0), (upper_ref, width), (lower_ref, rows - 2 * width), (bottom_ref, rows - width)
+    for ref, base in blocks:
+        for r in range(width):
+            ref[r, :mem, :] = load(base + r)
+            for i in range(count):
+                ref[r, mem + i:mem + i + 1, :] = coef_ref[i, base + r:base + r + 1, :]
+            ref[r, mem + count:, :] = jnp.zeros((ref.shape[1] - mem - count, cols), jnp.float32)
+
     def coef(r):
-        return mixers(row_ref[r:r + 1, :], col_ref[r:r + 1, :], diff_ref[r:r + 1, :])
+        return [coef_ref[i, r:r + 1, :] for i in range(count)]
 
     def store(r, value):
-        inner_ref[r - FSTEPS] = value
+        inner_ref[r - width] = value
 
     advance(load, coef, store, rows, (a_ref, b_ref))
 
 
+def split3(x):
+    high, rest = x.astype(jnp.bfloat16), x
+    rest = rest - high.astype(jnp.float32)
+    middle = rest.astype(jnp.bfloat16)
+    return high, middle, (rest - middle.astype(jnp.float32)).astype(jnp.bfloat16)
+
+
 def outer_kernel(
-    place_ref, owners_ref, offsets_ref, state_ref, row_ref, col_ref, diff_ref, up_ref, down_ref,
-    inner_ref, outer_ref, seen_ref, a_ref, b_ref, field_ref,
+    place_ref, owners_ref, offsets_ref, up_ref, top_ref, upper_ref, lower_ref, bottom_ref, down_ref,
+    inner_ref, outer_ref, seen_ref, a_ref, b_ref,
 ):
     width = FSTEPS
-    rows, mem, cols = field_ref.shape
-
-    for side in range(2):
-        base = rows - 2 * width if side else -width
-
-        def place(r, side=side):
-            row = r + (rows - 2 * width if side else -width)
-            if row < 0:
-                return up_ref, row + width
-            if row >= rows:
-                return down_ref, row - rows
-            return None, row
-
-        def load(r, place=place):
-            ref, row = place(r)
-            return state_ref[pl.ds(row, mem, stride=rows), :] if ref is None else ref[row, :mem, :]
-
-        def coef(r, place=place):
-            ref, row = place(r)
-            if ref is None:
-                return mixers(*[c[row:row + 1, :] for c in (row_ref, col_ref, diff_ref)])
-            return mixers(*[ref[row, mem + i:mem + i + 1, :] for i in range(3)])
-
-        def store(r, value, side=side, base=base):
+    inner, mem, cols = inner_ref.shape
+    rows = inner + 2 * width
+    observed = seen_ref.shape[1]
+
+    for side, refs in enumerate(((up_ref, top_ref, upper_ref), (lower_ref, bottom_ref, down_ref))):
+
+        def load(r, refs=refs):
+            return refs[r // width][r % width, :mem, :]
+
+        def coef(r, refs=refs):
+            return [refs[r // width][r % width, mem + i:mem + i + 1, :] for i in range(4)]
+
+        def store(r, value, side=side):
             outer_ref[side * width + r - width] = value
-            field_ref[r + base] = value
 
         advance(load, coef, store, 3 * width, (a_ref, b_ref))
 
-    for r in range(rows - 2 * width):
-        field_ref[width + r] = inner_ref[r]
-
-    batch = own_batch(place_ref, owners_ref)
-    lanes = lax.broadcasted_iota(jnp.int32, (mem, cols), 1)
-    for part in range(seen_ref.shape[1] // cols):
-
-        def pick(k, total, part=part):
-            cell = offsets_ref[batch, part * cols + k]
-            row = cell // cols
-            lane = cell - row * cols
-            moved = pltpu.roll(field_ref[row], lax.rem(k - lane + cols, cols), 1)
-            return jnp.where(lanes == k, moved, total)
-
-        total = lax.fori_loop(0, cols, pick, jnp.zeros((mem, cols), jnp.float32), unroll=32)
-        seen_ref[:, part * cols:(part + 1) * cols] = total
+    def field(r):
+        if width <= r < rows - width:
+            return inner_ref[r - width]
+        return outer_ref[r if r < width else r - inner]
+
+    cells = offsets_ref[pl.ds(own_batch(place_ref, owners_ref), 1), :]
+    index = lax.broadcasted_iota(jnp.int32, (2 * cols, observed), 0)
+    total = jnp.zeros((3 * mem, observed), jnp.float32)
+    for r in range(0, rows, 2):
+        parts = jnp.concatenate(split3(jnp.concatenate([field(r), field(r + 1)], axis=1)), axis=0)
+        chosen = (index == cells - r * cols).astype(jnp.float32).astype(jnp.bfloat16)
+        total = total + jnp.dot(parts, chosen, preferred_element_type=jnp.float32)
+    seen_ref[...] = total[:mem] + total[mem:2 * mem] + total[2 * mem:]
 
 
 def gram_kernel(place_ref, owners_ref, obs_ref, var_ref, *refs):
@@ -257,40 +245,35 @@
     f32 = functools.partial(jax.ShapeDtypeStruct, dtype=jnp.float32)
     scratch = functools.partial(pltpu.VMEM, dtype=jnp.float32)
     place = lax.axis_index("dom").astype(jnp.int32).reshape(1)
-    state = state.reshape(mem * rows, cols)
-    coefs = (row_courant, col_courant, diffusion)
-
-    top, bottom = pl.pallas_call(
-        edge_kernel,
-        out_shape=(f32((width, mem + 8, cols)),) * 2,
-        in_specs=[VMEM] * 4,
-        out_specs=(VMEM, VMEM),
-        compiler_params=PARAMS,
-        cost_estimate=estimate(0.5),
-        name="edges",
-    )(state, *coefs)
+    mixers = jnp.stack([
+        1.0 - row_courant - col_courant - 4.0 * diffusion,
+        row_courant + diffusion,
+        col_courant + diffusion,
+        diffusion,
+    ])
+    edge = f32((width, mem + 8, cols))
+    top, upper, lower, bottom, inner = pl.pallas_call(
+        inner_kernel,
+        out_shape=(edge,) * 4 + (f32((rows - 2 * width, mem, cols)),),
+        in_specs=[VMEM] * 2,
+        out_specs=(VMEM,) * 5,
+        scratch_shapes=[scratch((rows, mem, cols))] * 2,
+        compiler_params=PARAMS,
+        cost_estimate=estimate(3),
+        name="inner",
+    )(state.reshape(mem * rows, cols), mixers)
     up = shift(bottom, "dom", 1)
     down = shift(top, "dom", -1)
-    inner = pl.pallas_call(
-        inner_kernel,
-        out_shape=f32((rows - 2 * width, mem, cols)),
-        in_specs=[VMEM] * 4,
-        out_specs=VMEM,
-        scratch_shapes=[scratch((rows, mem, cols))] * 2,
-        compiler_params=PARAMS,
-        cost_estimate=estimate(2),
-        name="inner",
-    )(state, *coefs)
     outer, seen = pl.pallas_call(
         outer_kernel,
         out_shape=(f32((2 * width, mem, cols)), f32((mem, observed))),
-        in_specs=[SMEM] * 3 + [VMEM] * 7,
+        in_specs=[SMEM] * 2 + [VMEM] * 8,
         out_specs=(VMEM, VMEM),
-        scratch_shapes=[scratch((3 * width, mem, cols))] * 2 + [scratch((rows, mem, cols))],
-        compiler_params=PARAMS,
-        cost_estimate=estimate(3),
+        scratch_shapes=[scratch((3 * width, mem, cols))] * 2,
+        compiler_params=PARAMS,
+        cost_estimate=estimate(2),
         name="outer",
-    )(place, owners, obs_offsets, state, *coefs, up, down, inner)
+    )(place, owners, obs_offsets, up, top, upper, lower, bottom, down, inner)
 
     seens = [seen] + [shift(seen, "ens", k) for k in range(1, ens)]
     gram = pl.pallas_call(
@@ -320,7 +303,7 @@
         in_specs=[SMEM, VMEM],
         out_specs=VMEM,
         compiler_params=PARAMS,
-        cost_estimate=estimate(8),
+        cost_estimate=estimate(CHAIN_US),
         name="chain",
     )(owners, grams)
     out = pl.pallas_call(

time: 60.9 us -> 48.7 us (0.80)
  starting transfers between devices: 21.6 us -> 16 us
  Pallas kernels: 15.7 us -> 12.9 us
  waiting for transfers between devices: 9.12 us -> 6.87 us
  local copies, waits for them, and re-layouts: 3.83 us -> 1.7 us
  other arithmetic: 0 us -> 0.8 us
    ppermute x11, starting transfers between devices: 21.6 us -> 16 us  [shift(): lax.ppermute(x, axis, [(i, (i + step) % count) for i in range(count)])]
    pallas_call x1, Pallas kernels: 4.39 us -> 1.53 us  [on_device(): pl.pallas_call(outer_kernel, out_shape=(f32((2 * width, mem, cols)), f32(...]
    ppermute x11, waiting for transfers between devices: 9.12 us -> 6.87 us  [shift(): lax.ppermute(x, axis, [(i, (i + step) % count) for i in range(count)])]
    unnamed x24 -> x12, local copies, waits for them, and re-layouts: 3.83 us -> 1.7 us
    another operation x0 -> x2, other arithmetic: none -> 0.8 us  [on_device(): jnp.stack([1.0 - row_courant - col_courant - 4.0 * diffusion, row_courant...]
    pallas_call x2 -> x1, Pallas kernels: 1.35 us -> 1.39 us  [on_device(): pl.pallas_call(inner_kernel, out_shape=(edge,) * 4 + (f32((rows - 2 * wid...]
  transfers between devices with their start and end apart: 11 -> 11, of which waited for: 3 -> 2; matrix products, arithmetic and copies ran while one was open for 0% -> 0% of each run, Pallas kernels for 23% -> 21%
where the time goes in v3:
time: 48.7 us; the launch traced here: 48.4 us
  starting transfers between devices  16 us (33%)
  Pallas kernels  12.9 us (26%)
  blocking collectives  10.1 us (21%)
  waiting for transfers between devices  6.87 us (14%)
  local copies, waits for them, and re-layouts  1.7 us (3%)
  other arithmetic  0.8 us (2%)
    ppermute x11, starting transfers between devices, shift(): lax.ppermute(x, axis, [(i, (i + step) % count) for i in range(count)])  16 us
    all_gather x1, blocking collectives, on_device(): grams = lax.all_gather(gram, 'dom')  10.1 us
    pallas_call x1, Pallas kernels, on_device(): pl.pallas_call(chain_kernel, out_shape=f32((mem, members)), in_specs=[SME...  7.57 us
    ppermute x11, waiting for transfers between devices, shift(): lax.ppermute(x, axis, [(i, (i + step) % count) for i in range(count)])  6.87 us
    unnamed x12, local copies, waits for them, and re-layouts  1.7 us
    pallas_call x1, Pallas kernels, on_device(): pl.pallas_call(outer_kernel, out_shape=(f32((2 * width, mem, cols)), f32(...  1.53 us
    pallas_call x1, Pallas kernels, on_device(): pl.pallas_call(apply_kernel, out_shape=f32((mem * rows, cols)), in_specs=...  1.53 us
    pallas_call x1, Pallas kernels, on_device(): pl.pallas_call(inner_kernel, out_shape=(edge,) * 4 + (f32((rows - 2 * wid...  1.39 us
  transfers between devices with their start and end apart: 11, of which 2 were waited for; matrix products, arithmetic and copies ran while one was open for 0% of the time, Pallas kernels for 21%

profile of v3, /device:TPU:0, one launch (start us, length us, event | category | flops | bytes accessed | tf_op | source)
XLA Modules:
  0.0 48.4 jit_solution(7976652631295324836)
XLA Ops:
  0.0 0.8 %subtract_bitcast_fusion = (f32[1,32,128]{2,1,0:T(8,128)S(1)}, f32[1,32,128]{2,1,0:T(8,128)S(1)}, f32[1,32,128]{2,1,0:T(8,128)S(1)}) fusion(f32[32,128]{1,0:T(8,128)} %param.11, f32[32,128]{1,0:T(8,128)} %param.10, f32[32,128]{1,0:T(8,128)} %param.9), kind=kLoop, calls=%fused_computation.3 | loop fusion | flops 24576 | bytes 98304 | tf_op jit(solution)/shard_map/stack | solution.py:248
  0.8 0.0 copy-start
  0.8 1.0 %copy-done = f32[32,32,128]{2,1,0:T(8,128)S(1)} copy-done((f32[32,32,128]{2,1,0:T(8,128)S(1)}, f32[32,32,128]{2,1,0:T(8,128)}, u32[]{:S(2)}) %copy-start) | copy-done | bytes 524312
  1.9 1.4 %inner.1 = (f32[4,40,128]{2,1,0:T(8,128)S(1)}, f32[4,40,128]{2,1,0:T(8,128)S(1)}, f32[4,40,128]{2,1,0:T(8,128)S(1)}, f32[4,40,128]{2,1,0:T(8,128)S(1)}, f32[24,32,128]{2,1,0:T(8,128)S(1)}) custom-call(f32[1024,128]{1,0:T(8,128)S(1)} %bitcast.12, f32[4,32,128]{2,1,0:T(8,128)S(1)} %pad_maximum_fusion.coef_ref), custom_call_target="tpu_custom_call" | custom-call | flops 3449999872 | tf_op jit(solution)/shard_map/inner/pallas_call | solution.py:255
  3.3 3.1 %collective-permute-start.5 = (f32[24,32,128]{2,1,0:T(8,128)S(1)}, f32[24,32,128]{2,1,0:T(8,128)S(1)}, u32[]{:S(2)}, u32[]{:S(2)}) collective-permute-start(f32[24,32,128]{2,1,0:T(8,128)S(1)} %get-tuple-element.16.inner_ref.refs_0_), channel_id=1, source_target_pairs={{0,8},{8,16},{16,24},{24,0},{1,9},{9,17},{17,25},{25,1},{2,10},{10... | collective-permute-start | bytes 1179656 | tf_op jit(solution)/shard_map/ppermute | solution.py:234
  6.3 0.0 collective-permute-start
  6.3 2.6 %collective-permute-start.1 = (f32[4,40,128]{2,1,0:T(8,128)S(1)}, f32[4,40,128]{2,1,0:T(8,128)S(1)}, u32[]{:S(2)}, u32[]{:S(2)}) collective-permute-start(f32[4,40,128]{2,1,0:T(8,128)S(1)} %get-tuple-element.13.top_ref), channel_id=1, source_target_pairs={{0,7},{1,0},{2,1},{3,2},{4,3},{5,4},{6,5},{7,6},{8,15},{9,8},{10,9... | collective-permute-start | bytes 245768 | tf_op jit(solution)/shard_map/ppermute | solution.py:234
  9.0 2.1 %collective-permute-done.up_ref = f32[4,40,128]{2,1,0:T(8,128)S(1)} collective-permute-done((f32[4,40,128]{2,1,0:T(8,128)S(1)}, f32[4,40,128]{2,1,0:T(8,128)S(1)}, u32[]{:S(2)}, u32[]{:S(2)}) %collective-permute-start) | collective-permute-done | bytes 81952 | tf_op jit(solution)/shard_map/ppermute | solution.py:234
  11.1 0.6 %copy-done.4 = s32[4]{0:T(128)S(1)} copy-done((s32[4]{0:T(128)S(1)}, s32[4]{0:T(128)}, u32[]{:S(2)}) %copy-start.4) | copy-done | bytes 40
  11.8 1.5 %outer.1 = (f32[8,32,128]{2,1,0:T(8,128)S(1)}, f32[32,256]{1,0:T(8,128)S(1)}) custom-call(s32[1]{0:T(128)} %bitcast.place_ref, s32[4]{0:T(128)S(1)} %copy-done.4, s32[4,256]{1,0:T(4,128)S(1)} %copy-done.1, f32[4,40,128]{2,1,0:T(8,128)S(1)} %collective-permute-done.up_ref, f32[4,40,128]{2,1,0:T(8,128)S(1)} %get-tuple-element.13.top_ref, ...), custom_call_target="tpu_custom_call" | custom-call | flops 2300000000 | tf_op jit(solution)/shard_map/outer/pallas_call | solution.py:267
  13.3 1.6 %collective-permute-start.2 = (f32[32,256]{1,0:T(8,128)S(1)}, f32[32,256]{1,0:T(8,128)S(1)}, u32[]{:S(2)}, u32[]{:S(2)}) collective-permute-start(f32[32,256]{1,0:T(8,128)S(1)} %get-tuple-element.17.refs_0_), channel_id=1, source_target_pairs={{0,8},{8,16},{16,24},{24,0},{1,9},{9,17},{17,25},{25,1},{2,10},{10... | collective-permute-start | bytes 98312 | tf_op jit(solution)/shard_map/ppermute | solution.py:234
  14.9 1.1 %collective-permute-start.3 = (f32[32,256]{1,0:T(8,128)S(1)}, f32[32,256]{1,0:T(8,128)S(1)}, u32[]{:S(2)}, u32[]{:S(2)}) collective-permute-start(f32[32,256]{1,0:T(8,128)S(1)} %get-tuple-element.17.refs_0_), channel_id=1, source_target_pairs={{0,16},{8,24},{16,0},{24,8},{1,17},{9,25},{17,1},{25,9},{2,18},{10... | collective-permute-start | bytes 98312 | tf_op jit(solution)/shard_map/ppermute | solution.py:234
  16.0 2.9 %collective-permute-start.4 = (f32[32,256]{1,0:T(8,128)S(1)}, f32[32,256]{1,0:T(8,128)S(1)}, u32[]{:S(2)}, u32[]{:S(2)}) collective-permute-start(f32[32,256]{1,0:T(8,128)S(1)} %get-tuple-element.17.refs_0_), channel_id=1, source_target_pairs={{0,24},{8,0},{16,8},{24,16},{1,25},{9,1},{17,9},{25,17},{2,26},{10... | collective-permute-start | bytes 98312 | tf_op jit(solution)/shard_map/ppermute | solution.py:234
  18.8 0.5 collective-permute-start.9
  19.3 0.0 collective-permute-done.2.refs_1_
  19.3 1.5 %collective-permute-start.6 = (f32[8,32,128]{2,1,0:T(8,128)S(1)}, f32[8,32,128]{2,1,0:T(8,128)S(1)}, u32[]{:S(2)}, u32[]{:S(2)}) collective-permute-start(f32[8,32,128]{2,1,0:T(8,128)S(1)} %get-tuple-element.18.refs_1_), channel_id=1, source_target_pairs={{0,8},{8,16},{16,24},{24,0},{1,9},{9,17},{17,25},{25,1},{2,10},{10... | collective-permute-start | bytes 393224 | tf_op jit(solution)/shard_map/ppermute | solution.py:234
  20.9 2.3 %collective-permute-start.10 = (f32[8,32,128]{2,1,0:T(8,128)S(1)}, f32[8,32,128]{2,1,0:T(8,128)S(1)}, u32[]{:S(2)}, u32[]{:S(2)}) collective-permute-start(f32[8,32,128]{2,1,0:T(8,128)S(1)} %get-tuple-element.18.refs_1_), channel_id=1, source_target_pairs={{0,24},{8,0},{16,8},{24,16},{1,25},{9,1},{17,9},{25,17},{2,26},{10... | collective-permute-start | bytes 393224 | tf_op jit(solution)/shard_map/ppermute | solution.py:234
  23.2 0.9 %gram.1 = f32[136,128]{1,0:T(8,128)S(1)} custom-call(s32[1]{0:T(128)} %bitcast.place_ref, s32[4]{0:T(128)S(1)} %copy-done.4, f32[4,256]{1,0:T(4,128)S(1)} %copy-done.2, f32[4,256]{1,0:T(4,128)S(1)} %copy-done.3, f32[32,256]{1,0:T(8,128)S(1)} %get-tuple-element.17.refs_0_, f32[32,256]{1,0:T(8,128)S(1)} %collective-permute-done.2.refs_1_, ...), custom_call_target="tpu_custom_call" | custom-call | flops 1150000000 | tf_op jit(solution)/shard_map/gram/pallas_call | solution.py:279
  24.0 10.1 %all-gather = f32[1088,128]{1,0:T(8,128)S(1)} all-gather(f32[136,128]{1,0:T(8,128)S(1)} %gram.1), channel_id=2, replica_groups=mesh['ens'=4,'dom'=8] {'dom'}, dimensions={0}, use_global_device_ids=true | all-gather | bytes 626688 | tf_op jit(solution)/shard_map/all_gather | solution.py:288
  34.2 0.5 collective-permute-start.8
  34.6 7.6 %chain.1.mix_ref = f32[32,128]{1,0:T(8,128)S(1)} custom-call(s32[4]{0:T(128)S(1)} %copy-done.4, f32[8,136,128]{2,1,0:T(8,128)S(1)} %bitcast.11), custom_call_target="tpu_custom_call" | custom-call | flops 2300000000 | tf_op jit(solution)/shard_map/chain/pallas_call | solution.py:300
  42.2 0.0 collective-permute-done.10.refs_7_
  42.2 4.7 %collective-permute-done.8.refs_5_ = f32[8,32,128]{2,1,0:T(8,128)S(1)} collective-permute-done((f32[8,32,128]{2,1,0:T(8,128)S(1)}, f32[8,32,128]{2,1,0:T(8,128)S(1)}, u32[]{:S(2)}, u32[]{:S(2)}) %collective-permute-start.8) | collective-permute-done | bytes 131104 | tf_op jit(solution)/shard_map/ppermute | solution.py:234
  46.9 1.5 %apply.1 = f32[1024,128]{1,0:T(8,128)} custom-call(f32[32,128]{1,0:T(8,128)S(1)} %chain.1.mix_ref, f32[24,32,128]{2,1,0:T(8,128)S(1)} %get-tuple-element.16.inner_ref.refs_0_, f32[8,32,128]{2,1,0:T(8,128)S(1)} %get-tuple-element.18.refs_1_, f32[24,32,128]{2,1,0:T(8,128)S(1)} %collective-permute-done.5.refs_2_, ...), custom_call_target="tpu_custom_call" | custom-call | flops 2300000000 | tf_op jit(solution)/shard_map/apply/pallas_call | solution.py:309
  (18 shorter events, 0.0 us)
Async XLA Ops:
  0.0 0.8 %copy-start.5 = (f32[32,128]{1,0:T(8,128)S(1)}, f32[32,128]{1,0:T(8,128)}, u32[]{:S(2)}) copy-start(f32[32,128]{1,0:T(8,128)} %param.11) | copy-start | bytes 49156
  0.8 1.0 %copy-start = (f32[32,32,128]{2,1,0:T(8,128)S(1)}, f32[32,32,128]{2,1,0:T(8,128)}, u32[]{:S(2)}) copy-start(f32[32,32,128]{2,1,0:T(8,128)} %param.8) | copy-start | bytes 1572868
  3.3 19.9 %collective-permute-start.5 = (f32[24,32,128]{2,1,0:T(8,128)S(1)}, f32[24,32,128]{2,1,0:T(8,128)S(1)}, u32[]{:S(2)}, u32[]{:S(2)}) collective-permute-start(f32[24,32,128]{2,1,0:T(8,128)S(1)} %get-tuple-element.16.inner_ref.refs_0_), channel_id=1, source_target_pairs={{0,8},{8,16},{16,24},{24,0},{1,9},{9,17},{17,25},{25,1},{2,10},{10... | collective-permute-start | bytes 1179656 | tf_op jit(solution)/shard_map/ppermute | solution.py:234
  6.3 4.8 %collective-permute-start = (f32[4,40,128]{2,1,0:T(8,128)S(1)}, f32[4,40,128]{2,1,0:T(8,128)S(1)}, u32[]{:S(2)}, u32[]{:S(2)}) collective-permute-start(f32[4,40,128]{2,1,0:T(8,128)S(1)} %get-tuple-element.12.bottom_ref), channel_id=1, source_target_pairs={{0,1},{1,2},{2,3},{3,4},{4,5},{5,6},{6,7},{7,0},{8,9},{9,10},{10,1... | collective-permute-start | bytes 245768 | tf_op jit(solution)/shard_map/ppermute | solution.py:234
  6.3 4.8 %collective-permute-start.1 = (f32[4,40,128]{2,1,0:T(8,128)S(1)}, f32[4,40,128]{2,1,0:T(8,128)S(1)}, u32[]{:S(2)}, u32[]{:S(2)}) collective-permute-start(f32[4,40,128]{2,1,0:T(8,128)S(1)} %get-tuple-element.13.top_ref), channel_id=1, source_target_pairs={{0,7},{1,0},{2,1},{3,2},{4,3},{5,4},{6,5},{7,6},{8,15},{9,8},{10,9... | collective-permute-start | bytes 245768 | tf_op jit(solution)/shard_map/ppermute | solution.py:234
  9.0 2.1 %copy-start.1 = (s32[4,256]{1,0:T(4,128)S(1)}, s32[4,256]{1,0:T(4,128)}, u32[]{:S(2)}) copy-start(s32[4,256]{1,0:T(4,128)} %offsets_ref.1) | copy-start | bytes 12292
  11.1 0.7 %copy-start.4 = (s32[4]{0:T(128)S(1)}, s32[4]{0:T(128)}, u32[]{:S(2)}) copy-start(s32[4]{0:T(128)} %owners_ref.5) | copy-start | bytes 52
  11.8 11.4 %copy-start.2 = (f32[4,256]{1,0:T(4,128)S(1)}, f32[4,256]{1,0:T(4,128)}, u32[]{:S(2)}) copy-start(f32[4,256]{1,0:T(4,128)} %obs_ref.1) | copy-start | bytes 12292
  11.8 11.4 %copy-start.3 = (f32[4,256]{1,0:T(4,128)S(1)}, f32[4,256]{1,0:T(4,128)}, u32[]{:S(2)}) copy-start(f32[4,256]{1,0:T(4,128)} %var_ref.1) | copy-start | bytes 12292
  13.3 6.0 %collective-permute-start.2 = (f32[32,256]{1,0:T(8,128)S(1)}, f32[32,256]{1,0:T(8,128)S(1)}, u32[]{:S(2)}, u32[]{:S(2)}) collective-permute-start(f32[32,256]{1,0:T(8,128)S(1)} %get-tuple-element.17.refs_0_), channel_id=1, source_target_pairs={{0,8},{8,16},{16,24},{24,0},{1,9},{9,17},{17,25},{25,1},{2,10},{10... | collective-permute-start | bytes 98312 | tf_op jit(solution)/shard_map/ppermute | solution.py:234
  14.9 6.0 %collective-permute-start.3 = (f32[32,256]{1,0:T(8,128)S(1)}, f32[32,256]{1,0:T(8,128)S(1)}, u32[]{:S(2)}, u32[]{:S(2)}) collective-permute-start(f32[32,256]{1,0:T(8,128)S(1)} %get-tuple-element.17.refs_0_), channel_id=1, source_target_pairs={{0,16},{8,24},{16,0},{24,8},{1,17},{9,25},{17,1},{25,9},{2,18},{10... | collective-permute-start | bytes 98312 | tf_op jit(solution)/shard_map/ppermute | solution.py:234
  16.0 7.2 %collective-permute-start.4 = (f32[32,256]{1,0:T(8,128)S(1)}, f32[32,256]{1,0:T(8,128)S(1)}, u32[]{:S(2)}, u32[]{:S(2)}) collective-permute-start(f32[32,256]{1,0:T(8,128)S(1)} %get-tuple-element.17.refs_0_), channel_id=1, source_target_pairs={{0,24},{8,0},{16,8},{24,16},{1,25},{9,1},{17,9},{25,17},{2,26},{10... | collective-permute-start | bytes 98312 | tf_op jit(solution)/shard_map/ppermute | solution.py:234
  18.8 28.1 %collective-permute-start.9 = (f32[24,32,128]{2,1,0:T(8,128)S(1)}, f32[24,32,128]{2,1,0:T(8,128)S(1)}, u32[]{:S(2)}, u32[]{:S(2)}) collective-permute-start(f32[24,32,128]{2,1,0:T(8,128)S(1)} %get-tuple-element.16.inner_ref.refs_0_), channel_id=1, source_target_pairs={{0,24},{8,0},{16,8},{24,16},{1,25},{9,1},{17,9},{25,17},{2,26},{10... | collective-permute-start | bytes 1179656 | tf_op jit(solution)/shard_map/ppermute | solution.py:234
  19.3 14.9 %collective-permute-start.6 = (f32[8,32,128]{2,1,0:T(8,128)S(1)}, f32[8,32,128]{2,1,0:T(8,128)S(1)}, u32[]{:S(2)}, u32[]{:S(2)}) collective-permute-start(f32[8,32,128]{2,1,0:T(8,128)S(1)} %get-tuple-element.18.refs_1_), channel_id=1, source_target_pairs={{0,8},{8,16},{16,24},{24,0},{1,9},{9,17},{17,25},{25,1},{2,10},{10... | collective-permute-start | bytes 393224 | tf_op jit(solution)/shard_map/ppermute | solution.py:234
  20.9 21.4 %collective-permute-start.10 = (f32[8,32,128]{2,1,0:T(8,128)S(1)}, f32[8,32,128]{2,1,0:T(8,128)S(1)}, u32[]{:S(2)}, u32[]{:S(2)}) collective-permute-start(f32[8,32,128]{2,1,0:T(8,128)S(1)} %get-tuple-element.18.refs_1_), channel_id=1, source_target_pairs={{0,24},{8,0},{16,8},{24,16},{1,25},{9,1},{17,9},{25,17},{2,26},{10... | collective-permute-start | bytes 393224 | tf_op jit(solution)/shard_map/ppermute | solution.py:234
  23.1 23.8 %collective-permute-start.7 = (f32[24,32,128]{2,1,0:T(8,128)S(1)}, f32[24,32,128]{2,1,0:T(8,128)S(1)}, u32[]{:S(2)}, u32[]{:S(2)}) collective-permute-start(f32[24,32,128]{2,1,0:T(8,128)S(1)} %collective-permute-done.5.refs_2_), channel_id=1, source_target_pairs={{0,8},{8,16},{16,24},{24,0},{1,9},{9,17},{17,25},{25,1},{2,10},{10... | collective-permute-start | bytes 1179656 | tf_op jit(solution)/shard_map/ppermute | solution.py:234
  34.2 12.7 %collective-permute-start.8 = (f32[8,32,128]{2,1,0:T(8,128)S(1)}, f32[8,32,128]{2,1,0:T(8,128)S(1)}, u32[]{:S(2)}, u32[]{:S(2)}) collective-permute-start(f32[8,32,128]{2,1,0:T(8,128)S(1)} %collective-permute-done.6.refs_3_), channel_id=1, source_target_pairs={{0,8},{8,16},{16,24},{24,0},{1,9},{9,17},{17,25},{25,1},{2,10},{10... | collective-permute-start | bytes 393224 | tf_op jit(solution)/shard_map/ppermute | solution.py:234

commit v4 on v3

--- a/solution.py
+++ b/solution.py
@@ -11,12 +11,14 @@
 TOLERANCE = 1e-6
 WIDE_BOUND = 16.0
 CHAIN_US = 2
+EARLY_US = 0.1
 HIGHEST = lax.Precision.HIGHEST
 NN = (((1,), (0,)), ((), ()))
 NT = (((1,), (1,)), ((), ()))
 
 VMEM = pl.BlockSpec(memory_space=pltpu.VMEM)
 SMEM = pl.BlockSpec(memory_space=pltpu.SMEM)
+ANY = pl.BlockSpec(memory_space=pl.ANY)
 PARAMS = pltpu.CompilerParams(vmem_limit_bytes=40 * 1024 * 1024)
 
 
@@ -29,6 +31,13 @@
 
 def estimate(micros):
     return pl.CostEstimate(flops=int(1.15e9 * micros), bytes_accessed=0, transcendentals=0)
+
+
+def rows_kernel(place_ref, owners_ref, offsets_ref, obs_ref, var_ref, cells_ref, own_ref):
+    batch = pl.ds(own_batch(place_ref, owners_ref), 1)
+    cells_ref[...] = jnp.broadcast_to(offsets_ref[batch, :], cells_ref.shape)
+    own_ref[:8] = jnp.broadcast_to(obs_ref[batch, :], cells_ref.shape)
+    own_ref[8:] = jnp.broadcast_to(var_ref[batch, :], cells_ref.shape)
 
 
 def advance(load, coef, store, count, scratches):
@@ -51,25 +60,31 @@
 
 
 def inner_kernel(
-    state_ref, coef_ref, top_ref, upper_ref, lower_ref, bottom_ref, inner_ref, a_ref, b_ref
+    state_ref, row_ref, col_ref, diff_ref, top_ref, upper_ref, lower_ref, bottom_ref, inner_ref,
+    coef_ref, a_ref, b_ref,
 ):
     width = FSTEPS
-    count, rows, cols = coef_ref.shape
-    mem = state_ref.shape[0] // rows
+    rows, mem, cols = a_ref.shape
+    count = coef_ref.shape[0]
+    row_c, col_c, diff_c = row_ref[...], col_ref[...], diff_ref[...]
+    coef_ref[0] = 1.0 - row_c - col_c - 4.0 * diff_c
+    coef_ref[1] = row_c + diff_c
+    coef_ref[2] = col_c + diff_c
+    coef_ref[3] = diff_c
 
     def load(r):
         return state_ref[pl.ds(r, mem, stride=rows), :]
+
+    def coef(r):
+        return [coef_ref[i, r:r + 1, :] for i in range(count)]
 
     blocks = (top_ref, 0), (upper_ref, width), (lower_ref, rows - 2 * width), (bottom_ref, rows - width)
     for ref, base in blocks:
         for r in range(width):
             ref[r, :mem, :] = load(base + r)
-            for i in range(count):
-                ref[r, mem + i:mem + i + 1, :] = coef_ref[i, base + r:base + r + 1, :]
+            for i, row in enumerate(coef(base + r)):
+                ref[r, mem + i:mem + i + 1, :] = row
             ref[r, mem + count:, :] = jnp.zeros((ref.shape[1] - mem - count, cols), jnp.float32)
-
-    def coef(r):
-        return [coef_ref[i, r:r + 1, :] for i in range(count)]
 
     def store(r, value):
         inner_ref[r - width] = value
@@ -85,7 +100,7 @@
 
 
 def outer_kernel(
-    place_ref, owners_ref, offsets_ref, up_ref, top_ref, upper_ref, lower_ref, bottom_ref, down_ref,
+    cells_ref, up_ref, top_ref, upper_ref, lower_ref, bottom_ref, down_ref,
     inner_ref, outer_ref, seen_ref, a_ref, b_ref,
 ):
     width = FSTEPS
@@ -111,7 +126,7 @@
             return inner_ref[r - width]
         return outer_ref[r if r < width else r - inner]
 
-    cells = offsets_ref[pl.ds(own_batch(place_ref, owners_ref), 1), :]
+    cells = cells_ref[:1, :]
     index = lax.broadcasted_iota(jnp.int32, (2 * cols, observed), 0)
     total = jnp.zeros((3 * mem, observed), jnp.float32)
     for r in range(0, rows, 2):
@@ -121,15 +136,14 @@
     seen_ref[...] = total[:mem] + total[mem:2 * mem] + total[2 * mem:]
 
 
-def gram_kernel(place_ref, owners_ref, obs_ref, var_ref, *refs):
+def gram_kernel(own_ref, *refs):
     seen_refs, out_ref = refs[:-1], refs[-1]
-    batch = own_batch(place_ref, owners_ref)
     seen = jnp.concatenate([ref[...] for ref in seen_refs], axis=0)
     members, count = seen.shape
     ybar = jnp.mean(seen, axis=0, keepdims=True)
     anom = seen - ybar
-    weight = 1.0 / (var_ref[pl.ds(batch, 1), :] * (members - 1.0))
-    gap = obs_ref[pl.ds(batch, 1), :] - ybar
+    weight = 1.0 / (own_ref[8:9, :] * (members - 1.0))
+    gap = own_ref[:1, :] - ybar
     left = jnp.concatenate([anom * weight, jnp.broadcast_to(gap * weight, (8, count))], axis=0)
     out_ref[...] = lax.dot_general(
         left, anom, NT, precision=HIGHEST, preferred_element_type=jnp.float32
@@ -152,8 +166,9 @@
     return dot(a_high, b_high) + (dot(a_high, b_low) + dot(a_low, b_high))
 
 
-def chain_kernel(owners_ref, gram_ref, out_ref):
-    mem, members = out_ref.shape
+def chain_kernel(soon, late, owners_ref, gram_ref, soon_ref, late_ref):
+    mem = soon_ref.shape[0]
+    members = gram_ref.shape[2]
     batches = owners_ref.shape[0]
     eye = (
         lax.broadcasted_iota(jnp.int32, (members, members), 0)
@@ -198,7 +213,10 @@
             mean_row = mean_row + (move if b == 0 else mul(move, forward))
             trans = 0.5 * (trans + power[:members])
             forward = trans.T
-        out_ref[...] = forward[:mem] + mean_row[:1]
+        mix = forward[:mem] + mean_row[:1]
+        for ref, slots in ((soon_ref, soon), (late_ref, late)):
+            parts = [mix[:, j * mem:(j + 1) * mem] for j in slots]
+            ref[...] = jnp.concatenate(parts, axis=1)
 
     worst = jnp.float32(0.0)
     for b in range(batches):
@@ -208,25 +226,50 @@
     pl.when(jnp.logical_not(worst > WIDE_BOUND))(lambda: chain(False))
 
 
-def apply_kernel(mix_ref, *refs):
-    field_refs, out_ref = refs[:-1], refs[-1]
-    inner_refs, outer_refs = field_refs[::2], field_refs[1::2]
-    inner, mem, cols = inner_refs[0].shape
-    outer = outer_refs[0].shape[0]
-    rows, width = inner + outer, outer // 2
-    mix_high, mix_low = split(mix_ref[...])
+def row_of(pair, r):
+    inner_ref, outer_ref = pair
+    inner, width = inner_ref.shape[0], outer_ref.shape[0] // 2
+    if width <= r < inner + width:
+        return inner_ref[r - width]
+    return outer_ref[r if r < width else r - inner]
+
+
+def share(mix, pairs, r):
+    high, low = split(mix)
+    x = jnp.concatenate(
+        [jnp.concatenate([row_of(pair, r + i) for pair in pairs], axis=0) for i in range(2)], axis=1
+    )
+    x_high, x_low = split(x)
     dot = functools.partial(jnp.dot, preferred_element_type=jnp.float32)
-
-    def part(r):
-        if width <= r < rows - width:
-            return jnp.concatenate([ref[r - width] for ref in inner_refs], axis=0)
-        return jnp.concatenate([ref[r if r < width else r - inner] for ref in outer_refs], axis=0)
-
+    return dot(high, x_high) + (dot(high, x_low) + dot(low, x_high))
+
+
+def early_kernel(mix_ref, *refs):
+    field_refs, sum_ref = refs[:-1], refs[-1]
+    pairs = list(zip(field_refs[::2], field_refs[1::2]))
+    for r in range(0, 2 * sum_ref.shape[0], 2):
+        sum_ref[r // 2] = share(mix_ref[...], pairs, r)
+
+
+def late_kernel(mix_ref, sum_ref, *refs):
+    field_refs, out_ref, stage_ref, sems = refs[:-3], refs[-3], refs[-2], refs[-1]
+    pairs = list(zip(field_refs[::2], field_refs[1::2]))
+    rows, cols = stage_ref.shape[1:]
+    chunk = rows // sems.shape[0]
+    copies = []
     for r in range(0, rows, 2):
-        high, low = split(jnp.concatenate([part(r), part(r + 1)], axis=1))
-        fresh = dot(mix_high, high) + (dot(mix_high, low) + dot(mix_low, high))
+        fresh = sum_ref[r // 2] + share(mix_ref[...], pairs, r)
         for i in range(2):
-            out_ref[pl.ds(r + i, mem, stride=rows), :] = fresh[:, i * cols:(i + 1) * cols]
+            stage_ref[:, r + i, :] = fresh[:, i * cols:(i + 1) * cols]
+        if (r + 2) % chunk == 0:
+            block = pl.ds(r + 2 - chunk, chunk)
+            copy = pltpu.make_async_copy(
+                stage_ref.at[:, block, :], out_ref.at[:, block, :], sems.at[len(copies)]
+            )
+            copy.start()
+            copies.append(copy)
+    for copy in copies:
+        copy.wait()
 
 
 def shift(x, axis, step):
@@ -245,46 +288,50 @@
     f32 = functools.partial(jax.ShapeDtypeStruct, dtype=jnp.float32)
     scratch = functools.partial(pltpu.VMEM, dtype=jnp.float32)
     place = lax.axis_index("dom").astype(jnp.int32).reshape(1)
-    mixers = jnp.stack([
-        1.0 - row_courant - col_courant - 4.0 * diffusion,
-        row_courant + diffusion,
-        col_courant + diffusion,
-        diffusion,
-    ])
+    staged = jnp.pad(state, ((0, 1), (0, 0), (0, 0))).reshape(-1, cols)
     edge = f32((width, mem + 8, cols))
+    cells, own = pl.pallas_call(
+        rows_kernel,
+        out_shape=(jax.ShapeDtypeStruct((8, observed), jnp.int32), f32((16, observed))),
+        in_specs=[SMEM] * 2 + [VMEM] * 3,
+        out_specs=(VMEM, VMEM),
+        compiler_params=PARAMS,
+        cost_estimate=estimate(1),
+        name="rows",
+    )(place, owners, obs_offsets, obs_values, obs_variance)
     top, upper, lower, bottom, inner = pl.pallas_call(
         inner_kernel,
         out_shape=(edge,) * 4 + (f32((rows - 2 * width, mem, cols)),),
-        in_specs=[VMEM] * 2,
+        in_specs=[VMEM] * 4,
         out_specs=(VMEM,) * 5,
-        scratch_shapes=[scratch((rows, mem, cols))] * 2,
+        scratch_shapes=[scratch((4, rows, cols))] + [scratch((rows, mem, cols))] * 2,
         compiler_params=PARAMS,
         cost_estimate=estimate(3),
         name="inner",
-    )(state.reshape(mem * rows, cols), mixers)
+    )(staged, row_courant, col_courant, diffusion)
     up = shift(bottom, "dom", 1)
     down = shift(top, "dom", -1)
     outer, seen = pl.pallas_call(
         outer_kernel,
         out_shape=(f32((2 * width, mem, cols)), f32((mem, observed))),
-        in_specs=[SMEM] * 2 + [VMEM] * 8,
+        in_specs=[VMEM] * 8,
         out_specs=(VMEM, VMEM),
         scratch_shapes=[scratch((3 * width, mem, cols))] * 2,
         compiler_params=PARAMS,
         cost_estimate=estimate(2),
         name="outer",
-    )(place, owners, obs_offsets, up, top, upper, lower, bottom, down, inner)
+    )(cells, up, top, upper, lower, bottom, down, inner)
 
     seens = [seen] + [shift(seen, "ens", k) for k in range(1, ens)]
     gram = pl.pallas_call(
         gram_kernel,
         out_shape=f32((members + 8, members)),
-        in_specs=[SMEM] * 2 + [VMEM] * (2 + ens),
+        in_specs=[VMEM] * (1 + ens),
         out_specs=VMEM,
         compiler_params=PARAMS,
         cost_estimate=estimate(1),
         name="gram",
-    )(place, owners, obs_values, obs_variance, *seens)
+    )(own, *seens)
     grams = lax.all_gather(gram, "dom")
 
     def around(part):
@@ -295,27 +342,38 @@
             slots[ens - j] = shift(slots[(ens - j + 1) % ens], "ens", -1)
         return slots
 
-    fields = [x for pair in zip(around(inner), around(outer)) for x in pair]
-
-    mix = pl.pallas_call(
-        chain_kernel,
-        out_shape=f32((mem, members)),
+    slots = list(zip(around(inner), around(outer)))
+    late = list(range(2, ens - 1))
+    soon = [j for j in range(ens) if j not in late]
+
+    mix_soon, mix_late = pl.pallas_call(
+        functools.partial(chain_kernel, soon, late),
+        out_shape=(f32((mem, mem * len(soon))), f32((mem, mem * len(late)))),
         in_specs=[SMEM, VMEM],
-        out_specs=VMEM,
+        out_specs=(VMEM, VMEM),
         compiler_params=PARAMS,
         cost_estimate=estimate(CHAIN_US),
         name="chain",
     )(owners, grams)
-    out = pl.pallas_call(
-        apply_kernel,
-        out_shape=f32((mem * rows, cols)),
-        in_specs=[VMEM] * (1 + 2 * ens),
+    sums = pl.pallas_call(
+        early_kernel,
+        out_shape=f32((rows // 2, mem, 2 * cols)),
+        in_specs=[VMEM] * (1 + 2 * len(soon)),
         out_specs=VMEM,
         compiler_params=PARAMS,
-        cost_estimate=estimate(2),
-        name="apply",
-    )(mix, *fields)
-    return out.reshape(mem, rows, cols)
+        cost_estimate=estimate(EARLY_US),
+        name="early",
+    )(mix_soon, *[x for j in soon for x in slots[j]])
+    return pl.pallas_call(
+        late_kernel,
+        out_shape=f32((mem, rows, cols)),
+        in_specs=[VMEM] * (2 + 2 * len(late)),
+        out_specs=ANY,
+        scratch_shapes=[scratch((mem, rows, cols)), pltpu.SemaphoreType.DMA((rows // 8,))],
+        compiler_params=PARAMS,
+        cost_estimate=estimate(1),
+        name="late",
+    )(mix_late, sums, *[x for j in late for x in slots[j]])
 
 
 def solution(mesh):

time: 48.7 us -> 46.4 us (0.953)
  waiting for transfers between devices: 6.87 us -> 5.4 us
  other arithmetic: 0.8 us -> 0 us
    ppermute x11, waiting for transfers between devices: 6.87 us -> 5.4 us  [shift(): lax.ppermute(x, axis, [(i, (i + step) % count) for i in range(count)])]
    pad x0 -> x1, local copies, waits for them, and re-layouts: none -> 1.1 us  [on_device(): staged = jnp.pad(state, ((0, 1), (0, 0), (0, 0))).reshape(-1, cols)]
    unnamed x12 -> x14, local copies, waits for them, and re-layouts: 1.7 us -> 0.67 us
    another operation x2 -> x0, other arithmetic: 0.8 us -> none  [on_device(): jnp.stack([1.0 - row_courant - col_courant - 4.0 * diffusion, row_courant...]
    pallas_call x2 -> x4, Pallas kernels: 9.1 us -> 9.83 us  [the longest x1 7.67 us: on_device(): pl.pallas_call(functools.partial(chain_kernel, soon, late), out_shape=(f3...]
    pallas_call x1, Pallas kernels: 1.53 us -> 0.98 us  [on_device(): pl.pallas_call(outer_kernel, out_shape=(f32((2 * width, mem, cols)), f32(...]
    pallas_call x1, Pallas kernels: 0.85 us -> 0.31 us  [on_device(): pl.pallas_call(gram_kernel, out_shape=f32((members + 8, members)), in_spe...]
  transfers between devices with their start and end apart: 11 -> 11, of which waited for: 2 -> 2; matrix products, arithmetic and copies ran while one was open for 0% -> 0% of each run, Pallas kernels for 21% -> 22%
where the time goes in v4:
time: 46.4 us; the launch traced here: 46.2 us
  starting transfers between devices  16.2 us (35%)
  Pallas kernels  12.6 us (27%)
  blocking collectives  10.2 us (22%)
  waiting for transfers between devices  5.4 us (12%)
  local copies, waits for them, and re-layouts  1.77 us (4%)
    ppermute x11, starting transfers between devices, shift(): lax.ppermute(x, axis, [(i, (i + step) % count) for i in range(count)])  16.2 us
    all_gather x1, blocking collectives, on_device(): grams = lax.all_gather(gram, 'dom')  10.2 us
    pallas_call x1, Pallas kernels, on_device(): pl.pallas_call(functools.partial(chain_kernel, soon, late), out_shape=(f3...  7.67 us
    ppermute x11, waiting for transfers between devices, shift(): lax.ppermute(x, axis, [(i, (i + step) % count) for i in range(count)])  5.4 us
    pallas_call x1, Pallas kernels, on_device(): pl.pallas_call(inner_kernel, out_shape=(edge,) * 4 + (f32((rows - 2 * wid...  1.43 us
    pallas_call x1, Pallas kernels, on_device(): pl.pallas_call(late_kernel, out_shape=f32((mem, rows, cols)), in_specs=[V...  1.17 us
    pad x1, local copies, waits for them, and re-layouts, on_device(): staged = jnp.pad(state, ((0, 1), (0, 0), (0, 0))).reshape(-1, cols)  1.1 us
    pallas_call x1, Pallas kernels, on_device(): pl.pallas_call(outer_kernel, out_shape=(f32((2 * width, mem, cols)), f32(...  0.98 us
  transfers between devices with their start and end apart: 11, of which 2 were waited for; matrix products, arithmetic and copies ran while one was open for 0% of the time, Pallas kernels for 22%

profile of v4, /device:TPU:0, one launch (start us, length us, event | category | flops | bytes accessed | tf_op | source)
XLA Modules:
  0.0 46.2 jit_solution(11079314488347758166)
XLA Ops:
  0.0 1.1 %pad.4 = f32[33,32,128]{2,1,0:T(8,128)S(1)} pad(f32[32,32,128]{2,1,0:T(8,128)} %param.8, f32[]{:T(128)} %constant.6.clone.1), padding=0_1x0_0x0_0 | pad | bytes 1064964 | tf_op jit(solution)/shard_map/jit(_pad)/pad | solution.py:291
  1.1 0.0 copy-start.5
  1.2 1.4 %inner.1 = (f32[4,40,128]{2,1,0:T(8,128)S(1)}, f32[4,40,128]{2,1,0:T(8,128)S(1)}, f32[4,40,128]{2,1,0:T(8,128)S(1)}, f32[4,40,128]{2,1,0:T(8,128)S(1)}, f32[24,32,128]{2,1,0:T(8,128)S(1)}) custom-call(f32[1056,128]{1,0:T(8,128)S(1)} %bitcast.4, f32[32,128]{1,0:T(8,128)S(1)} %copy-done, f32[32,128]{1,0:T(8,128)S(1)} %copy-done.1, f32[32,128]{1,0:T(8,128)S(1)} %copy-done.2), custom_call_target="tpu_custom_call" | custom-call | flops 3449999872 | tf_op jit(solution)/shard_map/inner/pallas_call | solution.py:302
  2.6 3.1 %collective-permute-start.5 = (f32[24,32,128]{2,1,0:T(8,128)S(1)}, f32[24,32,128]{2,1,0:T(8,128)S(1)}, u32[]{:S(2)}, u32[]{:S(2)}) collective-permute-start(f32[24,32,128]{2,1,0:T(8,128)S(1)} %get-tuple-element.22.inner_ref.refs_0_), channel_id=1, source_target_pairs={{0,8},{8,16},{16,24},{24,0},{1,9},{9,17},{17,25},{25,1},{2,10},{10... | collective-permute-start | bytes 1179656 | tf_op jit(solution)/shard_map/ppermute | solution.py:277
  5.7 0.0 collective-permute-start
  5.7 2.6 %collective-permute-start.1 = (f32[4,40,128]{2,1,0:T(8,128)S(1)}, f32[4,40,128]{2,1,0:T(8,128)S(1)}, u32[]{:S(2)}, u32[]{:S(2)}) collective-permute-start(f32[4,40,128]{2,1,0:T(8,128)S(1)} %get-tuple-element.19.top_ref), channel_id=1, source_target_pairs={{0,7},{1,0},{2,1},{3,2},{4,3},{5,4},{6,5},{7,6},{8,15},{9,8},{10,9... | collective-permute-start | bytes 245768 | tf_op jit(solution)/shard_map/ppermute | solution.py:277
  8.3 0.6 %copy-done.6 = s32[4]{0:T(128)S(1)} copy-done((s32[4]{0:T(128)S(1)}, s32[4]{0:T(128)}, u32[]{:S(2)}) %copy-start.6) | copy-done | bytes 40
  9.0 0.5 %rows.1 = (s32[8,256]{1,0:T(8,128)S(1)}, f32[16,256]{1,0:T(8,128)S(1)}) custom-call(s32[1]{0:T(128)} %bitcast.place_ref, s32[4]{0:T(128)S(1)} %copy-done.6, s32[4,256]{1,0:T(4,128)S(1)} %copy-done.3, f32[4,256]{1,0:T(4,128)S(1)} %copy-done.4, f32[4,256]{1,0:T(4,128)S(1)} %copy-done.5), custom_call_target="tpu_custom_call" | custom-call | flops 1150000000 | tf_op jit(solution)/shard_map/rows/pallas_call | solution.py:293
  9.5 0.9 %collective-permute-done.up_ref = f32[4,40,128]{2,1,0:T(8,128)S(1)} collective-permute-done((f32[4,40,128]{2,1,0:T(8,128)S(1)}, f32[4,40,128]{2,1,0:T(8,128)S(1)}, u32[]{:S(2)}, u32[]{:S(2)}) %collective-permute-start) | collective-permute-done | bytes 81952 | tf_op jit(solution)/shard_map/ppermute | solution.py:277
  10.4 0.0 collective-permute-done.1.down_ref
  10.5 1.0 %outer.1 = (f32[8,32,128]{2,1,0:T(8,128)S(1)}, f32[32,256]{1,0:T(8,128)S(1)}) custom-call(s32[8,256]{1,0:T(8,128)S(1)} %get-tuple-element.17.cells_ref, f32[4,40,128]{2,1,0:T(8,128)S(1)} %collective-permute-done.up_ref, f32[4,40,128]{2,1,0:T(8,128)S(1)} %get-tuple-element.19.top_ref, f32[4,40,128]{2,1,0:T(8,128)S(1)} %get-tuple-element.20.upper_ref, ...), custom_call_target="tpu_custom_call" | custom-call | flops 2300000000 | tf_op jit(solution)/shard_map/outer/pallas_call | solution.py:314
  11.4 1.6 %collective-permute-start.2 = (f32[32,256]{1,0:T(8,128)S(1)}, f32[32,256]{1,0:T(8,128)S(1)}, u32[]{:S(2)}, u32[]{:S(2)}) collective-permute-start(f32[32,256]{1,0:T(8,128)S(1)} %get-tuple-element.23.refs_0_), channel_id=1, source_target_pairs={{0,8},{8,16},{16,24},{24,0},{1,9},{9,17},{17,25},{25,1},{2,10},{10... | collective-permute-start | bytes 98312 | tf_op jit(solution)/shard_map/ppermute | solution.py:277
  13.0 1.1 %collective-permute-start.3 = (f32[32,256]{1,0:T(8,128)S(1)}, f32[32,256]{1,0:T(8,128)S(1)}, u32[]{:S(2)}, u32[]{:S(2)}) collective-permute-start(f32[32,256]{1,0:T(8,128)S(1)} %get-tuple-element.23.refs_0_), channel_id=1, source_target_pairs={{0,16},{8,24},{16,0},{24,8},{1,17},{9,25},{17,1},{25,9},{2,18},{10... | collective-permute-start | bytes 98312 | tf_op jit(solution)/shard_map/ppermute | solution.py:277
  14.1 2.9 %collective-permute-start.4 = (f32[32,256]{1,0:T(8,128)S(1)}, f32[32,256]{1,0:T(8,128)S(1)}, u32[]{:S(2)}, u32[]{:S(2)}) collective-permute-start(f32[32,256]{1,0:T(8,128)S(1)} %get-tuple-element.23.refs_0_), channel_id=1, source_target_pairs={{0,24},{8,0},{16,8},{24,16},{1,25},{9,1},{17,9},{25,17},{2,26},{10... | collective-permute-start | bytes 98312 | tf_op jit(solution)/shard_map/ppermute | solution.py:277
  17.0 0.4 collective-permute-start.7
  17.4 1.6 %collective-permute-start.6 = (f32[8,32,128]{2,1,0:T(8,128)S(1)}, f32[8,32,128]{2,1,0:T(8,128)S(1)}, u32[]{:S(2)}, u32[]{:S(2)}) collective-permute-start(f32[8,32,128]{2,1,0:T(8,128)S(1)} %get-tuple-element.26.refs_1_), channel_id=1, source_target_pairs={{0,8},{8,16},{16,24},{24,0},{1,9},{9,17},{17,25},{25,1},{2,10},{10... | collective-permute-start | bytes 393224 | tf_op jit(solution)/shard_map/ppermute | solution.py:277
  19.0 2.2 %collective-permute-start.8 = (f32[8,32,128]{2,1,0:T(8,128)S(1)}, f32[8,32,128]{2,1,0:T(8,128)S(1)}, u32[]{:S(2)}, u32[]{:S(2)}) collective-permute-start(f32[8,32,128]{2,1,0:T(8,128)S(1)} %get-tuple-element.26.refs_1_), channel_id=1, source_target_pairs={{0,24},{8,0},{16,8},{24,16},{1,25},{9,1},{17,9},{25,17},{2,26},{10... | collective-permute-start | bytes 393224 | tf_op jit(solution)/shard_map/ppermute | solution.py:277
  21.3 0.3 gram.1
  21.6 10.2 %all-gather = f32[1088,128]{1,0:T(8,128)S(1)} all-gather(f32[136,128]{1,0:T(8,128)S(1)} %gram.1), channel_id=2, replica_groups=mesh['ens'=4,'dom'=8] {'dom'}, dimensions={0}, use_global_device_ids=true | all-gather | bytes 626688 | tf_op jit(solution)/shard_map/all_gather | solution.py:335
  31.7 0.7 %collective-permute-start.10 = (f32[8,32,128]{2,1,0:T(8,128)S(1)}, f32[8,32,128]{2,1,0:T(8,128)S(1)}, u32[]{:S(2)}, u32[]{:S(2)}) collective-permute-start(f32[8,32,128]{2,1,0:T(8,128)S(1)} %collective-permute-done.6.refs_3_), channel_id=1, source_target_pairs={{0,8},{8,16},{16,24},{24,0},{1,9},{9,17},{17,25},{25,1},{2,10},{10... | collective-permute-start | bytes 393224 | tf_op jit(solution)/shard_map/ppermute | solution.py:277
  32.4 7.7 %chain.1 = (f32[32,96]{1,0:T(8,128)S(1)}, f32[32,32]{1,0:T(8,128)S(1)}) custom-call(s32[4]{0:T(128)S(1)} %copy-done.6, f32[8,136,128]{2,1,0:T(8,128)S(1)} %bitcast.3), custom_call_target="tpu_custom_call" | custom-call | flops 2300000000 | tf_op jit(solution)/shard_map/chain/pallas_call | solution.py:349
  40.1 0.4 early.1.sum_ref
  40.6 4.5 %collective-permute-done.10.refs_1_ = f32[8,32,128]{2,1,0:T(8,128)S(1)} collective-permute-done((f32[8,32,128]{2,1,0:T(8,128)S(1)}, f32[8,32,128]{2,1,0:T(8,128)S(1)}, u32[]{:S(2)}, u32[]{:S(2)}) %collective-permute-start.10) | collective-permute-done | bytes 131104 | tf_op jit(solution)/shard_map/ppermute | solution.py:277
  45.1 1.2 %late.1 = f32[32,32,128]{2,1,0:T(8,128)} custom-call(f32[32,32]{1,0:T(8,128)S(1)} %get-tuple-element.24.mix_ref, f32[16,32,256]{2,1,0:T(8,128)S(1)} %early.1.sum_ref, f32[24,32,128]{2,1,0:T(8,128)S(1)} %collective-permute-done.9.refs_0_, f32[8,32,128]{2,1,0:T(8,128)S(1)} %collective-permute-done.10.refs_1_), custom_call_target="tpu_custom_call" | custom-call | flops 1150000000 | tf_op jit(solution)/shard_map/late/pallas_call | solution.py:367
  (21 shorter events, 0.0 us)
Async XLA Ops:
  0.0 1.1 %copy-start = (f32[32,128]{1,0:T(8,128)S(1)}, f32[32,128]{1,0:T(8,128)}, u32[]{:S(2)}) copy-start(f32[32,128]{1,0:T(8,128)} %row_ref.1) | copy-start | bytes 49156
  0.0 1.1 %copy-start.1 = (f32[32,128]{1,0:T(8,128)S(1)}, f32[32,128]{1,0:T(8,128)}, u32[]{:S(2)}) copy-start(f32[32,128]{1,0:T(8,128)} %col_ref.1) | copy-start | bytes 49156
  0.0 1.1 %copy-start.2 = (f32[32,128]{1,0:T(8,128)S(1)}, f32[32,128]{1,0:T(8,128)}, u32[]{:S(2)}) copy-start(f32[32,128]{1,0:T(8,128)} %diff_ref.1) | copy-start | bytes 49156
  1.1 7.2 %copy-start.5 = (f32[4,256]{1,0:T(4,128)S(1)}, f32[4,256]{1,0:T(4,128)}, u32[]{:S(2)}) copy-start(f32[4,256]{1,0:T(4,128)} %var_ref.1) | copy-start | bytes 12292
  2.6 18.7 %collective-permute-start.5 = (f32[24,32,128]{2,1,0:T(8,128)S(1)}, f32[24,32,128]{2,1,0:T(8,128)S(1)}, u32[]{:S(2)}, u32[]{:S(2)}) collective-permute-start(f32[24,32,128]{2,1,0:T(8,128)S(1)} %get-tuple-element.22.inner_ref.refs_0_), channel_id=1, source_target_pairs={{0,8},{8,16},{16,24},{24,0},{1,9},{9,17},{17,25},{25,1},{2,10},{10... | collective-permute-start | bytes 1179656 | tf_op jit(solution)/shard_map/ppermute | solution.py:277
  5.7 4.8 %collective-permute-start = (f32[4,40,128]{2,1,0:T(8,128)S(1)}, f32[4,40,128]{2,1,0:T(8,128)S(1)}, u32[]{:S(2)}, u32[]{:S(2)}) collective-permute-start(f32[4,40,128]{2,1,0:T(8,128)S(1)} %get-tuple-element.18.bottom_ref), channel_id=1, source_target_pairs={{0,1},{1,2},{2,3},{3,4},{4,5},{5,6},{6,7},{7,0},{8,9},{9,10},{10,1... | collective-permute-start | bytes 245768 | tf_op jit(solution)/shard_map/ppermute | solution.py:277
  5.7 2.7 %copy-start.4 = (f32[4,256]{1,0:T(4,128)S(1)}, f32[4,256]{1,0:T(4,128)}, u32[]{:S(2)}) copy-start(f32[4,256]{1,0:T(4,128)} %obs_ref.1) | copy-start | bytes 12292
  5.7 2.7 %copy-start.3 = (s32[4,256]{1,0:T(4,128)S(1)}, s32[4,256]{1,0:T(4,128)}, u32[]{:S(2)}) copy-start(s32[4,256]{1,0:T(4,128)} %offsets_ref.1) | copy-start | bytes 12292
  5.7 4.8 %collective-permute-start.1 = (f32[4,40,128]{2,1,0:T(8,128)S(1)}, f32[4,40,128]{2,1,0:T(8,128)S(1)}, u32[]{:S(2)}, u32[]{:S(2)}) collective-permute-start(f32[4,40,128]{2,1,0:T(8,128)S(1)} %get-tuple-element.19.top_ref), channel_id=1, source_target_pairs={{0,7},{1,0},{2,1},{3,2},{4,3},{5,4},{6,5},{7,6},{8,15},{9,8},{10,9... | collective-permute-start | bytes 245768 | tf_op jit(solution)/shard_map/ppermute | solution.py:277
  8.3 0.7 %copy-start.6 = (s32[4]{0:T(128)S(1)}, s32[4]{0:T(128)}, u32[]{:S(2)}) copy-start(s32[4]{0:T(128)} %owners_ref.3) | copy-start | bytes 52
  11.4 6.0 %collective-permute-start.2 = (f32[32,256]{1,0:T(8,128)S(1)}, f32[32,256]{1,0:T(8,128)S(1)}, u32[]{:S(2)}, u32[]{:S(2)}) collective-permute-start(f32[32,256]{1,0:T(8,128)S(1)} %get-tuple-element.23.refs_0_), channel_id=1, source_target_pairs={{0,8},{8,16},{16,24},{24,0},{1,9},{9,17},{17,25},{25,1},{2,10},{10... | collective-permute-start | bytes 98312 | tf_op jit(solution)/shard_map/ppermute | solution.py:277
  13.0 6.0 %collective-permute-start.3 = (f32[32,256]{1,0:T(8,128)S(1)}, f32[32,256]{1,0:T(8,128)S(1)}, u32[]{:S(2)}, u32[]{:S(2)}) collective-permute-start(f32[32,256]{1,0:T(8,128)S(1)} %get-tuple-element.23.refs_0_), channel_id=1, source_target_pairs={{0,16},{8,24},{16,0},{24,8},{1,17},{9,25},{17,1},{25,9},{2,18},{10... | collective-permute-start | bytes 98312 | tf_op jit(solution)/shard_map/ppermute | solution.py:277
  14.1 7.1 %collective-permute-start.4 = (f32[32,256]{1,0:T(8,128)S(1)}, f32[32,256]{1,0:T(8,128)S(1)}, u32[]{:S(2)}, u32[]{:S(2)}) collective-permute-start(f32[32,256]{1,0:T(8,128)S(1)} %get-tuple-element.23.refs_0_), channel_id=1, source_target_pairs={{0,24},{8,0},{16,8},{24,16},{1,25},{9,1},{17,9},{25,17},{2,26},{10... | collective-permute-start | bytes 98312 | tf_op jit(solution)/shard_map/ppermute | solution.py:277
  17.0 23.2 %collective-permute-start.7 = (f32[24,32,128]{2,1,0:T(8,128)S(1)}, f32[24,32,128]{2,1,0:T(8,128)S(1)}, u32[]{:S(2)}, u32[]{:S(2)}) collective-permute-start(f32[24,32,128]{2,1,0:T(8,128)S(1)} %get-tuple-element.22.inner_ref.refs_0_), channel_id=1, source_target_pairs={{0,24},{8,0},{16,8},{24,16},{1,25},{9,1},{17,9},{25,17},{2,26},{10... | collective-permute-start | bytes 1179656 | tf_op jit(solution)/shard_map/ppermute | solution.py:277
  17.4 14.3 %collective-permute-start.6 = (f32[8,32,128]{2,1,0:T(8,128)S(1)}, f32[8,32,128]{2,1,0:T(8,128)S(1)}, u32[]{:S(2)}, u32[]{:S(2)}) collective-permute-start(f32[8,32,128]{2,1,0:T(8,128)S(1)} %get-tuple-element.26.refs_1_), channel_id=1, source_target_pairs={{0,8},{8,16},{16,24},{24,0},{1,9},{9,17},{17,25},{25,1},{2,10},{10... | collective-permute-start | bytes 393224 | tf_op jit(solution)/shard_map/ppermute | solution.py:277
  19.0 21.1 %collective-permute-start.8 = (f32[8,32,128]{2,1,0:T(8,128)S(1)}, f32[8,32,128]{2,1,0:T(8,128)S(1)}, u32[]{:S(2)}, u32[]{:S(2)}) collective-permute-start(f32[8,32,128]{2,1,0:T(8,128)S(1)} %get-tuple-element.26.refs_1_), channel_id=1, source_target_pairs={{0,24},{8,0},{16,8},{24,16},{1,25},{9,1},{17,9},{25,17},{2,26},{10... | collective-permute-start | bytes 393224 | tf_op jit(solution)/shard_map/ppermute | solution.py:277
  21.3 23.8 %collective-permute-start.9 = (f32[24,32,128]{2,1,0:T(8,128)S(1)}, f32[24,32,128]{2,1,0:T(8,128)S(1)}, u32[]{:S(2)}, u32[]{:S(2)}) collective-permute-start(f32[24,32,128]{2,1,0:T(8,128)S(1)} %collective-permute-done.5.refs_2_), channel_id=1, source_target_pairs={{0,8},{8,16},{16,24},{24,0},{1,9},{9,17},{17,25},{25,1},{2,10},{10... | collective-permute-start | bytes 1179656 | tf_op jit(solution)/shard_map/ppermute | solution.py:277
  31.7 13.3 %collective-permute-start.10 = (f32[8,32,128]{2,1,0:T(8,128)S(1)}, f32[8,32,128]{2,1,0:T(8,128)S(1)}, u32[]{:S(2)}, u32[]{:S(2)}) collective-permute-start(f32[8,32,128]{2,1,0:T(8,128)S(1)} %collective-permute-done.6.refs_3_), channel_id=1, source_target_pairs={{0,8},{8,16},{16,24},{24,0},{1,9},{9,17},{17,25},{25,1},{2,10},{10... | collective-permute-start | bytes 393224 | tf_op jit(solution)/shard_map/ppermute | solution.py:277

commit v5 on v4

--- a/solution.py
+++ b/solution.py
@@ -214,6 +214,7 @@
             trans = 0.5 * (trans + power[:members])
             forward = trans.T
         mix = forward[:mem] + mean_row[:1]
+        mix = mix - (jnp.sum(mix, axis=1, keepdims=True) - 1.0) / members
         for ref, slots in ((soon_ref, soon), (late_ref, late)):
             parts = [mix[:, j * mem:(j + 1) * mem] for j in slots]
             ref[...] = jnp.concatenate(parts, axis=1)

time: 46.4 us -> 46.4 us (level)
  no operation moved by 1% of the time
where the time goes in v5:
time: 46.4 us; the launch traced here: 46.2 us
  starting transfers between devices  16.2 us (35%)
  Pallas kernels  12.9 us (28%)
  blocking collectives  10.2 us (22%)
  waiting for transfers between devices  5.01 us (11%)
  local copies, waits for them, and re-layouts  1.77 us (4%)
    ppermute x11, starting transfers between devices, shift(): lax.ppermute(x, axis, [(i, (i + step) % count) for i in range(count)])  16.2 us
    all_gather x1, blocking collectives, on_device(): grams = lax.all_gather(gram, 'dom')  10.2 us
    pallas_call x1, Pallas kernels, on_device(): pl.pallas_call(functools.partial(chain_kernel, soon, late), out_shape=(f3...  8.06 us
    ppermute x11, waiting for transfers between devices, shift(): lax.ppermute(x, axis, [(i, (i + step) % count) for i in range(count)])  5.01 us
    pallas_call x1, Pallas kernels, on_device(): pl.pallas_call(inner_kernel, out_shape=(edge,) * 4 + (f32((rows - 2 * wid...  1.43 us
    pallas_call x1, Pallas kernels, on_device(): pl.pallas_call(late_kernel, out_shape=f32((mem, rows, cols)), in_specs=[V...  1.17 us
    pad x1, local copies, waits for them, and re-layouts, on_device(): staged = jnp.pad(state, ((0, 1), (0, 0), (0, 0))).reshape(-1, cols)  1.1 us
    pallas_call x1, Pallas kernels, on_device(): pl.pallas_call(outer_kernel, out_shape=(f32((2 * width, mem, cols)), f32(...  0.98 us
  transfers between devices with their start and end apart: 11, of which 2 were waited for; matrix products, arithmetic and copies ran while one was open for 0% of the time, Pallas kernels for 22%

profile of v5, /device:TPU:0, one launch (start us, length us, event | category | flops | bytes accessed | tf_op | source)
XLA Modules:
  0.0 46.2 jit_solution(10755949111859465100)
XLA Ops:
  0.0 1.1 %pad.4 = f32[33,32,128]{2,1,0:T(8,128)S(1)} pad(f32[32,32,128]{2,1,0:T(8,128)} %param.8, f32[]{:T(128)} %constant.6.clone.1), padding=0_1x0_0x0_0 | pad | bytes 1064964 | tf_op jit(solution)/shard_map/jit(_pad)/pad | solution.py:292
  1.1 0.0 copy-start.5
  1.2 1.4 %inner.1 = (f32[4,40,128]{2,1,0:T(8,128)S(1)}, f32[4,40,128]{2,1,0:T(8,128)S(1)}, f32[4,40,128]{2,1,0:T(8,128)S(1)}, f32[4,40,128]{2,1,0:T(8,128)S(1)}, f32[24,32,128]{2,1,0:T(8,128)S(1)}) custom-call(f32[1056,128]{1,0:T(8,128)S(1)} %bitcast.4, f32[32,128]{1,0:T(8,128)S(1)} %copy-done, f32[32,128]{1,0:T(8,128)S(1)} %copy-done.1, f32[32,128]{1,0:T(8,128)S(1)} %copy-done.2), custom_call_target="tpu_custom_call" | custom-call | flops 3449999872 | tf_op jit(solution)/shard_map/inner/pallas_call | solution.py:303
  2.6 3.1 %collective-permute-start.5 = (f32[24,32,128]{2,1,0:T(8,128)S(1)}, f32[24,32,128]{2,1,0:T(8,128)S(1)}, u32[]{:S(2)}, u32[]{:S(2)}) collective-permute-start(f32[24,32,128]{2,1,0:T(8,128)S(1)} %get-tuple-element.22.inner_ref.refs_0_), channel_id=1, source_target_pairs={{0,8},{8,16},{16,24},{24,0},{1,9},{9,17},{17,25},{25,1},{2,10},{10... | collective-permute-start | bytes 1179656 | tf_op jit(solution)/shard_map/ppermute | solution.py:278
  5.7 0.0 collective-permute-start
  5.7 2.6 %collective-permute-start.1 = (f32[4,40,128]{2,1,0:T(8,128)S(1)}, f32[4,40,128]{2,1,0:T(8,128)S(1)}, u32[]{:S(2)}, u32[]{:S(2)}) collective-permute-start(f32[4,40,128]{2,1,0:T(8,128)S(1)} %get-tuple-element.19.top_ref), channel_id=1, source_target_pairs={{0,7},{1,0},{2,1},{3,2},{4,3},{5,4},{6,5},{7,6},{8,15},{9,8},{10,9... | collective-permute-start | bytes 245768 | tf_op jit(solution)/shard_map/ppermute | solution.py:278
  8.3 0.6 %copy-done.6 = s32[4]{0:T(128)S(1)} copy-done((s32[4]{0:T(128)S(1)}, s32[4]{0:T(128)}, u32[]{:S(2)}) %copy-start.6) | copy-done | bytes 40
  9.0 0.5 %rows.1 = (s32[8,256]{1,0:T(8,128)S(1)}, f32[16,256]{1,0:T(8,128)S(1)}) custom-call(s32[1]{0:T(128)} %bitcast.place_ref, s32[4]{0:T(128)S(1)} %copy-done.6, s32[4,256]{1,0:T(4,128)S(1)} %copy-done.3, f32[4,256]{1,0:T(4,128)S(1)} %copy-done.4, f32[4,256]{1,0:T(4,128)S(1)} %copy-done.5), custom_call_target="tpu_custom_call" | custom-call | flops 1150000000 | tf_op jit(solution)/shard_map/rows/pallas_call | solution.py:294
  9.5 0.9 %collective-permute-done.up_ref = f32[4,40,128]{2,1,0:T(8,128)S(1)} collective-permute-done((f32[4,40,128]{2,1,0:T(8,128)S(1)}, f32[4,40,128]{2,1,0:T(8,128)S(1)}, u32[]{:S(2)}, u32[]{:S(2)}) %collective-permute-start) | collective-permute-done | bytes 81952 | tf_op jit(solution)/shard_map/ppermute | solution.py:278
  10.4 0.0 collective-permute-done.1.down_ref
  10.5 1.0 %outer.1 = (f32[8,32,128]{2,1,0:T(8,128)S(1)}, f32[32,256]{1,0:T(8,128)S(1)}) custom-call(s32[8,256]{1,0:T(8,128)S(1)} %get-tuple-element.17.cells_ref, f32[4,40,128]{2,1,0:T(8,128)S(1)} %collective-permute-done.up_ref, f32[4,40,128]{2,1,0:T(8,128)S(1)} %get-tuple-element.19.top_ref, f32[4,40,128]{2,1,0:T(8,128)S(1)} %get-tuple-element.20.upper_ref, ...), custom_call_target="tpu_custom_call" | custom-call | flops 2300000000 | tf_op jit(solution)/shard_map/outer/pallas_call | solution.py:315
  11.4 1.6 %collective-permute-start.2 = (f32[32,256]{1,0:T(8,128)S(1)}, f32[32,256]{1,0:T(8,128)S(1)}, u32[]{:S(2)}, u32[]{:S(2)}) collective-permute-start(f32[32,256]{1,0:T(8,128)S(1)} %get-tuple-element.23.refs_0_), channel_id=1, source_target_pairs={{0,8},{8,16},{16,24},{24,0},{1,9},{9,17},{17,25},{25,1},{2,10},{10... | collective-permute-start | bytes 98312 | tf_op jit(solution)/shard_map/ppermute | solution.py:278
  13.0 1.1 %collective-permute-start.3 = (f32[32,256]{1,0:T(8,128)S(1)}, f32[32,256]{1,0:T(8,128)S(1)}, u32[]{:S(2)}, u32[]{:S(2)}) collective-permute-start(f32[32,256]{1,0:T(8,128)S(1)} %get-tuple-element.23.refs_0_), channel_id=1, source_target_pairs={{0,16},{8,24},{16,0},{24,8},{1,17},{9,25},{17,1},{25,9},{2,18},{10... | collective-permute-start | bytes 98312 | tf_op jit(solution)/shard_map/ppermute | solution.py:278
  14.1 2.9 %collective-permute-start.4 = (f32[32,256]{1,0:T(8,128)S(1)}, f32[32,256]{1,0:T(8,128)S(1)}, u32[]{:S(2)}, u32[]{:S(2)}) collective-permute-start(f32[32,256]{1,0:T(8,128)S(1)} %get-tuple-element.23.refs_0_), channel_id=1, source_target_pairs={{0,24},{8,0},{16,8},{24,16},{1,25},{9,1},{17,9},{25,17},{2,26},{10... | collective-permute-start | bytes 98312 | tf_op jit(solution)/shard_map/ppermute | solution.py:278
  17.0 0.4 collective-permute-start.7
  17.4 1.6 %collective-permute-start.6 = (f32[8,32,128]{2,1,0:T(8,128)S(1)}, f32[8,32,128]{2,1,0:T(8,128)S(1)}, u32[]{:S(2)}, u32[]{:S(2)}) collective-permute-start(f32[8,32,128]{2,1,0:T(8,128)S(1)} %get-tuple-element.26.refs_1_), channel_id=1, source_target_pairs={{0,8},{8,16},{16,24},{24,0},{1,9},{9,17},{17,25},{25,1},{2,10},{10... | collective-permute-start | bytes 393224 | tf_op jit(solution)/shard_map/ppermute | solution.py:278
  19.0 2.2 %collective-permute-start.8 = (f32[8,32,128]{2,1,0:T(8,128)S(1)}, f32[8,32,128]{2,1,0:T(8,128)S(1)}, u32[]{:S(2)}, u32[]{:S(2)}) collective-permute-start(f32[8,32,128]{2,1,0:T(8,128)S(1)} %get-tuple-element.26.refs_1_), channel_id=1, source_target_pairs={{0,24},{8,0},{16,8},{24,16},{1,25},{9,1},{17,9},{25,17},{2,26},{10... | collective-permute-start | bytes 393224 | tf_op jit(solution)/shard_map/ppermute | solution.py:278
  21.3 0.3 gram.1
  21.6 10.2 %all-gather = f32[1088,128]{1,0:T(8,128)S(1)} all-gather(f32[136,128]{1,0:T(8,128)S(1)} %gram.1), channel_id=2, replica_groups=mesh['ens'=4,'dom'=8] {'dom'}, dimensions={0}, use_global_device_ids=true | all-gather | bytes 626688 | tf_op jit(solution)/shard_map/all_gather | solution.py:336
  31.7 0.7 %collective-permute-start.10 = (f32[8,32,128]{2,1,0:T(8,128)S(1)}, f32[8,32,128]{2,1,0:T(8,128)S(1)}, u32[]{:S(2)}, u32[]{:S(2)}) collective-permute-start(f32[8,32,128]{2,1,0:T(8,128)S(1)} %collective-permute-done.6.refs_3_), channel_id=1, source_target_pairs={{0,8},{8,16},{16,24},{24,0},{1,9},{9,17},{17,25},{25,1},{2,10},{10... | collective-permute-start | bytes 393224 | tf_op jit(solution)/shard_map/ppermute | solution.py:278
  32.4 8.1 %chain.1 = (f32[32,96]{1,0:T(8,128)S(1)}, f32[32,32]{1,0:T(8,128)S(1)}) custom-call(s32[4]{0:T(128)S(1)} %copy-done.6, f32[8,136,128]{2,1,0:T(8,128)S(1)} %bitcast.3), custom_call_target="tpu_custom_call" | custom-call | flops 2300000000 | tf_op jit(solution)/shard_map/chain/pallas_call | solution.py:350
  40.5 0.4 early.1.sum_ref
  41.0 4.1 %collective-permute-done.10.refs_1_ = f32[8,32,128]{2,1,0:T(8,128)S(1)} collective-permute-done((f32[8,32,128]{2,1,0:T(8,128)S(1)}, f32[8,32,128]{2,1,0:T(8,128)S(1)}, u32[]{:S(2)}, u32[]{:S(2)}) %collective-permute-start.10) | collective-permute-done | bytes 131104 | tf_op jit(solution)/shard_map/ppermute | solution.py:278
  45.1 1.2 %late.1 = f32[32,32,128]{2,1,0:T(8,128)} custom-call(f32[32,32]{1,0:T(8,128)S(1)} %get-tuple-element.24.mix_ref, f32[16,32,256]{2,1,0:T(8,128)S(1)} %early.1.sum_ref, f32[24,32,128]{2,1,0:T(8,128)S(1)} %collective-permute-done.9.refs_0_, f32[8,32,128]{2,1,0:T(8,128)S(1)} %collective-permute-done.10.refs_1_), custom_call_target="tpu_custom_call" | custom-call | flops 1150000000 | tf_op jit(solution)/shard_map/late/pallas_call | solution.py:368
  (21 shorter events, 0.0 us)
Async XLA Ops:
  0.0 1.1 %copy-start = (f32[32,128]{1,0:T(8,128)S(1)}, f32[32,128]{1,0:T(8,128)}, u32[]{:S(2)}) copy-start(f32[32,128]{1,0:T(8,128)} %row_ref.1) | copy-start | bytes 49156
  0.0 1.1 %copy-start.1 = (f32[32,128]{1,0:T(8,128)S(1)}, f32[32,128]{1,0:T(8,128)}, u32[]{:S(2)}) copy-start(f32[32,128]{1,0:T(8,128)} %col_ref.1) | copy-start | bytes 49156
  0.0 1.1 %copy-start.2 = (f32[32,128]{1,0:T(8,128)S(1)}, f32[32,128]{1,0:T(8,128)}, u32[]{:S(2)}) copy-start(f32[32,128]{1,0:T(8,128)} %diff_ref.1) | copy-start | bytes 49156
  1.1 7.2 %copy-start.5 = (f32[4,256]{1,0:T(4,128)S(1)}, f32[4,256]{1,0:T(4,128)}, u32[]{:S(2)}) copy-start(f32[4,256]{1,0:T(4,128)} %var_ref.1) | copy-start | bytes 12292
  2.6 18.7 %collective-permute-start.5 = (f32[24,32,128]{2,1,0:T(8,128)S(1)}, f32[24,32,128]{2,1,0:T(8,128)S(1)}, u32[]{:S(2)}, u32[]{:S(2)}) collective-permute-start(f32[24,32,128]{2,1,0:T(8,128)S(1)} %get-tuple-element.22.inner_ref.refs_0_), channel_id=1, source_target_pairs={{0,8},{8,16},{16,24},{24,0},{1,9},{9,17},{17,25},{25,1},{2,10},{10... | collective-permute-start | bytes 1179656 | tf_op jit(solution)/shard_map/ppermute | solution.py:278
  5.7 4.8 %collective-permute-start = (f32[4,40,128]{2,1,0:T(8,128)S(1)}, f32[4,40,128]{2,1,0:T(8,128)S(1)}, u32[]{:S(2)}, u32[]{:S(2)}) collective-permute-start(f32[4,40,128]{2,1,0:T(8,128)S(1)} %get-tuple-element.18.bottom_ref), channel_id=1, source_target_pairs={{0,1},{1,2},{2,3},{3,4},{4,5},{5,6},{6,7},{7,0},{8,9},{9,10},{10,1... | collective-permute-start | bytes 245768 | tf_op jit(solution)/shard_map/ppermute | solution.py:278
  5.7 2.7 %copy-start.4 = (f32[4,256]{1,0:T(4,128)S(1)}, f32[4,256]{1,0:T(4,128)}, u32[]{:S(2)}) copy-start(f32[4,256]{1,0:T(4,128)} %obs_ref.1) | copy-start | bytes 12292
  5.7 2.7 %copy-start.3 = (s32[4,256]{1,0:T(4,128)S(1)}, s32[4,256]{1,0:T(4,128)}, u32[]{:S(2)}) copy-start(s32[4,256]{1,0:T(4,128)} %offsets_ref.1) | copy-start | bytes 12292
  5.7 4.8 %collective-permute-start.1 = (f32[4,40,128]{2,1,0:T(8,128)S(1)}, f32[4,40,128]{2,1,0:T(8,128)S(1)}, u32[]{:S(2)}, u32[]{:S(2)}) collective-permute-start(f32[4,40,128]{2,1,0:T(8,128)S(1)} %get-tuple-element.19.top_ref), channel_id=1, source_target_pairs={{0,7},{1,0},{2,1},{3,2},{4,3},{5,4},{6,5},{7,6},{8,15},{9,8},{10,9... | collective-permute-start | bytes 245768 | tf_op jit(solution)/shard_map/ppermute | solution.py:278
  8.3 0.7 %copy-start.6 = (s32[4]{0:T(128)S(1)}, s32[4]{0:T(128)}, u32[]{:S(2)}) copy-start(s32[4]{0:T(128)} %owners_ref.3) | copy-start | bytes 52
  11.4 6.0 %collective-permute-start.2 = (f32[32,256]{1,0:T(8,128)S(1)}, f32[32,256]{1,0:T(8,128)S(1)}, u32[]{:S(2)}, u32[]{:S(2)}) collective-permute-start(f32[32,256]{1,0:T(8,128)S(1)} %get-tuple-element.23.refs_0_), channel_id=1, source_target_pairs={{0,8},{8,16},{16,24},{24,0},{1,9},{9,17},{17,25},{25,1},{2,10},{10... | collective-permute-start | bytes 98312 | tf_op jit(solution)/shard_map/ppermute | solution.py:278
  13.0 6.0 %collective-permute-start.3 = (f32[32,256]{1,0:T(8,128)S(1)}, f32[32,256]{1,0:T(8,128)S(1)}, u32[]{:S(2)}, u32[]{:S(2)}) collective-permute-start(f32[32,256]{1,0:T(8,128)S(1)} %get-tuple-element.23.refs_0_), channel_id=1, source_target_pairs={{0,16},{8,24},{16,0},{24,8},{1,17},{9,25},{17,1},{25,9},{2,18},{10... | collective-permute-start | bytes 98312 | tf_op jit(solution)/shard_map/ppermute | solution.py:278
  14.1 7.1 %collective-permute-start.4 = (f32[32,256]{1,0:T(8,128)S(1)}, f32[32,256]{1,0:T(8,128)S(1)}, u32[]{:S(2)}, u32[]{:S(2)}) collective-permute-start(f32[32,256]{1,0:T(8,128)S(1)} %get-tuple-element.23.refs_0_), channel_id=1, source_target_pairs={{0,24},{8,0},{16,8},{24,16},{1,25},{9,1},{17,9},{25,17},{2,26},{10... | collective-permute-start | bytes 98312 | tf_op jit(solution)/shard_map/ppermute | solution.py:278
  17.0 23.5 %collective-permute-start.7 = (f32[24,32,128]{2,1,0:T(8,128)S(1)}, f32[24,32,128]{2,1,0:T(8,128)S(1)}, u32[]{:S(2)}, u32[]{:S(2)}) collective-permute-start(f32[24,32,128]{2,1,0:T(8,128)S(1)} %get-tuple-element.22.inner_ref.refs_0_), channel_id=1, source_target_pairs={{0,24},{8,0},{16,8},{24,16},{1,25},{9,1},{17,9},{25,17},{2,26},{10... | collective-permute-start | bytes 1179656 | tf_op jit(solution)/shard_map/ppermute | solution.py:278
  17.4 14.3 %collective-permute-start.6 = (f32[8,32,128]{2,1,0:T(8,128)S(1)}, f32[8,32,128]{2,1,0:T(8,128)S(1)}, u32[]{:S(2)}, u32[]{:S(2)}) collective-permute-start(f32[8,32,128]{2,1,0:T(8,128)S(1)} %get-tuple-element.26.refs_1_), channel_id=1, source_target_pairs={{0,8},{8,16},{16,24},{24,0},{1,9},{9,17},{17,25},{25,1},{2,10},{10... | collective-permute-start | bytes 393224 | tf_op jit(solution)/shard_map/ppermute | solution.py:278
  19.0 21.5 %collective-permute-start.8 = (f32[8,32,128]{2,1,0:T(8,128)S(1)}, f32[8,32,128]{2,1,0:T(8,128)S(1)}, u32[]{:S(2)}, u32[]{:S(2)}) collective-permute-start(f32[8,32,128]{2,1,0:T(8,128)S(1)} %get-tuple-element.26.refs_1_), channel_id=1, source_target_pairs={{0,24},{8,0},{16,8},{24,16},{1,25},{9,1},{17,9},{25,17},{2,26},{10... | collective-permute-start | bytes 393224 | tf_op jit(solution)/shard_map/ppermute | solution.py:278
  21.3 23.8 %collective-permute-start.9 = (f32[24,32,128]{2,1,0:T(8,128)S(1)}, f32[24,32,128]{2,1,0:T(8,128)S(1)}, u32[]{:S(2)}, u32[]{:S(2)}) collective-permute-start(f32[24,32,128]{2,1,0:T(8,128)S(1)} %collective-permute-done.5.refs_2_), channel_id=1, source_target_pairs={{0,8},{8,16},{16,24},{24,0},{1,9},{9,17},{17,25},{25,1},{2,10},{10... | collective-permute-start | bytes 1179656 | tf_op jit(solution)/shard_map/ppermute | solution.py:278
  31.7 13.3 %collective-permute-start.10 = (f32[8,32,128]{2,1,0:T(8,128)S(1)}, f32[8,32,128]{2,1,0:T(8,128)S(1)}, u32[]{:S(2)}, u32[]{:S(2)}) collective-permute-start(f32[8,32,128]{2,1,0:T(8,128)S(1)} %collective-permute-done.6.refs_3_), channel_id=1, source_target_pairs={{0,8},{8,16},{16,24},{24,0},{1,9},{9,17},{17,25},{25,1},{2,10},{10... | collective-permute-start | bytes 393224 | tf_op jit(solution)/shard_map/ppermute | solution.py:278

commit v6 on v5

--- a/solution.py
+++ b/solution.py
@@ -42,7 +42,7 @@
 
 def advance(load, coef, store, count, scratches):
     for step in range(1, FSTEPS + 1):
-        source = load if step == 1 else scratches[step % 2].__getitem__
+        source = functools.cache(load) if step == 1 else scratches[step % 2].__getitem__
         for r in range(step, count - step):
             x = source(r)
             cols = x.shape[1]
@@ -60,12 +60,9 @@
 
 
 def inner_kernel(
-    state_ref, row_ref, col_ref, diff_ref, top_ref, upper_ref, lower_ref, bottom_ref, inner_ref,
-    coef_ref, a_ref, b_ref,
+    state_ref, row_ref, col_ref, diff_ref, inner_ref, coef_ref, a_ref, b_ref
 ):
-    width = FSTEPS
-    rows, mem, cols = a_ref.shape
-    count = coef_ref.shape[0]
+    rows, mem, _ = a_ref.shape
     row_c, col_c, diff_c = row_ref[...], col_ref[...], diff_ref[...]
     coef_ref[0] = 1.0 - row_c - col_c - 4.0 * diff_c
     coef_ref[1] = row_c + diff_c
@@ -76,20 +73,26 @@
         return state_ref[pl.ds(r, mem, stride=rows), :]
 
     def coef(r):
-        return [coef_ref[i, r:r + 1, :] for i in range(count)]
-
-    blocks = (top_ref, 0), (upper_ref, width), (lower_ref, rows - 2 * width), (bottom_ref, rows - width)
-    for ref, base in blocks:
+        return [coef_ref[i, r:r + 1, :] for i in range(4)]
+
+    def store(r, value):
+        inner_ref[r - FSTEPS] = value
+
+    advance(load, coef, store, rows, (a_ref, b_ref))
+
+
+def border_kernel(state_ref, coef_ref, top_ref, upper_ref, lower_ref, bottom_ref):
+    width, lanes, cols = top_ref.shape
+    count, rows, _ = coef_ref.shape
+    mem = lanes - 8
+    bases = 0, width, rows - 2 * width, rows - width
+    for ref, base in zip((top_ref, upper_ref, lower_ref, bottom_ref), bases):
         for r in range(width):
-            ref[r, :mem, :] = load(base + r)
-            for i, row in enumerate(coef(base + r)):
-                ref[r, mem + i:mem + i + 1, :] = row
-            ref[r, mem + count:, :] = jnp.zeros((ref.shape[1] - mem - count, cols), jnp.float32)
-
-    def store(r, value):
-        inner_ref[r - width] = value
-
-    advance(load, coef, store, rows, (a_ref, b_ref))
+            row = base + r
+            ref[r, :mem, :] = state_ref[pl.ds(row, mem, stride=rows), :]
+            for i in range(count):
+                ref[r, mem + i:mem + i + 1, :] = coef_ref[i, row:row + 1, :]
+            ref[r, mem + count:, :] = jnp.zeros((8 - count, cols), jnp.float32)
 
 
 def split3(x):
@@ -228,6 +231,8 @@
 
 
 def row_of(pair, r):
+    if len(pair) == 1:
+        return pair[0][r - FSTEPS]
     inner_ref, outer_ref = pair
     inner, width = inner_ref.shape[0], outer_ref.shape[0] // 2
     if width <= r < inner + width:
@@ -252,23 +257,22 @@
         sum_ref[r // 2] = share(mix_ref[...], pairs, r)
 
 
-def late_kernel(mix_ref, sum_ref, *refs):
-    field_refs, out_ref, stage_ref, sems = refs[:-3], refs[-3], refs[-2], refs[-1]
-    pairs = list(zip(field_refs[::2], field_refs[1::2]))
-    rows, cols = stage_ref.shape[1:]
-    chunk = rows // sems.shape[0]
+def late_kernel(blocks, pieces, mix_ref, sum_ref, *refs):
+    out_ref, stage_ref, sems = refs[-3:]
+    groups = [refs[i:i + pieces] for i in range(0, mix_ref.shape[1] // stage_ref.shape[0] * pieces, pieces)]
+    chunk, cols = 8, stage_ref.shape[2]
     copies = []
-    for r in range(0, rows, 2):
-        fresh = sum_ref[r // 2] + share(mix_ref[...], pairs, r)
-        for i in range(2):
-            stage_ref[:, r + i, :] = fresh[:, i * cols:(i + 1) * cols]
-        if (r + 2) % chunk == 0:
-            block = pl.ds(r + 2 - chunk, chunk)
-            copy = pltpu.make_async_copy(
-                stage_ref.at[:, block, :], out_ref.at[:, block, :], sems.at[len(copies)]
-            )
-            copy.start()
-            copies.append(copy)
+    for block in blocks:
+        for r in range(block, block + chunk, 2):
+            fresh = sum_ref[r // 2] + share(mix_ref[...], groups, r)
+            for i in range(2):
+                stage_ref[:, r + i, :] = fresh[:, i * cols:(i + 1) * cols]
+        rows = pl.ds(block, chunk)
+        copy = pltpu.make_async_copy(
+            stage_ref.at[:, rows, :], out_ref.at[:, rows, :], sems.at[len(copies)]
+        )
+        copy.start()
+        copies.append(copy)
     for copy in copies:
         copy.wait()
 
@@ -290,6 +294,14 @@
     scratch = functools.partial(pltpu.VMEM, dtype=jnp.float32)
     place = lax.axis_index("dom").astype(jnp.int32).reshape(1)
     staged = jnp.pad(state, ((0, 1), (0, 0), (0, 0))).reshape(-1, cols)
+    def around(part):
+        slots = [part] * ens
+        for j in range(1, ens // 2 + 1):
+            slots[j] = shift(slots[j - 1], "ens", 1)
+        for j in range(1, (ens - 1) // 2 + 1):
+            slots[ens - j] = shift(slots[(ens - j + 1) % ens], "ens", -1)
+        return slots
+
     edge = f32((width, mem + 8, cols))
     cells, own = pl.pallas_call(
         rows_kernel,
@@ -300,16 +312,25 @@
         cost_estimate=estimate(1),
         name="rows",
     )(place, owners, obs_offsets, obs_values, obs_variance)
-    top, upper, lower, bottom, inner = pl.pallas_call(
+    inner, mixers = pl.pallas_call(
         inner_kernel,
-        out_shape=(edge,) * 4 + (f32((rows - 2 * width, mem, cols)),),
+        out_shape=(f32((rows - 2 * width, mem, cols)), f32((4, rows, cols))),
         in_specs=[VMEM] * 4,
-        out_specs=(VMEM,) * 5,
-        scratch_shapes=[scratch((4, rows, cols))] + [scratch((rows, mem, cols))] * 2,
+        out_specs=(VMEM,) * 2,
+        scratch_shapes=[scratch((rows, mem, cols))] * 2,
         compiler_params=PARAMS,
         cost_estimate=estimate(3),
         name="inner",
     )(staged, row_courant, col_courant, diffusion)
+    top, upper, lower, bottom = pl.pallas_call(
+        border_kernel,
+        out_shape=(edge,) * 4,
+        in_specs=[VMEM] * 2,
+        out_specs=(VMEM,) * 4,
+        compiler_params=PARAMS,
+        cost_estimate=estimate(0.2),
+        name="border",
+    )(staged, mixers)
     up = shift(bottom, "dom", 1)
     down = shift(top, "dom", -1)
     outer, seen = pl.pallas_call(
@@ -335,14 +356,6 @@
     )(own, *seens)
     grams = lax.all_gather(gram, "dom")
 
-    def around(part):
-        slots = [part] * ens
-        for j in range(1, ens // 2 + 1):
-            slots[j] = shift(slots[j - 1], "ens", 1)
-        for j in range(1, (ens - 1) // 2 + 1):
-            slots[ens - j] = shift(slots[(ens - j + 1) % ens], "ens", -1)
-        return slots
-
     slots = list(zip(around(inner), around(outer)))
     late = list(range(2, ens - 1))
     soon = [j for j in range(ens) if j not in late]
@@ -365,16 +378,23 @@
         cost_estimate=estimate(EARLY_US),
         name="early",
     )(mix_soon, *[x for j in soon for x in slots[j]])
-    return pl.pallas_call(
-        late_kernel,
-        out_shape=f32((mem, rows, cols)),
-        in_specs=[VMEM] * (2 + 2 * len(late)),
-        out_specs=ANY,
-        scratch_shapes=[scratch((mem, rows, cols)), pltpu.SemaphoreType.DMA((rows // 8,))],
-        compiler_params=PARAMS,
-        cost_estimate=estimate(1),
-        name="late",
-    )(mix_late, sums, *[x for j in late for x in slots[j]])
+    blocks = list(range(0, rows, 8))
+    out = None
+    for chosen, width_of in ((blocks[1:-1], 1), ((blocks[0], blocks[-1]), 2)):
+        given = [x for j in late for x in slots[j][:width_of]]
+        previous = [] if out is None else [out]
+        out = pl.pallas_call(
+            functools.partial(late_kernel, chosen, width_of),
+            out_shape=f32((mem, rows, cols)),
+            in_specs=[VMEM] * (2 + len(given)) + [ANY] * len(previous),
+            out_specs=ANY,
+            input_output_aliases={2 + len(given): 0} if previous else {},
+            scratch_shapes=[scratch((mem, rows, cols)), pltpu.SemaphoreType.DMA((len(chosen),))],
+            compiler_params=PARAMS,
+            cost_estimate=estimate(0.1),
+            name="late",
+        )(mix_late, sums, *given, *previous)
+    return out
 
 
 def solution(mesh):

time: 46.4 us -> 46.1 us (level)
  waiting for transfers between devices: 5.01 us -> 3.75 us
  Pallas kernels: 12.9 us -> 13.9 us
    ppermute x11, waiting for transfers between devices: 5.01 us -> 3.75 us  [shift(): lax.ppermute(x, axis, [(i, (i + step) % count) for i in range(count)])]
    pallas_call x2 -> x4, Pallas kernels: 2.61 us -> 3.25 us  [the longest x2 1.96 us: on_device(): pl.pallas_call(functools.partial(late_kernel, chosen, width_of), out_shap...]
  transfers between devices with their start and end apart: 11 -> 11, of which waited for: 2 -> 3; matrix products, arithmetic and copies ran while one was open for 0% -> 0% of each run, Pallas kernels for 22% -> 26%
where the time goes in v6:
time: 46.1 us; the launch traced here: 45.9 us
  starting transfers between devices  16.3 us (35%)
  Pallas kernels  13.9 us (30%)
  blocking collectives  10.1 us (22%)
  waiting for transfers between devices  3.75 us (8%)
  local copies, waits for them, and re-layouts  1.77 us (4%)
    ppermute x11, starting transfers between devices, shift(): lax.ppermute(x, axis, [(i, (i + step) % count) for i in range(count)])  16.3 us
    all_gather x1, blocking collectives, on_device(): grams = lax.all_gather(gram, 'dom')  10.1 us
    pallas_call x1, Pallas kernels, on_device(): pl.pallas_call(functools.partial(chain_kernel, soon, late), out_shape=(f3...  8.35 us
    ppermute x11, waiting for transfers between devices, shift(): lax.ppermute(x, axis, [(i, (i + step) % count) for i in range(count)])  3.75 us
    pallas_call x2, Pallas kernels, on_device(): pl.pallas_call(functools.partial(late_kernel, chosen, width_of), out_shap...  1.96 us
    pallas_call x1, Pallas kernels, on_device(): pl.pallas_call(inner_kernel, out_shape=(f32((rows - 2 * width, mem, cols)...  1.11 us
    pad x1, local copies, waits for them, and re-layouts, on_device(): staged = jnp.pad(state, ((0, 1), (0, 0), (0, 0))).reshape(-1, cols)  1.1 us
    pallas_call x1, Pallas kernels, on_device(): pl.pallas_call(outer_kernel, out_shape=(f32((2 * width, mem, cols)), f32(...  0.97 us
  transfers between devices with their start and end apart: 11, of which 3 were waited for; matrix products, arithmetic and copies ran while one was open for 0% of the time, Pallas kernels for 26%

profile of v6, /device:TPU:0, one launch (start us, length us, event | category | flops | bytes accessed | tf_op | source)
XLA Modules:
  0.0 45.9 jit_solution(17025981228793963589)
XLA Ops:
  0.0 1.1 %pad.4 = f32[33,32,128]{2,1,0:T(8,128)S(1)} pad(f32[32,32,128]{2,1,0:T(8,128)} %param.8, f32[]{:T(128)} %constant.6.clone.1), padding=0_1x0_0x0_0 | pad | bytes 1064964 | tf_op jit(solution)/shard_map/jit(_pad)/pad | solution.py:296
  1.1 1.1 %inner.1 = (f32[24,32,128]{2,1,0:T(8,128)S(1)}, f32[4,32,128]{2,1,0:T(8,128)S(1)}) custom-call(f32[1056,128]{1,0:T(8,128)S(1)} %bitcast.4, f32[32,128]{1,0:T(8,128)S(1)} %copy-done, f32[32,128]{1,0:T(8,128)S(1)} %copy-done.1, f32[32,128]{1,0:T(8,128)S(1)} %copy-done.2), custom_call_target="tpu_custom_call" | custom-call | flops 3449999872 | tf_op jit(solution)/shard_map/inner/pallas_call | solution.py:315
  2.3 3.1 %collective-permute-start.5 = (f32[24,32,128]{2,1,0:T(8,128)S(1)}, f32[24,32,128]{2,1,0:T(8,128)S(1)}, u32[]{:S(2)}, u32[]{:S(2)}) collective-permute-start(f32[24,32,128]{2,1,0:T(8,128)S(1)} %get-tuple-element.24.inner_ref.refs_0_), channel_id=1, source_target_pairs={{0,8},{8,16},{16,24},{24,0},{1,9},{9,17},{17,25},{25,1},{2,10},{10... | collective-permute-start | bytes 1179656 | tf_op jit(solution)/shard_map/ppermute | solution.py:282
  5.4 0.2 border.1
  5.6 2.6 %collective-permute-start.1 = (f32[4,40,128]{2,1,0:T(8,128)S(1)}, f32[4,40,128]{2,1,0:T(8,128)S(1)}, u32[]{:S(2)}, u32[]{:S(2)}) collective-permute-start(f32[4,40,128]{2,1,0:T(8,128)S(1)} %get-tuple-element.21.top_ref), channel_id=1, source_target_pairs={{0,7},{1,0},{2,1},{3,2},{4,3},{5,4},{6,5},{7,6},{8,15},{9,8},{10,9... | collective-permute-start | bytes 245768 | tf_op jit(solution)/shard_map/ppermute | solution.py:282
  8.2 0.6 %copy-done.6 = s32[4]{0:T(128)S(1)} copy-done((s32[4]{0:T(128)S(1)}, s32[4]{0:T(128)}, u32[]{:S(2)}) %copy-start.6) | copy-done | bytes 40
  8.9 0.5 %rows.1 = (s32[8,256]{1,0:T(8,128)S(1)}, f32[16,256]{1,0:T(8,128)S(1)}) custom-call(s32[1]{0:T(128)} %bitcast.place_ref, s32[4]{0:T(128)S(1)} %copy-done.6, s32[4,256]{1,0:T(4,128)S(1)} %copy-done.3, f32[4,256]{1,0:T(4,128)S(1)} %copy-done.4, f32[4,256]{1,0:T(4,128)S(1)} %copy-done.5), custom_call_target="tpu_custom_call" | custom-call | flops 1150000000 | tf_op jit(solution)/shard_map/rows/pallas_call | solution.py:306
  9.4 0.9 %collective-permute-done.up_ref = f32[4,40,128]{2,1,0:T(8,128)S(1)} collective-permute-done((f32[4,40,128]{2,1,0:T(8,128)S(1)}, f32[4,40,128]{2,1,0:T(8,128)S(1)}, u32[]{:S(2)}, u32[]{:S(2)}) %collective-permute-start) | collective-permute-done | bytes 81952 | tf_op jit(solution)/shard_map/ppermute | solution.py:282
  10.4 1.0 %outer.1 = (f32[8,32,128]{2,1,0:T(8,128)S(1)}, f32[32,256]{1,0:T(8,128)S(1)}) custom-call(s32[8,256]{1,0:T(8,128)S(1)} %get-tuple-element.18.cells_ref, f32[4,40,128]{2,1,0:T(8,128)S(1)} %collective-permute-done.up_ref, f32[4,40,128]{2,1,0:T(8,128)S(1)} %get-tuple-element.21.top_ref, f32[4,40,128]{2,1,0:T(8,128)S(1)} %get-tuple-element.22.upper_ref, ...), custom_call_target="tpu_custom_call" | custom-call | flops 2300000000 | tf_op jit(solution)/shard_map/outer/pallas_call | solution.py:336
  11.3 1.6 %collective-permute-start.2 = (f32[32,256]{1,0:T(8,128)S(1)}, f32[32,256]{1,0:T(8,128)S(1)}, u32[]{:S(2)}, u32[]{:S(2)}) collective-permute-start(f32[32,256]{1,0:T(8,128)S(1)} %get-tuple-element.25.refs_0_), channel_id=1, source_target_pairs={{0,8},{8,16},{16,24},{24,0},{1,9},{9,17},{17,25},{25,1},{2,10},{10... | collective-permute-start | bytes 98312 | tf_op jit(solution)/shard_map/ppermute | solution.py:282
  12.9 1.1 %collective-permute-start.3 = (f32[32,256]{1,0:T(8,128)S(1)}, f32[32,256]{1,0:T(8,128)S(1)}, u32[]{:S(2)}, u32[]{:S(2)}) collective-permute-start(f32[32,256]{1,0:T(8,128)S(1)} %get-tuple-element.25.refs_0_), channel_id=1, source_target_pairs={{0,16},{8,24},{16,0},{24,8},{1,17},{9,25},{17,1},{25,9},{2,18},{10... | collective-permute-start | bytes 98312 | tf_op jit(solution)/shard_map/ppermute | solution.py:282
  14.0 2.9 %collective-permute-start.4 = (f32[32,256]{1,0:T(8,128)S(1)}, f32[32,256]{1,0:T(8,128)S(1)}, u32[]{:S(2)}, u32[]{:S(2)}) collective-permute-start(f32[32,256]{1,0:T(8,128)S(1)} %get-tuple-element.25.refs_0_), channel_id=1, source_target_pairs={{0,24},{8,0},{16,8},{24,16},{1,25},{9,1},{17,9},{25,17},{2,26},{10... | collective-permute-start | bytes 98312 | tf_op jit(solution)/shard_map/ppermute | solution.py:282
  16.9 0.4 collective-permute-start.7
  17.4 1.5 %collective-permute-start.6 = (f32[8,32,128]{2,1,0:T(8,128)S(1)}, f32[8,32,128]{2,1,0:T(8,128)S(1)}, u32[]{:S(2)}, u32[]{:S(2)}) collective-permute-start(f32[8,32,128]{2,1,0:T(8,128)S(1)} %get-tuple-element.28.refs_1_), channel_id=1, source_target_pairs={{0,8},{8,16},{16,24},{24,0},{1,9},{9,17},{17,25},{25,1},{2,10},{10... | collective-permute-start | bytes 393224 | tf_op jit(solution)/shard_map/ppermute | solution.py:282
  18.9 2.3 %collective-permute-start.8 = (f32[8,32,128]{2,1,0:T(8,128)S(1)}, f32[8,32,128]{2,1,0:T(8,128)S(1)}, u32[]{:S(2)}, u32[]{:S(2)}) collective-permute-start(f32[8,32,128]{2,1,0:T(8,128)S(1)} %get-tuple-element.28.refs_1_), channel_id=1, source_target_pairs={{0,24},{8,0},{16,8},{24,16},{1,25},{9,1},{17,9},{25,17},{2,26},{10... | collective-permute-start | bytes 393224 | tf_op jit(solution)/shard_map/ppermute | solution.py:282
  21.2 0.3 gram.1
  21.5 10.1 %all-gather = f32[1088,128]{1,0:T(8,128)S(1)} all-gather(f32[136,128]{1,0:T(8,128)S(1)} %gram.1), channel_id=2, replica_groups=mesh['ens'=4,'dom'=8] {'dom'}, dimensions={0}, use_global_device_ids=true | all-gather | bytes 626688 | tf_op jit(solution)/shard_map/all_gather | solution.py:357
  31.7 0.7 %collective-permute-start.10 = (f32[8,32,128]{2,1,0:T(8,128)S(1)}, f32[8,32,128]{2,1,0:T(8,128)S(1)}, u32[]{:S(2)}, u32[]{:S(2)}) collective-permute-start(f32[8,32,128]{2,1,0:T(8,128)S(1)} %collective-permute-done.6.refs_3_), channel_id=1, source_target_pairs={{0,8},{8,16},{16,24},{24,0},{1,9},{9,17},{17,25},{25,1},{2,10},{10... | collective-permute-start | bytes 393224 | tf_op jit(solution)/shard_map/ppermute | solution.py:282
  32.3 8.4 %chain.1 = (f32[32,96]{1,0:T(8,128)S(1)}, f32[32,32]{1,0:T(8,128)S(1)}) custom-call(s32[4]{0:T(128)S(1)} %copy-done.6, f32[8,136,128]{2,1,0:T(8,128)S(1)} %bitcast.3), custom_call_target="tpu_custom_call" | custom-call | flops 2300000000 | tf_op jit(solution)/shard_map/chain/pallas_call | solution.py:363
  40.7 0.4 early.1.sum_ref
  41.2 1.5 %collective-permute-done.9.refs_0_ = f32[24,32,128]{2,1,0:T(8,128)S(1)} collective-permute-done((f32[24,32,128]{2,1,0:T(8,128)S(1)}, f32[24,32,128]{2,1,0:T(8,128)S(1)}, u32[]{:S(2)}, u32[]{:S(2)}) %collective-permute-start.9) | collective-permute-done | bytes 393248 | tf_op jit(solution)/shard_map/ppermute | solution.py:282
  42.7 1.0 %late.2.refs_2_ = f32[32,32,128]{2,1,0:T(8,128)} custom-call(f32[32,32]{1,0:T(8,128)S(1)} %get-tuple-element.26.mix_ref, f32[16,32,256]{2,1,0:T(8,128)S(1)} %early.1.sum_ref, f32[24,32,128]{2,1,0:T(8,128)S(1)} %collective-permute-done.9.refs_0_), custom_call_target="tpu_custom_call" | custom-call | flops 115000000 | tf_op jit(solution)/shard_map/late/pallas_call | solution.py:386
  43.7 1.3 %collective-permute-done.10.refs_1_ = f32[8,32,128]{2,1,0:T(8,128)S(1)} collective-permute-done((f32[8,32,128]{2,1,0:T(8,128)S(1)}, f32[8,32,128]{2,1,0:T(8,128)S(1)}, u32[]{:S(2)}, u32[]{:S(2)}) %collective-permute-start.10) | collective-permute-done | bytes 131104 | tf_op jit(solution)/shard_map/ppermute | solution.py:282
  44.9 1.0 %late.3 = f32[32,32,128]{2,1,0:T(8,128)} custom-call(f32[32,32]{1,0:T(8,128)S(1)} %get-tuple-element.26.mix_ref, f32[16,32,256]{2,1,0:T(8,128)S(1)} %early.1.sum_ref, f32[24,32,128]{2,1,0:T(8,128)S(1)} %collective-permute-done.9.refs_0_, f32[8,32,128]{2,1,0:T(8,128)S(1)} %collective-permute-done.10.refs_1_, ...), custom_call_target="tpu_custom_call", output_to_operand_aliasing={{}: (4, {})} | custom-call | flops 115000000 | tf_op jit(solution)/shard_map/late/pallas_call | solution.py:386
  (23 shorter events, 0.1 us)
Async XLA Ops:
  0.0 1.1 %copy-start = (f32[32,128]{1,0:T(8,128)S(1)}, f32[32,128]{1,0:T(8,128)}, u32[]{:S(2)}) copy-start(f32[32,128]{1,0:T(8,128)} %row_ref.1) | copy-start | bytes 49156
  0.0 1.1 %copy-start.1 = (f32[32,128]{1,0:T(8,128)S(1)}, f32[32,128]{1,0:T(8,128)}, u32[]{:S(2)}) copy-start(f32[32,128]{1,0:T(8,128)} %col_ref.1) | copy-start | bytes 49156
  0.0 1.1 %copy-start.2 = (f32[32,128]{1,0:T(8,128)S(1)}, f32[32,128]{1,0:T(8,128)}, u32[]{:S(2)}) copy-start(f32[32,128]{1,0:T(8,128)} %diff_ref.1) | copy-start | bytes 49156
  2.3 18.9 %collective-permute-start.5 = (f32[24,32,128]{2,1,0:T(8,128)S(1)}, f32[24,32,128]{2,1,0:T(8,128)S(1)}, u32[]{:S(2)}, u32[]{:S(2)}) collective-permute-start(f32[24,32,128]{2,1,0:T(8,128)S(1)} %get-tuple-element.24.inner_ref.refs_0_), channel_id=1, source_target_pairs={{0,8},{8,16},{16,24},{24,0},{1,9},{9,17},{17,25},{25,1},{2,10},{10... | collective-permute-start | bytes 1179656 | tf_op jit(solution)/shard_map/ppermute | solution.py:282
  5.4 2.9 %copy-start.5 = (f32[4,256]{1,0:T(4,128)S(1)}, f32[4,256]{1,0:T(4,128)}, u32[]{:S(2)}) copy-start(f32[4,256]{1,0:T(4,128)} %var_ref.1) | copy-start | bytes 12292
  5.5 4.8 %collective-permute-start = (f32[4,40,128]{2,1,0:T(8,128)S(1)}, f32[4,40,128]{2,1,0:T(8,128)S(1)}, u32[]{:S(2)}, u32[]{:S(2)}) collective-permute-start(f32[4,40,128]{2,1,0:T(8,128)S(1)} %get-tuple-element.20.bottom_ref), channel_id=1, source_target_pairs={{0,1},{1,2},{2,3},{3,4},{4,5},{5,6},{6,7},{7,0},{8,9},{9,10},{10,1... | collective-permute-start | bytes 245768 | tf_op jit(solution)/shard_map/ppermute | solution.py:282
  5.6 2.6 %copy-start.4 = (f32[4,256]{1,0:T(4,128)S(1)}, f32[4,256]{1,0:T(4,128)}, u32[]{:S(2)}) copy-start(f32[4,256]{1,0:T(4,128)} %obs_ref.1) | copy-start | bytes 12292
  5.6 2.6 %copy-start.3 = (s32[4,256]{1,0:T(4,128)S(1)}, s32[4,256]{1,0:T(4,128)}, u32[]{:S(2)}) copy-start(s32[4,256]{1,0:T(4,128)} %offsets_ref.1) | copy-start | bytes 12292
  5.6 4.7 %collective-permute-start.1 = (f32[4,40,128]{2,1,0:T(8,128)S(1)}, f32[4,40,128]{2,1,0:T(8,128)S(1)}, u32[]{:S(2)}, u32[]{:S(2)}) collective-permute-start(f32[4,40,128]{2,1,0:T(8,128)S(1)} %get-tuple-element.21.top_ref), channel_id=1, source_target_pairs={{0,7},{1,0},{2,1},{3,2},{4,3},{5,4},{6,5},{7,6},{8,15},{9,8},{10,9... | collective-permute-start | bytes 245768 | tf_op jit(solution)/shard_map/ppermute | solution.py:282
  8.2 0.7 %copy-start.6 = (s32[4]{0:T(128)S(1)}, s32[4]{0:T(128)}, u32[]{:S(2)}) copy-start(s32[4]{0:T(128)} %owners_ref.3) | copy-start | bytes 52
  11.3 6.0 %collective-permute-start.2 = (f32[32,256]{1,0:T(8,128)S(1)}, f32[32,256]{1,0:T(8,128)S(1)}, u32[]{:S(2)}, u32[]{:S(2)}) collective-permute-start(f32[32,256]{1,0:T(8,128)S(1)} %get-tuple-element.25.refs_0_), channel_id=1, source_target_pairs={{0,8},{8,16},{16,24},{24,0},{1,9},{9,17},{17,25},{25,1},{2,10},{10... | collective-permute-start | bytes 98312 | tf_op jit(solution)/shard_map/ppermute | solution.py:282
  12.9 6.0 %collective-permute-start.3 = (f32[32,256]{1,0:T(8,128)S(1)}, f32[32,256]{1,0:T(8,128)S(1)}, u32[]{:S(2)}, u32[]{:S(2)}) collective-permute-start(f32[32,256]{1,0:T(8,128)S(1)} %get-tuple-element.25.refs_0_), channel_id=1, source_target_pairs={{0,16},{8,24},{16,0},{24,8},{1,17},{9,25},{17,1},{25,9},{2,18},{10... | collective-permute-start | bytes 98312 | tf_op jit(solution)/shard_map/ppermute | solution.py:282
  14.0 7.2 %collective-permute-start.4 = (f32[32,256]{1,0:T(8,128)S(1)}, f32[32,256]{1,0:T(8,128)S(1)}, u32[]{:S(2)}, u32[]{:S(2)}) collective-permute-start(f32[32,256]{1,0:T(8,128)S(1)} %get-tuple-element.25.refs_0_), channel_id=1, source_target_pairs={{0,24},{8,0},{16,8},{24,16},{1,25},{9,1},{17,9},{25,17},{2,26},{10... | collective-permute-start | bytes 98312 | tf_op jit(solution)/shard_map/ppermute | solution.py:282
  16.9 23.8 %collective-permute-start.7 = (f32[24,32,128]{2,1,0:T(8,128)S(1)}, f32[24,32,128]{2,1,0:T(8,128)S(1)}, u32[]{:S(2)}, u32[]{:S(2)}) collective-permute-start(f32[24,32,128]{2,1,0:T(8,128)S(1)} %get-tuple-element.24.inner_ref.refs_0_), channel_id=1, source_target_pairs={{0,24},{8,0},{16,8},{24,16},{1,25},{9,1},{17,9},{25,17},{2,26},{10... | collective-permute-start | bytes 1179656 | tf_op jit(solution)/shard_map/ppermute | solution.py:282
  17.4 14.3 %collective-permute-start.6 = (f32[8,32,128]{2,1,0:T(8,128)S(1)}, f32[8,32,128]{2,1,0:T(8,128)S(1)}, u32[]{:S(2)}, u32[]{:S(2)}) collective-permute-start(f32[8,32,128]{2,1,0:T(8,128)S(1)} %get-tuple-element.28.refs_1_), channel_id=1, source_target_pairs={{0,8},{8,16},{16,24},{24,0},{1,9},{9,17},{17,25},{25,1},{2,10},{10... | collective-permute-start | bytes 393224 | tf_op jit(solution)/shard_map/ppermute | solution.py:282
  18.9 21.8 %collective-permute-start.8 = (f32[8,32,128]{2,1,0:T(8,128)S(1)}, f32[8,32,128]{2,1,0:T(8,128)S(1)}, u32[]{:S(2)}, u32[]{:S(2)}) collective-permute-start(f32[8,32,128]{2,1,0:T(8,128)S(1)} %get-tuple-element.28.refs_1_), channel_id=1, source_target_pairs={{0,24},{8,0},{16,8},{24,16},{1,25},{9,1},{17,9},{25,17},{2,26},{10... | collective-permute-start | bytes 393224 | tf_op jit(solution)/shard_map/ppermute | solution.py:282
  21.2 21.5 %collective-permute-start.9 = (f32[24,32,128]{2,1,0:T(8,128)S(1)}, f32[24,32,128]{2,1,0:T(8,128)S(1)}, u32[]{:S(2)}, u32[]{:S(2)}) collective-permute-start(f32[24,32,128]{2,1,0:T(8,128)S(1)} %collective-permute-done.5.refs_2_), channel_id=1, source_target_pairs={{0,8},{8,16},{16,24},{24,0},{1,9},{9,17},{17,25},{25,1},{2,10},{10... | collective-permute-start | bytes 1179656 | tf_op jit(solution)/shard_map/ppermute | solution.py:282
  31.7 13.3 %collective-permute-start.10 = (f32[8,32,128]{2,1,0:T(8,128)S(1)}, f32[8,32,128]{2,1,0:T(8,128)S(1)}, u32[]{:S(2)}, u32[]{:S(2)}) collective-permute-start(f32[8,32,128]{2,1,0:T(8,128)S(1)} %collective-permute-done.6.refs_3_), channel_id=1, source_target_pairs={{0,8},{8,16},{16,24},{24,0},{1,9},{9,17},{17,25},{25,1},{2,10},{10... | collective-permute-start | bytes 393224 | tf_op jit(solution)/shard_map/ppermute | solution.py:282
